TPU v7x, 32 devices: a whole 2x2x4 slice. The times are simulated.
32 devices in a mesh: fsdp: 16 (over z, x, core), seq: 2 (over y).
Axes of the slice: x: 2, y: 2, z: 4, core: 2. Of those that a mesh axis runs over, the one named last changes fastest.
Arguments:
- frames_in: bfloat16 [16, 1024, 1280], P('fsdp', 'seq'), may hold values from -6 to 6
- clip_lengths: int32 [16], P('fsdp'), may hold values from 897 to 1024, as said below
- norm1_gain: bfloat16 [1280], P('fsdp'), may hold values from 0.5 to 1.5
- norm1_bias: bfloat16 [1280], P('fsdp'), may hold values from -2 to 2
- q_weight: bfloat16 [1280, 1280], P('fsdp')
- q_bias: bfloat16 [1280], P('fsdp'), may hold values from -2 to 2
- k_weight: bfloat16 [1280, 1280], P('fsdp'), may hold values from -0.15625 to 0.15625
- v_weight: bfloat16 [1280, 1280], P('fsdp'), may hold values from -0.15625 to 0.15625
- v_bias: bfloat16 [1280], P('fsdp'), may hold values from -2 to 2
- o_weight: bfloat16 [1280, 1280], P('fsdp'), may hold values from -0.625 to 0.625
- o_bias: bfloat16 [1280], P('fsdp'), may hold values from -2 to 2
- norm2_gain: bfloat16 [1280], P('fsdp'), may hold values from 0.5 to 1.5
- norm2_bias: bfloat16 [1280], P('fsdp'), may hold values from -2 to 2
- up_weight: bfloat16 [1280, 5120], P('fsdp'), may hold values from -0.15625 to 0.15625
- up_bias: bfloat16 [5120], P('fsdp'), may hold values from -2 to 2
- down_weight: bfloat16 [5120, 1280], P('fsdp'), may hold values from -0.078125 to 0.078125
- down_bias: bfloat16 [1280], P('fsdp'), may hold values from -2 to 2
- out_grad: bfloat16 [16, 1024, 1280], P('fsdp', 'seq'), may hold values from -6 to 6
Outputs:
- output: bfloat16 [16, 1024, 1280], P('fsdp', 'seq')
- in_grad: bfloat16 [16, 1024, 1280], P('fsdp', 'seq')
- norm1_gain_grad: float32 [1280], P('fsdp')
- norm1_bias_grad: float32 [1280], P('fsdp')
- q_weight_grad: float32 [1280, 1280], P('fsdp')
- q_bias_grad: float32 [1280], P('fsdp')
- k_weight_grad: float32 [1280, 1280], P('fsdp')
- v_weight_grad: float32 [1280, 1280], P('fsdp')
- v_bias_grad: float32 [1280], P('fsdp')
- o_weight_grad: float32 [1280, 1280], P('fsdp')
- o_bias_grad: float32 [1280], P('fsdp')
- norm2_gain_grad: float32 [1280], P('fsdp')
- norm2_bias_grad: float32 [1280], P('fsdp')
- up_weight_grad: float32 [1280, 5120], P('fsdp')
- up_bias_grad: float32 [5120], P('fsdp')
- down_weight_grad: float32 [5120, 1280], P('fsdp')
- down_bias_grad: float32 [1280], P('fsdp')
- logit_peak: float32 [16], replicated
- q_weight_clipped: float32 [1280, 1280], P('fsdp')
- q_bias_clipped: float32 [1280], P('fsdp')
- k_weight_clipped: float32 [1280, 1280], P('fsdp')
Inputs may be any that keep to these rules, and one draw needn't show every extreme that they name: `clip_lengths`: some clip has all 1024 frames valid, and some other clip has exactly 1024 - 1024 // 8 + 1.
All inputs are finite; a program needn't handle non-finite values.
Results may differ from a plain program's by a relative error of at most 0.019.
Values may be sent and summed in bfloat16 or wider, within the bound.
No kernel may reach another device: no remote copies, remote signals or barrier semaphores. Data moves between devices by JAX's collectives and lax.ppermute only.
A program may use at most 384 MiB of HBM per device.

v0:
```python
import math

import jax
import jax.numpy as jnp
from jax import lax
from jax.sharding import PartitionSpec as P

HEAD_DIM = 80


NEGATIVE = -1000000000.0
EPSILON = 1e-05
LOGIT_CAP = 10.0


def layer_norm(rows, gain, offset):
    centred = rows - jnp.mean(rows, axis=-1, keepdims=True)
    spread = jnp.mean(centred * centred, axis=-1, keepdims=True)
    return centred * lax.rsqrt(spread + EPSILON) * gain + offset


def normalized(rows):
    centred = rows - jnp.mean(rows, axis=-1, keepdims=True)
    spread = jnp.mean(centred * centred, axis=-1, keepdims=True)
    return centred * lax.rsqrt(spread + EPSILON)


def contract_last(left, right):
    return lax.dot_general(
        left, right, (((1,), (1,)), ((), ())), preferred_element_type=jnp.float32
    )


def contract_first(left, right):
    return lax.dot_general(
        left, right, (((0,), (0,)), ((), ())), preferred_element_type=jnp.float32
    )


def local(
    frames_in,
    clip_lengths,
    norm1_gain,
    norm1_bias,
    q_weight,
    q_bias,
    k_weight,
    v_weight,
    v_bias,
    o_weight,
    o_bias,
    norm2_gain,
    norm2_bias,
    up_weight,
    up_bias,
    down_weight,
    down_bias,
    out_grad,
):
    clip_count, local_frames, model_width = frames_in.shape
    hidden = up_weight.shape[1]
    expand_ratio = hidden // model_width
    groups = lax.axis_size("seq")
    shards = lax.axis_size("fsdp")
    frames = local_frames * groups
    tokens = clip_count * local_frames
    head_dim = HEAD_DIM
    head_count = model_width // head_dim
    local_heads = head_count // groups
    slab_width = model_width // groups
    block_rows = min(512, frames)
    block_count = frames // block_rows
    score_scale = 1.0 / math.sqrt(head_dim)
    own_rows = model_width // shards
    own_hidden = hidden // shards
    fsdp_index = lax.axis_index("fsdp")
    positions = lax.axis_index("seq") * local_frames + jnp.arange(local_frames, dtype=jnp.int32)
    live_mask = (positions[None, :] < clip_lengths[:, None]).astype(jnp.float32).reshape(tokens, 1)
    residual = frames_in.reshape(tokens, model_width).astype(jnp.float32)
    plain1 = normalized(residual)
    query_part = lax.all_gather(q_weight, "fsdp", axis=0, tiled=True)
    key_part = lax.all_gather(k_weight, "fsdp", axis=0, tiled=True)
    value_part = lax.all_gather(v_weight, "fsdp", axis=0, tiled=True)
    gain_part = lax.all_gather(norm1_gain, "fsdp", axis=0, tiled=True)
    shift_part = lax.all_gather(norm1_bias, "fsdp", axis=0, tiled=True)
    qbias_part = lax.all_gather(q_bias, "fsdp", axis=0, tiled=True)
    vbias_part = lax.all_gather(v_bias, "fsdp", axis=0, tiled=True)
    out_part = lax.all_gather(o_weight, "fsdp", axis=0, tiled=True)
    obias_part = lax.all_gather(o_bias, "fsdp", axis=0, tiled=True)
    columns = plain1
    blocked = (columns * gain_part.astype(jnp.float32) + shift_part.astype(jnp.float32)).astype(
        jnp.bfloat16
    )
    joined = jnp.concatenate([query_part, key_part, value_part], axis=1)
    totals = jnp.dot(blocked, joined, preferred_element_type=jnp.float32)
    normed = blocked
    vector_part = jnp.stack([gain_part, shift_part, qbias_part, vbias_part, obias_part]).astype(
        jnp.float32
    )
    vectors = vector_part
    projected = totals
    normed1 = normed
    vectors1 = vectors
    queries = (
        (projected[:, :model_width] + vectors1[2])
        .astype(jnp.bfloat16)
        .reshape(clip_count, local_frames, model_width)
    )
    keys_tok = (
        projected[:, model_width : 2 * model_width]
        .astype(jnp.bfloat16)
        .reshape(clip_count, local_frames, model_width)
    )
    values_tok = (
        (projected[:, 2 * model_width :] + vectors1[3])
        .astype(jnp.bfloat16)
        .reshape(clip_count, local_frames, model_width)
    )
    head_q, head_k, head_v = (
        lax.all_to_all(queries, "seq", split_axis=2, concat_axis=1, tiled=True),
        lax.all_to_all(keys_tok, "seq", split_axis=2, concat_axis=1, tiled=True),
        lax.all_to_all(values_tok, "seq", split_axis=2, concat_axis=1, tiled=True),
    )
    frame_index = jnp.arange(frames, dtype=jnp.int32)

    def forward_block(query_block, query_live, key_heads, value_heads, key_live):
        scores = (
            jnp.einsum("qhd,khd->hqk", query_block, key_heads, preferred_element_type=jnp.float32)
            * score_scale
        )
        masked = jnp.where(key_live[None, None, :], scores, NEGATIVE)
        highest = jnp.max(masked, axis=-1, keepdims=True)
        log_total = highest + jnp.log(jnp.sum(jnp.exp(masked - highest), axis=-1, keepdims=True))
        weights = jnp.exp(masked - log_total).astype(jnp.bfloat16)
        mixed_rows = jnp.einsum(
            "hqk,khd->qhd", weights, value_heads, preferred_element_type=jnp.float32
        ).astype(jnp.bfloat16)
        valid_pair = jnp.logical_and(key_live[None, None, :], query_live[None, :, None])
        peak_logit = jnp.max(jnp.where(valid_pair, scores, NEGATIVE), axis=(1, 2))
        return (mixed_rows, log_total[:, :, 0], peak_logit)

    def forward_clip(inputs):
        clip_query, clip_key, clip_value, length = inputs
        key_heads = clip_key.reshape(frames, local_heads, head_dim)
        value_heads = clip_value.reshape(frames, local_heads, head_dim)
        key_live = frame_index < length
        query_blocks = clip_query.reshape(block_count, block_rows, local_heads, head_dim)
        live_blocks = key_live.reshape(block_count, block_rows)
        mixed_rows, log_total, peak_logit = lax.map(
            lambda element: forward_block(element[0], element[1], key_heads, value_heads, key_live),
            (query_blocks, live_blocks),
        )
        return (mixed_rows.reshape(frames, slab_width), log_total, jnp.max(peak_logit, axis=0))

    attended, log_totals, peaks = lax.map(forward_clip, (head_q, head_k, head_v, clip_lengths))
    local_peak = jnp.max(peaks, axis=0)
    peak_full = lax.dynamic_update_slice_in_dim(
        jnp.full((head_count,), NEGATIVE, jnp.float32),
        local_peak,
        lax.axis_index("seq") * local_heads,
        0,
    )
    logit_peak = lax.pmax(peak_full, ("fsdp", "seq"))
    merged = lax.all_to_all(attended, "seq", split_axis=1, concat_axis=2, tiled=True).reshape(
        tokens, model_width
    )
    after1 = residual + (
        jnp.dot(merged, out_part, preferred_element_type=jnp.float32) + vectors1[4]
    )
    plain2 = normalized(after1)
    up_part = lax.all_gather(up_weight, "fsdp", axis=0, tiled=True)
    gain_part = lax.all_gather(norm2_gain, "fsdp", axis=0, tiled=True)
    shift_part = lax.all_gather(norm2_bias, "fsdp", axis=0, tiled=True)
    dbias_part = lax.all_gather(down_bias, "fsdp", axis=0, tiled=True)
    columns = plain2
    blocked = (columns * gain_part.astype(jnp.float32) + shift_part.astype(jnp.float32)).astype(
        jnp.bfloat16
    )
    totals = jnp.dot(blocked, up_part, preferred_element_type=jnp.float32)
    normed = blocked
    vector_part = jnp.stack([gain_part, shift_part, dbias_part]).astype(jnp.float32)
    vectors = vector_part
    up_sums = totals
    down_part = lax.all_gather(down_weight, "fsdp", axis=0, tiled=True)
    ubias_part = lax.all_gather(up_bias, "fsdp", axis=0, tiled=True)
    shift_vector = ubias_part.astype(jnp.float32)
    before = up_sums + shift_vector
    active = jax.nn.gelu(before, approximate=False).astype(jnp.bfloat16)
    totals = jnp.dot(active, down_part, preferred_element_type=jnp.float32)
    output = (
        (after1 + (totals + vectors[2]))
        .astype(jnp.bfloat16)
        .reshape(clip_count, local_frames, model_width)
    )
    live_grad = out_grad.reshape(tokens, model_width).astype(jnp.float32) * live_mask
    live_grad_low = live_grad.astype(jnp.bfloat16)
    before_full = up_sums + shift_vector

    def down_back(down_part):
        grad_active = contract_last(live_grad_low, down_part)
        _, pullback = jax.vjp(lambda inside: jax.nn.gelu(inside, approximate=False), before_full)
        return pullback(grad_active)[0]

    grad_before = down_back(lax.all_gather(down_weight, "fsdp", axis=0, tiled=True)).astype(
        jnp.bfloat16
    )
    grad_normed2 = contract_last(grad_before, lax.all_gather(up_weight, "fsdp", axis=0, tiled=True))
    _, pull_second = jax.vjp(layer_norm, after1, vectors[0], vectors[1])
    back_after, grad_gain2, grad_shift2 = pull_second(grad_normed2)
    grad_after1 = live_grad + back_after
    grad_attn = grad_after1.astype(jnp.bfloat16)
    grad_merged = (
        contract_last(grad_attn, out_part)
        .astype(jnp.bfloat16)
        .reshape(clip_count, local_frames, model_width)
    )
    grad_heads = lax.all_to_all(grad_merged, "seq", split_axis=2, concat_axis=1, tiled=True)

    def backward_clip(inputs):
        clip_query, clip_key, clip_value, clip_grad, clip_log, length = inputs
        key_heads = clip_key.reshape(frames, local_heads, head_dim)
        value_heads = clip_value.reshape(frames, local_heads, head_dim)
        key_live = frame_index < length
        query_blocks = clip_query.reshape(block_count, block_rows, local_heads, head_dim)
        grad_blocks = clip_grad.reshape(block_count, block_rows, local_heads, head_dim)

        def backward_block(carry, element):
            grad_keys, grad_values = carry
            query_block, grad_block, log_total = element
            scores = (
                jnp.einsum(
                    "qhd,khd->hqk", query_block, key_heads, preferred_element_type=jnp.float32
                )
                * score_scale
            )
            masked = jnp.where(key_live[None, None, :], scores, NEGATIVE)
            probs = jnp.exp(masked - log_total[:, :, None])
            probs_low = probs.astype(jnp.bfloat16)
            grad_probs = jnp.einsum(
                "qhd,khd->hqk", grad_block, value_heads, preferred_element_type=jnp.float32
            )
            inner_sum = jnp.sum(probs * grad_probs, axis=-1, keepdims=True)
            grad_scores = (probs * (grad_probs - inner_sum)).astype(jnp.bfloat16)
            grad_query = (
                jnp.einsum(
                    "hqk,khd->qhd", grad_scores, key_heads, preferred_element_type=jnp.float32
                )
                * score_scale
            ).astype(jnp.bfloat16)
            grad_keys = (
                grad_keys
                + jnp.einsum(
                    "hqk,qhd->khd", grad_scores, query_block, preferred_element_type=jnp.float32
                )
                * score_scale
            )
            grad_values = grad_values + jnp.einsum(
                "hqk,qhd->khd", probs_low, grad_block, preferred_element_type=jnp.float32
            )
            return ((grad_keys, grad_values), grad_query)

        zero_heads = jnp.zeros((frames, local_heads, head_dim), jnp.float32)
        (grad_keys, grad_values), grad_queries = lax.scan(
            backward_block, (zero_heads, zero_heads), (query_blocks, grad_blocks, clip_log)
        )
        return (
            grad_queries.reshape(frames, slab_width),
            grad_keys.reshape(frames, slab_width).astype(jnp.bfloat16),
            grad_values.reshape(frames, slab_width).astype(jnp.bfloat16),
        )

    head_gq, head_gk, head_gv = lax.map(
        backward_clip, (head_q, head_k, head_v, grad_heads, log_totals, clip_lengths)
    )
    back_query, back_key, back_value = (
        lax.all_to_all(head_gq, "seq", split_axis=1, concat_axis=2, tiled=True),
        lax.all_to_all(head_gk, "seq", split_axis=1, concat_axis=2, tiled=True),
        lax.all_to_all(head_gv, "seq", split_axis=1, concat_axis=2, tiled=True),
    )
    grad_proj = jnp.concatenate(
        [
            back_query.reshape(tokens, model_width),
            back_key.reshape(tokens, model_width),
            back_value.reshape(tokens, model_width),
        ],
        axis=1,
    )
    joined = jnp.concatenate(
        [
            lax.all_gather(q_weight, "fsdp", axis=0, tiled=True),
            lax.all_gather(k_weight, "fsdp", axis=0, tiled=True),
            lax.all_gather(v_weight, "fsdp", axis=0, tiled=True),
        ],
        axis=1,
    )
    grad_normed1 = contract_last(grad_proj, joined)
    _, pull_first = jax.vjp(layer_norm, residual, vectors1[0], vectors1[1])
    back_input, grad_gain1, grad_shift1 = pull_first(grad_normed1)
    in_grad = (
        (grad_after1 + back_input)
        .astype(jnp.bfloat16)
        .reshape(clip_count, local_frames, model_width)
    )
    part_qkv = contract_first(normed1, grad_proj)
    part_out = contract_first(merged, grad_attn)
    part_up = contract_first(normed, grad_before)
    part_down = contract_first(active, live_grad_low).reshape(
        own_rows * lax.axis_size("fsdp"), expand_ratio * model_width
    )
    grad_shard = lax.psum_scatter(
        jnp.concatenate([part_qkv, part_out, part_up, part_down], axis=1).astype(jnp.bfloat16),
        "fsdp",
        scatter_dimension=0,
        tiled=True,
    ).astype(jnp.float32)
    grad_shard = lax.psum(grad_shard.astype(jnp.bfloat16), "seq").astype(jnp.float32)
    small_stack = jnp.stack(
        [
            grad_gain1,
            grad_shift1,
            jnp.sum(grad_proj[:, :model_width], axis=0, dtype=jnp.float32),
            jnp.sum(grad_proj[:, 2 * model_width :], axis=0, dtype=jnp.float32),
            jnp.sum(grad_attn, axis=0, dtype=jnp.float32),
            grad_gain2,
            grad_shift2,
            jnp.sum(live_grad, axis=0),
        ]
    )
    up_bias_sum = jnp.sum(grad_before, axis=0, dtype=jnp.float32)
    small_total, up_bias_total = lax.psum((small_stack, up_bias_sum), ("fsdp", "seq"))
    small_own = lax.dynamic_slice_in_dim(small_total, fsdp_index * own_rows, own_rows, 1)
    up_bias_grad = lax.dynamic_slice_in_dim(up_bias_total, fsdp_index * own_hidden, own_hidden, 0)
    q_weight_grad = grad_shard[:, :model_width]
    k_weight_grad = grad_shard[:, model_width : 2 * model_width]
    v_weight_grad = grad_shard[:, 2 * model_width : 3 * model_width]
    o_weight_grad = grad_shard[:, 3 * model_width : 4 * model_width]
    up_weight_grad = grad_shard[:, 4 * model_width : 4 * model_width + hidden]
    down_weight_grad = grad_shard[:, 4 * model_width + hidden :].reshape(
        own_rows * expand_ratio, model_width
    )
    factor = jnp.sqrt(LOGIT_CAP / jnp.maximum(logit_peak, LOGIT_CAP))
    column_factor = jnp.repeat(factor, head_dim)
    q_weight_clipped = q_weight.astype(jnp.float32) * column_factor[None, :]
    k_weight_clipped = k_weight.astype(jnp.float32) * column_factor[None, :]
    q_bias_clipped = q_bias.astype(jnp.float32) * lax.dynamic_slice_in_dim(
        column_factor, fsdp_index * own_rows, own_rows, 0
    )
    return (
        output,
        in_grad,
        small_own[0],
        small_own[1],
        q_weight_grad,
        small_own[2],
        k_weight_grad,
        v_weight_grad,
        small_own[3],
        o_weight_grad,
        small_own[4],
        small_own[5],
        small_own[6],
        up_weight_grad,
        up_bias_grad,
        down_weight_grad,
        small_own[7],
        logit_peak,
        q_weight_clipped,
        q_bias_clipped,
        k_weight_clipped,
    )


def solution(mesh):
    placed = (
        P("fsdp", "seq", None),
        P("fsdp"),
        P("fsdp"),
        P("fsdp"),
        P("fsdp", None),
        P("fsdp"),
        P("fsdp", None),
        P("fsdp", None),
        P("fsdp"),
        P("fsdp", None),
        P("fsdp"),
        P("fsdp"),
        P("fsdp"),
        P("fsdp", None),
        P("fsdp"),
        P("fsdp", None),
        P("fsdp"),
        P("fsdp", "seq", None),
    )
    return jax.shard_map(
        local,
        mesh=mesh,
        in_specs=placed,
        out_specs=(
            P("fsdp", "seq", None),
            P("fsdp", "seq", None),
            P("fsdp"),
            P("fsdp"),
            P("fsdp", None),
            P("fsdp"),
            P("fsdp", None),
            P("fsdp", None),
            P("fsdp"),
            P("fsdp", None),
            P("fsdp"),
            P("fsdp"),
            P("fsdp"),
            P("fsdp", None),
            P("fsdp"),
            P("fsdp", None),
            P("fsdp"),
            P(),
            P("fsdp", None),
            P("fsdp"),
            P("fsdp", None),
        ),
        check_vma=False,
    )
```

profile of v0, /device:TPU:0, one launch (start us, length us, event | category | flops | bytes accessed | tf_op | source)
XLA Modules:
  0.0 1251.4 jit_solution(12656311066407338932)
XLA Ops:
  16.2 63.5 %all-reduce.10 = (bf16[1280]{0:T(1024)(128)(2,1)S(1)}, bf16[1280]{0:T(1024)(128)(2,1)S(1)}, bf16[1280]{0:T(1024)(128)(2,1)S(1)}, bf16[1280]{0:T(1024)(128)(2,1)S...) all-reduce(bf16[1280]{0:T(1024)(128)(2,1)S(1)} %dynamic-update-slic, ...), channel_id=1, replica_groups=mesh['fsdp'=16,'seq'=2] {'fsdp'}, use_global_device_ids=true, to_apply=%add.1 | all-reduce | flops 15360 | bytes 61440
  84.5 22.2 %all-gather.9.cloned.1.call-done = bf16[1280,1280]{1,0:T(8,128)(2,1)} async-done(((bf16[80,1280]{1,0:T(8,128)(2,1)}), bf16[1280,1280]{1,0:T(8,128)(2,1)}) %all-gather.9.cloned.1.call-update) | async-done | bytes 3276816 | tf_op jit(solution)/shard_map/all_gather | solution.py:82
  110.7 43.0 %all-gather.11.cloned.1.call-done = bf16[1280,1280]{1,0:T(8,128)(2,1)} async-done(((bf16[80,1280]{1,0:T(8,128)(2,1)}), bf16[1280,1280]{1,0:T(8,128)(2,1)}) %all-gather.11.cloned.1.call-update) | async-done | bytes 3276816 | tf_op jit(solution)/shard_map/all_gather | solution.py:83
  157.6 8.1 fusion.83
  169.5 5.7 copy.109
  175.8 9.5 reduce.17
  195.8 5.7 copy.110
  201.6 9.5 reduce.18
  218.5 5.7 copy.112
  224.2 9.5 reduce.19
  250.8 7.8 all-to-all-done.2
  271.0 34.8 %while.52 = (s32[]{:T(128)}, bf16[2,512,8,80]{1,3,2,0:T(8,128)(2,1)}, f32[2,8,512]{2,1,0:T(8,128)S(1)}, f32[2,8]{1,0:T(2,128)S(1)}, bf16[2,512,8,80]{1,3,2,0:T(8...) while((s32[]{:T(128)}, ...), condition=%wide.region_6.7_spmd.clone, body=%wide.region_2.6_spmd.clone.sunk | while | flops 1397552128 | bytes 65936164 | solution.py:149
  276.1 7.1 select_reduce_fusion.2
  293.4 7.1 select_reduce_fusion.2
  310.3 10.6 reshape.378
  321.0 9.7 reduce.20
  336.3 15.5 %all-to-all-done.3 = bf16[2,2,163840]{2,1,0:T(2,128)(2,1)S(1)} async-done(((bf16[2,2,163840]{2,1,0:T(2,128)(2,1)}), bf16[2,2,163840]{2,1,0:T(2,128)(2,1)S(1)}, u32[]{:S(2)}, u32[]{:S(2)}) %all-to-all-start.3) | async-done | bytes 1310752 | tf_op jit(solution)/shard_map/all_to_all | solution.py:164
  365.4 34.4 %multiply_convert_fusion.1 = (bf16[512,5120]{1,0:T(8,128)(2,1)}, f32[512,5120]{1,0:T(8,128)}, f32[512,5120]{1,0:T(8,128)}) fusion(f32[5120]{0:T(1024)S(1)} %convert_element_type.165, bf16[1280,5120]{1,0:T(8,128)(2,1)} %all-gather.15.cloned.1.call-done, f32[512,1280]{1,0:T(8,128)} %copy-done.11, f32[1280]{0:T(1024)S(1)} %convert_element_type.163, ...), kind=kOutput, calls=%fused_computation.57 | convolution fusion | flops 6887178240 | bytes 41977856 | tf_op jit(solution)/shard_map/dot_general | solution.py:179
  399.9 10.2 all-gather.17.cloned.1.call-done
  410.0 20.4 %convert_reduce_fusion = (f32[5120]{0:T(1024)}, bf16[512,5120]{1,0:T(8,128)(2,1)}) fusion(f32[512,5120]{1,0:T(8,128)} %get-tuple-element.318, bf16[5120,1280]{1,0:T(8,128)(2,1)} %all-gather.17.cloned.1.call-done, bf16[1,512,1280]{2,1,0:T(8,128)(2,1)} %param.39, f32[512]{0:T(512)S(1)} %fusion.77, f32[512,5120]{1,0:T(8,128)} %get-tuple-element.344, ...), kind=kOutput, calls=%fused_computation.55 | convolution fusion | flops 6757411840 | bytes 40675328 | tf_op jit(solution)/shard_map/dot_general | solution.py:29
  430.4 14.9 %multiply_reduce_fusion.1 = (f32[1280]{0:T(1024)}, f32[512]{0:T(512)S(1)}, f32[1280]{0:T(1024)}, f32[512,1280]{1,0:T(8,128)}) fusion(f32[512,1280]{1,0:T(8,128)S(1)} %copy-done.12, f32[512]{0:T(512)S(1)} %fusion.79, f32[512]{0:T(512)S(1)} %broadcast_multiply_fusion, f32[1280]{0:T(1024)S(1)} %get-tuple-element.260, ...), kind=kOutput, calls=%fused_computation.106 | convolution fusion | flops 6716126208 | bytes 23614464 | tf_op jit(solution)/shard_map/dot_general | solution.py:29
  454.3 5.7 copy.117
  460.0 9.5 reduce.21
  476.9 17.2 %all-to-all-done.4 = bf16[2,2,163840]{2,1,0:T(2,128)(2,1)} async-done(((bf16[2,2,163840]{2,1,0:T(2,128)(2,1)}), bf16[2,2,163840]{2,1,0:T(2,128)(2,1)}, u32[]{:S(2)}, u32[]{:S(2)}) %all-to-all-start.4) | async-done | bytes 1310752 | tf_op jit(solution)/shard_map/all_to_all | solution.py:217
  499.3 90.6 %while.53 = (s32[]{:T(128)}, f32[1024,8,80]{0,2,1:T(8,128)}, f32[1024,8,80]{0,2,1:T(8,128)}, bf16[2,512,8,80]{1,3,2,0:T(8,128)(2,1)}, bf16[2,512,8,80]{1,3,2,0:T...) while((s32[]{:T(128)}, f32[1024,8,80]{0,2,1:T(8,128)}, ...), condition=%wide.region_13.14_spmd.clone, body=%wide.region_11.13_spmd.clone.sunk | while | flops 3397121024 | bytes 252660080 | solution.py:263
  503.9 10.7 multiply_reduce_fusion.5
  514.6 9.3 multiply_convert_fusion.3
  523.9 6.8 bitcast_add_fusion.4
  536.2 7.0 fusion.146
  548.8 10.7 multiply_reduce_fusion.5
  559.6 9.3 multiply_convert_fusion.3
  568.9 7.6 bitcast_add_fusion.4
  581.9 7.0 fusion.146
  598.1 9.7 reduce.22
  621.2 9.7 reduce.23
  638.0 13.3 %convolution_convert_fusion.1 = bf16[1280,5120]{1,0:T(8,128)(2,1)} fusion(bf16[512,5120]{1,0:T(8,128)(2,1)} %get-tuple-element.348, f32[512,1280]{1,0:T(8,128)S(1)} %copy-done.13, f32[1280]{0:T(1024)S(1)} %copy-done.55, f32[1280]{0:T(1024)S(1)} %copy-done.57, f32[512]{0:T(512)S(1)} %copy-done.62, f32[512]{0:T(512)S(1)} %copy-done.49), kind=kOutput, calls=%fused_computation.51 | convolution fusion | flops 6720716800 | bytes 20985856 | tf_op jit(solution)/shard_map/dot_general | solution.py:35
  655.4 8.8 reshape.379
  664.3 9.7 reduce.24
  681.0 14.2 %convolution_convert_fusion = bf16[5120,1280]{1,0:T(8,128)(2,1)} fusion(bf16[512,5120]{1,0:T(8,128)(2,1)} %get-tuple-element.317, bf16[1,512,1280]{2,1,0:T(8,128)(2,1)S(1)} %copy-done.27, f32[512]{0:T(512)S(1)} %copy-done.45), kind=kOutput, calls=%fused_computation.50 | convolution fusion | flops 6719406080 | bytes 19662848 | tf_op jit(solution)/shard_map/dot_general | solution.py:35
  695.2 20.7 %reshape.330 = bf16[1280,5120]{1,0:T(8,128)(2,1)} reshape(bf16[5120,1280]{1,0:T(8,128)(2,1)} %convolution_convert_fusion) | data formatting | bytes 26214400 | tf_op jit(solution)/shard_map/reshape | solution.py:307
  747.8 10.4 convolution_convert_fusion.2
  758.2 26.4 %pad_maximum_fusion = bf16[1280,15360]{1,0:T(8,128)(2,1)} fusion(bf16[1280,5120]{1,0:T(8,128)(2,1)} %reshape.330, bf16[1280,5120]{1,0:T(8,128)(2,1)} %convolution_convert_fusion.1, bf16[1280,1280]{1,0:T(8,128)(2,1)} %copy.125, bf16[1280,3840]{1,0:T(8,128)(2,1)} %convolution_convert_fusion.2), kind=kLoop, calls=%fused_computation.49 | loop fusion | flops 157286400 | bytes 78643200 | tf_op jit(solution)/shard_map/concatenate | solution.py:311
  785.5 39.1 %pmax.7 = f32[16]{0:T(128)S(1)} all-reduce(f32[16]{0:T(128)S(1)} %dynamic_update_slice.33), channel_id=1, replica_groups=mesh['fsdp'=16,'seq'=2] {'fsdp','seq'}, use_global_device_ids=true, to_apply=%region_30.31 | all-reduce | flops 16 | bytes 128 | tf_op jit(solution)/shard_map/pmax | solution.py:163
  826.4 17.3 %fusion.52 = bf16[1,512,1280]{2,1,0:T(8,128)(2,1)} fusion(f32[512,1280]{1,0:T(8,128)} %copy-done.11, bf16[512,5120]{1,0:T(8,128)(2,1)} %get-tuple-element.317, bf16[5120,1280]{1,0:T(8,128)(2,1)} %all-gather.17.cloned.1.call-done, f32[1280]{0:T(1024)S(1)} %copy-done.60), kind=kOutput, calls=%fused_computation.90 | convolution fusion | flops 6712852480 | bytes 22287360 | tf_op jit(solution)/shard_map/dot_general | solution.py:189
  843.8 319.4 %reduce-scatter.2.cloned.1.call-done = bf16[80,15360]{1,0:T(8,128)(2,1)} async-done(((bf16[1280,15360]{1,0:T(8,128)(2,1)}), bf16[80,15360]{1,0:T(8,128)(2,1)}) %reduce-scatter.2.cloned.1.call-update) | async-done | bytes 2457616 | tf_op jit(solution)/shard_map/reduce_scatter | solution.py:310
  1163.2 10.4 fusion.87
  1176.4 40.5 %all-reduce.9 = (f32[8,1280]{1,0:T(8,128)S(1)}, f32[5120]{0:T(1024)S(1)}) all-reduce(f32[8,1280]{1,0:T(8,128)S(1)} %stack.63, f32[5120]{0:T(1024)S(1)} %copy-done.39), channel_id=1, replica_groups=mesh['fsdp'=16,'seq'=2] {'fsdp','seq'}, use_global_device_ids=true, to_apply=%region_24.25 | all-reduce | flops 15360 | bytes 122880 | tf_op jit(solution)/shard_map/psum | solution.py:330
  1222.6 14.2 %all-reduce.13.cloned.1.call-done = bf16[80,15360]{1,0:T(8,128)(2,1)} async-done(((bf16[80,15360]{1,0:T(8,128)(2,1)}), bf16[80,15360]{1,0:T(8,128)(2,1)}) %all-reduce.13.cloned.1.call-update) | async-done | bytes 2457616 | tf_op jit(solution)/shard_map/psum | solution.py:316
  (358 shorter events, 248.7 us)
Async XLA Ops:
  7.3 73.3 %all-gather.7.cloned.1.call-start = ((), (), s32[]{:S(2)}) async-start(), calls=%async_computation.9 | async-start | bytes 3481600 | tf_op jit(solution)/shard_map/all_gather | solution.py:81
  8.0 98.6 %all-gather.9.cloned.1.call-start = ((), (), s32[]{:S(2)}) async-start(), calls=%async_computation.10 | async-start | bytes 3481600 | tf_op jit(solution)/shard_map/all_gather | solution.py:82
  8.8 144.8 %all-gather.11.cloned.1.call-start = ((), (), s32[]{:S(2)}) async-start(), calls=%async_computation.11 | async-start | bytes 3481600 | tf_op jit(solution)/shard_map/all_gather | solution.py:83
  9.5 349.3 %all-gather.13.cloned.1.call-start = ((), (), s32[]{:S(2)}) async-start(), calls=%async_computation.12 | async-start | bytes 3481600 | tf_op jit(solution)/shard_map/all_gather | solution.py:88
  10.1 355.3 %all-gather.15.cloned.1.call-start = ((), (), s32[]{:S(2)}) async-start(), calls=%async_computation.13 | async-start | bytes 13926400 | tf_op jit(solution)/shard_map/all_gather | solution.py:171
  10.7 399.3 %all-gather.17.cloned.1.call-start = ((), (), s32[]{:S(2)}) async-start(), calls=%async_computation.14 | async-start | bytes 13926400 | tf_op jit(solution)/shard_map/all_gather | solution.py:184
  11.5 146.1 %copy-start.37 = (f32[512]{0:T(512)}, f32[512]{0:T(512)S(1)}, u32[]{:S(2)}) copy-start(f32[512]{0:T(512)S(1)} %broadcast_multiply_fusion.1) | copy-start | bytes 6148
  12.0 72.5 %copy-start.40 = (f32[512]{0:T(512)}, f32[512]{0:T(512)S(1)}, u32[]{:S(2)}) copy-start(f32[512]{0:T(512)S(1)} %fusion.57) | copy-start | bytes 6148
  79.8 77.8 %copy-start.50 = (f32[1280]{0:T(1024)}, f32[1280]{0:T(1024)S(1)}, u32[]{:S(2)}) copy-start(f32[1280]{0:T(1024)S(1)} %convert_element_type.157) | copy-start | bytes 15364
  79.8 77.8 %copy-start.52 = (f32[1280]{0:T(1024)}, f32[1280]{0:T(1024)S(1)}, u32[]{:S(2)}) copy-start(f32[1280]{0:T(1024)S(1)} %convert_element_type.156) | copy-start | bytes 15364
  80.6 77.0 %copy-start.42 = (f32[512]{0:T(512)}, f32[512]{0:T(512)S(1)}, u32[]{:S(2)}) copy-start(f32[512]{0:T(512)S(1)} %fusion.78) | copy-start | bytes 6148
  188.2 25.8 %all-to-all-start = ((bf16[2,2,163840]{2,1,0:T(2,128)(2,1)}), bf16[2,2,163840]{2,1,0:T(2,128)(2,1)}, u32[]{:S(2)}, u32[]{:S(2)}) async-start(bf16[2,2,163840]{2,1,0:T(2,128)(2,1)} %reshape.387), calls=%async_computation | async-start | bytes 2621440 | tf_op jit(solution)/shard_map/all_to_all | solution.py:120
  213.9 22.7 %all-to-all-start.1 = ((bf16[2,2,163840]{2,1,0:T(2,128)(2,1)}), bf16[2,2,163840]{2,1,0:T(2,128)(2,1)}, u32[]{:S(2)}, u32[]{:S(2)}) async-start(bf16[2,2,163840]{2,1,0:T(2,128)(2,1)} %reshape.389), calls=%async_computation.1 | async-start | bytes 2621440 | tf_op jit(solution)/shard_map/all_to_all | solution.py:121
  236.6 21.9 %all-to-all-start.2 = ((bf16[2,2,163840]{2,1,0:T(2,128)(2,1)}), bf16[2,2,163840]{2,1,0:T(2,128)(2,1)}, u32[]{:S(2)}, u32[]{:S(2)}) async-start(bf16[2,2,163840]{2,1,0:T(2,128)(2,1)} %reshape.391), calls=%async_computation.2 | async-start | bytes 2621440 | tf_op jit(solution)/shard_map/all_to_all | solution.py:122
  305.8 15.1 %copy-start.2 = (bf16[1024,8,80]{0,2,1:T(8,128)(2,1)}, bf16[1024,8,80]{0,2,1:T(8,128)(2,1)S(1)}, u32[]{:S(2)}) copy-start(bf16[1024,8,80]{0,2,1:T(8,128)(2,1)S(1)} %get-tuple-element.558) | copy-start | bytes 3932164
  305.9 15.1 %copy-start.4 = (bf16[1024,8,80]{0,2,1:T(8,128)(2,1)}, bf16[1024,8,80]{0,2,1:T(8,128)(2,1)S(1)}, u32[]{:S(2)}) copy-start(bf16[1024,8,80]{0,2,1:T(8,128)(2,1)S(1)} %get-tuple-element.561) | copy-start | bytes 3932164
  305.9 15.1 %copy-start.32 = (f32[2,8,512]{2,1,0:T(8,128)}, f32[2,8,512]{2,1,0:T(8,128)S(1)}, u32[]{:S(2)}) copy-start(f32[2,8,512]{2,1,0:T(8,128)S(1)} %get-tuple-element.520) | copy-start | bytes 98308
  305.9 15.1 %copy-start.64 = (f32[2,8]{1,0:T(2,128)}, f32[2,8]{1,0:T(2,128)S(1)}, u32[]{:S(2)}) copy-start(f32[2,8]{1,0:T(2,128)S(1)} %get-tuple-element.189) | copy-start | bytes 196
  331.9 19.9 %all-to-all-start.3 = ((bf16[2,2,163840]{2,1,0:T(2,128)(2,1)}), bf16[2,2,163840]{2,1,0:T(2,128)(2,1)S(1)}, u32[]{:S(2)}, u32[]{:S(2)}) async-start(bf16[2,2,163840]{2,1,0:T(2,128)(2,1)} %reshape.393), calls=%async_computation.3 | async-start | bytes 2621440 | tf_op jit(solution)/shard_map/all_to_all | solution.py:164
  335.5 29.9 %copy-start.54 = (f32[1280]{0:T(1024)}, f32[1280]{0:T(1024)S(1)}, u32[]{:S(2)}) copy-start(f32[1280]{0:T(1024)S(1)} %convert_element_type.163) | copy-start | bytes 15364
  335.6 29.9 %copy-start.56 = (f32[1280]{0:T(1024)}, f32[1280]{0:T(1024)S(1)}, u32[]{:S(2)}) copy-start(f32[1280]{0:T(1024)S(1)} %convert_element_type.162) | copy-start | bytes 15364
  336.3 111.7 %copy-start.44 = (f32[512]{0:T(512)}, f32[512]{0:T(512)S(1)}, u32[]{:S(2)}) copy-start(f32[512]{0:T(512)S(1)} %fusion.77) | copy-start | bytes 6148
  363.4 81.9 %copy-start.48 = (f32[512]{0:T(512)}, f32[512]{0:T(512)S(1)}, u32[]{:S(2)}) copy-start(f32[512]{0:T(512)S(1)} %broadcast_multiply_fusion) | copy-start | bytes 6148
  365.4 79.9 %copy-start.61 = (f32[512]{0:T(512)}, f32[512]{0:T(512)S(1)}, u32[]{:S(2)}) copy-start(f32[512]{0:T(512)S(1)} %fusion.79) | copy-start | bytes 6148
  410.0 20.4 %copy-start.12 = (f32[512,1280]{1,0:T(8,128)S(1)}, f32[512,1280]{1,0:T(8,128)}, u32[]{:S(2)}) copy-start(f32[512,1280]{1,0:T(8,128)} %copy-done.11) | copy-start | bytes 7864324
  472.4 21.7 %all-to-all-start.4 = ((bf16[2,2,163840]{2,1,0:T(2,128)(2,1)}), bf16[2,2,163840]{2,1,0:T(2,128)(2,1)}, u32[]{:S(2)}, u32[]{:S(2)}) async-start(bf16[2,2,163840]{2,1,0:T(2,128)(2,1)} %reshape.395), calls=%async_computation.4 | async-start | bytes 2621440 | tf_op jit(solution)/shard_map/all_to_all | solution.py:217
  523.9 10.4 copy-start.7
  568.9 10.8 copy-start.5
  568.9 11.1 copy-start.7
  610.2 23.1 %all-to-all-start.7 = ((bf16[2,2,163840]{2,1,0:T(2,128)(2,1)}), bf16[2,2,163840]{2,1,0:T(2,128)(2,1)}, u32[]{:S(2)}, u32[]{:S(2)}) async-start(bf16[2,2,163840]{2,1,0:T(2,128)(2,1)} %reshape.397), calls=%async_computation.7 | async-start | bytes 2621440 | tf_op jit(solution)/shard_map/all_to_all | solution.py:278
  633.4 43.0 %all-to-all-start.6 = ((bf16[2,2,163840]{2,1,0:T(2,128)(2,1)}), bf16[2,2,163840]{2,1,0:T(2,128)(2,1)}, u32[]{:S(2)}, u32[]{:S(2)}) async-start(bf16[2,2,163840]{2,1,0:T(2,128)(2,1)} %reshape.399), calls=%async_computation.6 | async-start | bytes 2621440 | tf_op jit(solution)/shard_map/all_to_all | solution.py:277
  676.4 62.5 %all-to-all-start.5 = ((bf16[2,2,163840]{2,1,0:T(2,128)(2,1)}), bf16[2,2,163840]{2,1,0:T(2,128)(2,1)}, u32[]{:S(2)}, u32[]{:S(2)}) async-start(bf16[2,2,163840]{2,1,0:T(2,128)(2,1)} %reshape.401), calls=%async_computation.5 | async-start | bytes 2621440 | tf_op jit(solution)/shard_map/all_to_all | solution.py:276
  680.9 482.2 %reduce-scatter.2.cloned.1.call-start = ((), (), s32[]{:S(2)}) async-start(), calls=%async_computation.15 | async-start | bytes 41779200 | tf_op jit(solution)/shard_map/reduce_scatter | solution.py:310
  695.2 20.7 %copy-start.19 = (bf16[1,512,2,640]{1,3,2,0:T(8,128)(2,1)S(1)}, bf16[1,512,2,640]{1,3,2,0:T(8,128)(2,1)}, u32[]{:S(2)}) copy-start(bf16[1,512,2,640]{1,3,2,0:T(8,128)(2,1)} %copy-done.18) | copy-start | bytes 3932164
  695.2 20.7 %copy-start.29 = (bf16[512,1280]{1,0:T(8,128)(2,1)S(1)}, bf16[512,1280]{1,0:T(8,128)(2,1)}, u32[]{:S(2)}) copy-start(bf16[512,1280]{1,0:T(8,128)(2,1)} %copy-done.28) | copy-start | bytes 3932164
  784.6 40.2 %copy-start.67 = (bf16[80]{0:T(256)(128)(2,1)S(1)}, bf16[80]{0:T(256)(128)(2,1)}, u32[]{:S(2)}) copy-start(bf16[80]{0:T(256)(128)(2,1)} %param.27) | copy-start | bytes 484
  784.6 40.8 %copy-start.30 = (bf16[80,1280]{1,0:T(8,128)(2,1)S(1)}, bf16[80,1280]{1,0:T(8,128)(2,1)}, u32[]{:S(2)}) copy-start(bf16[80,1280]{1,0:T(8,128)(2,1)} %param.26) | copy-start | bytes 614404
  784.6 40.7 %copy-start.31 = (bf16[80,1280]{1,0:T(8,128)(2,1)S(1)}, bf16[80,1280]{1,0:T(8,128)(2,1)}, u32[]{:S(2)}) copy-start(bf16[80,1280]{1,0:T(8,128)(2,1)} %param.28) | copy-start | bytes 614404
  784.6 41.7 %copy-start.36 = (f32[1280]{0:T(1024)S(1)}, f32[1280]{0:T(1024)}, u32[]{:S(2)}) copy-start(f32[1280]{0:T(1024)} %get-tuple-element.313) | copy-start | bytes 15364
  784.7 41.7 %copy-start.59 = (f32[1280]{0:T(1024)S(1)}, f32[1280]{0:T(1024)}, u32[]{:S(2)}) copy-start(f32[1280]{0:T(1024)} %get-tuple-element.249) | copy-start | bytes 15364
  784.7 41.7 %copy-start.58 = (f32[1280]{0:T(1024)S(1)}, f32[1280]{0:T(1024)}, u32[]{:S(2)}) copy-start(f32[1280]{0:T(1024)} %get-tuple-element.253) | copy-start | bytes 15364
  784.7 41.7 %copy-start.35 = (f32[1280]{0:T(1024)S(1)}, f32[1280]{0:T(1024)}, u32[]{:S(2)}) copy-start(f32[1280]{0:T(1024)} %get-tuple-element.331) | copy-start | bytes 15364
  784.7 41.7 %copy-start.60 = (f32[1280]{0:T(1024)S(1)}, f32[1280]{0:T(1024)}, u32[]{:S(2)}) copy-start(f32[1280]{0:T(1024)} %get-tuple-element.261) | copy-start | bytes 15364
  784.7 452.0 %all-reduce.13.cloned.1.call-start = ((), (), s32[]{:S(2)}) async-start(), calls=%async_computation.16 | async-start | bytes 4915200 | tf_op jit(solution)/shard_map/psum | solution.py:316
  824.6 19.2 %copy-start.76 = (f32[16]{0:T(128)}, f32[16]{0:T(128)S(1)}, u32[]{:S(2)}) copy-start(f32[16]{0:T(128)S(1)} %pmax.7) | copy-start | bytes 196
  826.4 336.8 %copy-start.34 = (f32[1280]{0:T(1024)S(1)}, f32[1280]{0:T(1024)}, u32[]{:S(2)}) copy-start(f32[1280]{0:T(1024)} %get-tuple-element.256) | copy-start | bytes 15364
  1163.2 10.4 copy-start.41
  1173.6 44.5 %copy-start.47 = (f32[512]{0:T(512)S(1)}, f32[512]{0:T(512)}, u32[]{:S(2)}) copy-start(f32[512]{0:T(512)} %copy-done.46) | copy-start | bytes 6148
  (54 other events, 270.4 us)
Sparse Core Ops, SparseCore 0:
  10.4 49.3 all-gather.6
  62.1 44.5 all-gather.8
  109.0 44.6 all-gather.10
  155.8 44.8 all-gather.12
  202.8 102.9 all-gather.14
  307.9 102.0 all-gather.16
  784.8 378.2 reduce-scatter.1
  1165.5 71.2 all-reduce.12
where the time goes:
time: 1260 us; the launch traced here: 1250 us
  waiting for transfers between devices  453 us (36%)
  matrix products  232 us (18%)
  local copies, waits for them, and re-layouts  210 us (17%)
  other arithmetic  159 us (13%)
  blocking collectives  143 us (11%)
  starting transfers between devices  36 us (3%)
  between operations  17.5 us (1%)
    reduce_scatter x1, waiting for transfers between devices, local(): lax.psum_scatter(jnp.concatenate([part_qkv, part_out, part_up, part_down]...  319 us
    unnamed x184, local copies, waits for them, and re-layouts  76.7 us
    unnamed x10, other arithmetic  76.6 us
    unnamed x1, blocking collectives  63.5 us
    dot_general x4, matrix products, contract_last(): lax.dot_general(left, right, (((1,), (1,)), ((), ())), preferred_element_...  48.6 us
    all_gather x1, waiting for transfers between devices, local(): value_part = lax.all_gather(v_weight, 'fsdp', axis=0, tiled=True)  43 us
    dot_general x4, matrix products, contract_first(): lax.dot_general(left, right, (((0,), (0,)), ((), ())), preferred_element_...  41.7 us
    psum x1, blocking collectives, local(): lax.psum((small_stack, up_bias_sum), ('fsdp', 'seq'))  40.5 us
  transfers between devices with their start and end apart: 16, of which 8 were waited for; matrix products, arithmetic and copies ran while one was open for 29% of the time, Pallas kernels for 0%

commit v1 on v0

v1 whole, which is shorter than its diff:
```python
import math

import jax
import jax.numpy as jnp
from jax import lax
from jax.experimental import pallas as pl
from jax.experimental.pallas import tpu as pltpu
from jax.sharding import PartitionSpec as P

HEAD_DIM = 80
NEGATIVE = -1000000000.0
EPSILON = 1e-05
LOGIT_CAP = 10.0
LOG2E = 1.4426950408889634
VMEM_LIMIT = 56 * 1024 * 1024
f32 = jnp.float32
bf16 = jnp.bfloat16


def dot(left, right, left_dim, right_dim):
    return lax.dot_general(
        left, right, (((left_dim,), (right_dim,)), ((), ())), preferred_element_type=f32
    )


def nt(a, b):
    return dot(a, b, 1, 1)


def nn(a, b):
    return dot(a, b, 1, 0)


def tn(a, b):
    return dot(a, b, 0, 0)


def normalized(rows):
    centred = rows - jnp.mean(rows, axis=-1, keepdims=True)
    spread = jnp.mean(centred * centred, axis=-1, keepdims=True)
    scale = lax.rsqrt(spread + EPSILON)
    return centred * scale, scale


def norm_back(plain, scale, grad):
    first = jnp.mean(grad, axis=-1, keepdims=True)
    second = jnp.mean(grad * plain, axis=-1, keepdims=True)
    return scale * (grad - first - plain * second)


def one_row(width):
    return jnp.where(lax.broadcasted_iota(jnp.int32, (16, width), 0) == 0, 1.0, 0.0).astype(bf16)


def attend_kernel(tile, scale2, q_ref, k_ref, v_ref, mask_ref, o_ref, lse_ref, peak_ref):
    frames = q_ref.shape[1]
    mask_rows = mask_ref[...]
    keys = jnp.concatenate([k_ref[...], mask_rows], axis=0).T
    values = jnp.concatenate([v_ref[...], one_row(frames)], axis=0)
    ones = one_row(tile)
    for at in range(frames // tile):
        cols = pl.ds(at * tile, tile)
        q = jnp.concatenate([q_ref[:, cols], ones], axis=0)
        s = nn(keys, q)
        top = jnp.max(s, axis=0, keepdims=True)
        p = jnp.exp2(s * scale2 - top * scale2).astype(bf16)
        mixed = nn(values, p)
        total = mixed[HEAD_DIM : HEAD_DIM + 1, :]
        o_ref[:, cols] = (mixed[:HEAD_DIM, :] * (1.0 / total)).astype(bf16)
        lse_ref[0, :, cols] = top * scale2 + jnp.log2(total)
        live = mask_rows[0:1, at * tile : (at + 1) * tile].astype(f32) == 0.0
        peak_ref[0, :, cols] = jnp.where(live, top, NEGATIVE)


def attend(qkv, mask, clips, heads):
    frames = qkv.shape[1] // clips
    tile = frames
    scale2 = LOG2E / math.sqrt(HEAD_DIM)

    def row(off):
        return pl.BlockSpec((HEAD_DIM, frames), lambda b, h: (off + h, b))

    vec = pl.BlockSpec((1, 1, frames), lambda b, h: (b * heads + h, 0, 0))
    return pl.pallas_call(
        lambda *refs: attend_kernel(tile, scale2, *refs),
        grid=(clips, heads),
        in_specs=[
            row(0),
            row(heads),
            row(2 * heads),
            pl.BlockSpec((16, frames), lambda b, h: (b, 0)),
        ],
        out_specs=[row(0), vec, vec],
        out_shape=[
            jax.ShapeDtypeStruct((heads * HEAD_DIM, clips * frames), bf16),
            jax.ShapeDtypeStruct((clips * heads, 1, frames), f32),
            jax.ShapeDtypeStruct((clips * heads, 1, frames), f32),
        ],
        compiler_params=pltpu.CompilerParams(vmem_limit_bytes=VMEM_LIMIT),
        cost_estimate=pl.CostEstimate(
            flops=clips * heads * frames * frames * 2000,
            bytes_accessed=qkv.size * 3,
            transcendentals=clips * heads * frames * frames,
        ),
        name="attend",
    )(qkv, qkv, qkv, mask)


def attend_back_kernel(
    tile, scale, q_ref, k_ref, v_ref, mask_ref, g_ref, lse_ref, out_ref, gk, gv
):
    frames = q_ref.shape[1]
    scale2 = LOG2E * scale
    key_rows = k_ref[...]
    keys = jnp.concatenate([key_rows, mask_ref[...]], axis=0).T
    values = v_ref[...].T
    ones = one_row(tile)
    for at in range(frames // tile):
        cols = pl.ds(at * tile, tile)
        q = q_ref[:, cols]
        g = g_ref[:, cols]
        s = nn(keys, jnp.concatenate([q, ones], axis=0))
        p = jnp.exp2(s * scale2 - lse_ref[0, :, cols])
        t = p * nn(values, g)
        inner = jnp.sum(t, axis=0, keepdims=True)
        ds = (t - p * inner).astype(bf16)
        out_ref[0, :, cols] = (nn(key_rows, ds) * scale).astype(bf16)
        dk = nt(q, ds)
        dv = nt(g, p.astype(bf16))
        if at == 0:
            gk[...] = dk
            gv[...] = dv
        else:
            gk[...] += dk
            gv[...] += dv
    out_ref[1] = (gk[...] * scale).astype(bf16)
    out_ref[2] = gv[...].astype(bf16)


def attend_back(qkv, mask, grad, lse, clips, heads):
    frames = qkv.shape[1] // clips
    tile = min(512, frames)

    def row(off):
        return pl.BlockSpec((HEAD_DIM, frames), lambda b, h: (off + h, b))

    vec = pl.BlockSpec((1, 1, frames), lambda b, h: (b * heads + h, 0, 0))
    return pl.pallas_call(
        lambda *refs: attend_back_kernel(tile, 1.0 / math.sqrt(HEAD_DIM), *refs),
        grid=(clips, heads),
        in_specs=[
            row(0),
            row(heads),
            row(2 * heads),
            pl.BlockSpec((16, frames), lambda b, h: (b, 0)),
            row(0),
            vec,
        ],
        out_specs=pl.BlockSpec((3, HEAD_DIM, frames), lambda b, h: (0, h, b)),
        out_shape=jax.ShapeDtypeStruct((3, heads * HEAD_DIM, clips * frames), bf16),
        scratch_shapes=[pltpu.VMEM((HEAD_DIM, frames), f32), pltpu.VMEM((HEAD_DIM, frames), f32)],
        compiler_params=pltpu.CompilerParams(vmem_limit_bytes=VMEM_LIMIT),
        cost_estimate=pl.CostEstimate(
            flops=clips * heads * frames * frames * 4000,
            bytes_accessed=qkv.size * 6,
            transcendentals=clips * heads * frames * frames,
        ),
        name="attend_back",
    )(qkv, qkv, qkv, mask, grad, lse)


def gelu_parts(v):
    bell = jnp.exp2(v * v * (-0.5 * LOG2E))
    t = 1.0 / (1.0 + (0.3275911 / math.sqrt(2.0)) * jnp.abs(v))
    poly = t * (
        0.5 * 0.254829592
        + t * (0.5 * -0.284496736 + t * (0.5 * 1.421413741 + t * (0.5 * -1.453152027 + t * (0.5 * 1.061405429))))
    )
    tail = poly * bell
    return jnp.where(v < 0.0, tail, 1.0 - tail), bell * (1.0 / math.sqrt(2.0 * math.pi))


def feed_kernel(rows, n_ref, g_ref, up_ref, bias_ref, down_ref, act_ref, grad_ref, sum_ref):
    up = up_ref[...]
    down = down_ref[...]
    total = jnp.zeros(sum_ref.shape, f32)
    for at in range(n_ref.shape[0] // rows):
        part = pl.ds(at * rows, rows)
        before = nn(n_ref[part, :], up) + bias_ref[...]
        grad_act = nt(g_ref[part, :], down)
        cumulative, density = gelu_parts(before)
        act_ref[part, :] = (before * cumulative).astype(bf16)
        grad = ((cumulative + before * density) * grad_act).astype(bf16)
        grad_ref[part, :] = grad
        total = total + jnp.sum(grad.astype(f32), axis=0, keepdims=True)
    sum_ref[...] = total


def feed(normed, grad, up, bias, down):
    tokens, width = normed.shape
    hidden = up.shape[1]
    tile = 256 if hidden % 256 == 0 else hidden
    rows = 256 if tokens % 256 == 0 else tokens
    whole = pl.BlockSpec((tokens, width), lambda i: (0, 0))
    column = pl.BlockSpec((tokens, tile), lambda i: (0, i))
    line = pl.BlockSpec((1, tile), lambda i: (0, i))
    return pl.pallas_call(
        lambda *refs: feed_kernel(rows, *refs),
        grid=(hidden // tile,),
        in_specs=[
            whole,
            whole,
            pl.BlockSpec((width, tile), lambda i: (0, i)),
            line,
            pl.BlockSpec((tile, width), lambda i: (i, 0)),
        ],
        out_specs=[column, column, line],
        out_shape=[
            jax.ShapeDtypeStruct((tokens, hidden), bf16),
            jax.ShapeDtypeStruct((tokens, hidden), bf16),
            jax.ShapeDtypeStruct((1, hidden), f32),
        ],
        compiler_params=pltpu.CompilerParams(vmem_limit_bytes=VMEM_LIMIT),
        cost_estimate=pl.CostEstimate(
            flops=4 * tokens * width * hidden,
            bytes_accessed=2 * (2 * tokens * width + 2 * width * hidden + 2 * tokens * hidden),
            transcendentals=tokens * hidden,
        ),
        name="feed",
    )(normed, grad, up, bias, down)


def place(blocks, slots, cuts):
    count, (rows, width) = len(blocks), blocks[0].shape
    spans = list(zip((0,) + cuts, cuts + (rows,), strict=True))

    def kernel(slots_ref, *refs):
        for i in range(count):
            for target, (low, high) in zip(refs[count:], spans, strict=True):
                target[slots_ref[i]] = refs[i][low:high, :]

    return pl.pallas_call(
        kernel,
        in_specs=[pl.BlockSpec(memory_space=pltpu.SMEM)]
        + [pl.BlockSpec(memory_space=pltpu.VMEM)] * count,
        out_specs=[pl.BlockSpec(memory_space=pltpu.VMEM)] * len(spans),
        out_shape=[
            jax.ShapeDtypeStruct((count, high - low, width), blocks[0].dtype) for low, high in spans
        ],
        compiler_params=pltpu.CompilerParams(vmem_limit_bytes=VMEM_LIMIT),
        cost_estimate=pl.CostEstimate(
            flops=0, bytes_accessed=4 * count * rows * width, transcendentals=0
        ),
        name="place",
    )(slots, *blocks)


def local(
    frames_in,
    clip_lengths,
    norm1_gain,
    norm1_bias,
    q_weight,
    q_bias,
    k_weight,
    v_weight,
    v_bias,
    o_weight,
    o_bias,
    norm2_gain,
    norm2_bias,
    up_weight,
    up_bias,
    down_weight,
    down_bias,
    out_grad,
):
    clip_count, local_frames, width = frames_in.shape
    hidden = up_weight.shape[1]
    groups = lax.axis_size("seq")
    shards = lax.axis_size("fsdp")
    pairs = shards // 2
    depth = pairs // 2
    ranks = groups * 2
    frames = local_frames * groups
    tokens = clip_count * local_frames
    head_count = width // HEAD_DIM
    heads = head_count // ranks
    slab = heads * HEAD_DIM
    own_rows = width // shards
    own_hidden = hidden // shards
    piece = own_hidden * 2 // ranks
    rank_hidden = piece * pairs
    fsdp = lax.axis_index("fsdp")
    seq = lax.axis_index("seq")
    core, pair = fsdp % 2, fsdp // 2
    xpos, zpos = pair % 2, pair // 2
    rank = core * groups + seq

    core_way = [(i, i ^ 1) for i in range(shards)]
    x_way = [(i, i ^ 2) for i in range(shards)]

    def z_way(step):
        return [(i, (i + 4 * step) % shards) for i in range(shards)]

    def over_core(v):
        return lax.ppermute(v, "fsdp", core_way)

    def over_x(v):
        return lax.ppermute(v, "fsdp", x_way)

    def over_z(v, step):
        return lax.ppermute(v, "fsdp", z_way(step))

    def from_seq(v, step):
        return lax.ppermute(v, "seq", [(i, (i - step) % groups) for i in range(groups)])

    def to_seq(v, step):
        return from_seq(v, -step % groups)

    def share(own):
        side = [from_seq(own, step) for step in range(1, groups)]
        return [own] + side, [over_core(v) for v in [own] + side]

    def butterfly(v, combine):
        v = combine(v, over_core(v))
        v = combine(v, over_x(v))
        step = 4
        while step < shards:
            v = combine(v, lax.ppermute(v, "fsdp", [(i, i ^ step) for i in range(shards)]))
            step *= 2
        step = 1
        while step < groups:
            v = combine(v, lax.ppermute(v, "seq", [(i, i ^ step) for i in range(groups)]))
            step *= 2
        return v

    slots = []
    for step in range(depth):
        for flip in range(2):
            slots.append(((zpos - step) % depth) * 2 + (xpos ^ flip))
    slots = jnp.stack(slots).astype(jnp.int32)

    def spread(payload, cuts=()):
        blocks = [payload] + [over_z(payload, step) for step in range(1, depth)]
        both = []
        for block in blocks:
            both += [block, over_x(block)]
        return place(both, slots, cuts)

    def by_core(mine, other):
        return jnp.where(
            core == 0, jnp.concatenate([mine, other]), jnp.concatenate([other, mine])
        )

    vectors = [norm1_gain, norm1_bias, q_bias, v_bias, o_bias, norm2_gain, norm2_bias, down_bias]
    small = jnp.concatenate(vectors + [up_bias])
    small_rows = -(-small.shape[0] // (3 * slab))
    small = jnp.pad(small, (0, small_rows * 3 * slab - small.shape[0])).reshape(small_rows, 3 * slab)

    def head_columns(of):
        return jnp.concatenate(
            [lax.dynamic_slice_in_dim(w, of * slab, slab, 1) for w in (q_weight, k_weight, v_weight)], axis=1
        )

    qkv_own = by_core(head_columns(rank), over_core(head_columns((1 - core) * groups + seq)))
    small_pair = by_core(small, over_core(small))
    extra = -(-2 * small_rows // 16) * 16
    small_pair = jnp.pad(small_pair, ((0, extra - 2 * small_rows), (0, 0)))
    qkv_part, small_part = spread(
        jnp.concatenate([qkv_own, small_pair]), (2 * own_rows,)
    )
    qkv_full = qkv_part.reshape(width, 3 * slab)
    small_all = small_part[:, : 2 * small_rows].reshape(shards, small_rows * 3 * slab)
    gain1, shift1, qbias, vbias, obias, gain2, shift2, dbias = [
        small_all[:, i * own_rows : (i + 1) * own_rows].reshape(width).astype(f32)
        for i in range(8)
    ]
    ubias = (
        small_all[:, 8 * own_rows : 8 * own_rows + own_hidden]
        .reshape(pairs, ranks, piece)
    )
    ubias = lax.dynamic_index_in_dim(ubias, rank, 1, keepdims=False).reshape(1, rank_hidden).astype(f32)

    same_core = [[i for i in range(shards) if i % 2 == c] for c in range(2)]
    up_cols = up_weight.reshape(own_rows, pairs, ranks, piece)

    def hidden_columns(of):
        return lax.dynamic_index_in_dim(up_cols, of, 2, keepdims=False).reshape(own_rows, rank_hidden)

    up_own = by_core(hidden_columns(rank), over_core(hidden_columns((1 - core) * groups + seq)))
    down_own = lax.dynamic_slice_in_dim(down_weight, seq * piece, piece, 0)
    feed_own = jnp.concatenate([up_own.reshape(2 * own_rows * rank_hidden // width, width), down_own])
    feed_full = lax.all_gather(feed_own, "fsdp", axis=0, axis_index_groups=same_core)
    up_rows = up_own.size // width
    up_full = feed_full[:, :up_rows].reshape(width, rank_hidden)
    down_full = feed_full[:, up_rows:].reshape(rank_hidden, width)

    half = width // 2

    def half_columns(of):
        return lax.dynamic_slice_in_dim(o_weight, of * half, half, 1)

    (out_half,) = spread(by_core(half_columns(core), over_core(half_columns(1 - core))))
    out_half = out_half.reshape(width, half)
    out_other = over_core(out_half)
    out_full = jnp.where(
        core == 0,
        jnp.concatenate([out_half, out_other], axis=1),
        jnp.concatenate([out_other, out_half], axis=1),
    )

    frames_own = frames_in.reshape(tokens, width)
    positions = jnp.concatenate(
        [
            ((seq + step) % groups) * local_frames + jnp.arange(local_frames, dtype=jnp.int32)
            for step in range(groups)
        ]
    )
    lengths_sent = jnp.broadcast_to(clip_lengths.astype(f32)[:, None], (clip_count, 128))
    lengths = jnp.concatenate(
        [clip_lengths, over_core(lengths_sent)[:, 0].astype(jnp.int32)]
    )
    clips = 2 * clip_count
    live = positions[None, :] < lengths[:, None]
    live_own = live[:clip_count, :local_frames].reshape(tokens, 1)
    mask = jnp.where(live, 0.0, NEGATIVE).astype(bf16)
    mask = jnp.pad(mask[:, None, :], ((0, 0), (0, 15), (0, 0))).reshape(clips * 16, frames)
    live_grad = jnp.where(live_own, out_grad.reshape(tokens, width), 0.0).astype(bf16)

    def by_clip(blocks):
        parts = [v.reshape(clip_count, local_frames, -1) for v in blocks]
        return jnp.concatenate(parts, axis=1).reshape(clip_count * frames, -1)

    mine, others = share(frames_own)
    frames_all = jnp.concatenate([by_clip(mine), by_clip(others)])

    residual = frames_own.astype(f32)
    plain1_all, _ = normalized(frames_all.astype(f32))
    normed1 = (plain1_all * gain1 + shift1).astype(bf16)
    zero_bias = jnp.zeros((slab,), f32)
    head_bias = jnp.concatenate(
        [
            lax.dynamic_slice_in_dim(qbias, rank * slab, slab, 0),
            zero_bias,
            lax.dynamic_slice_in_dim(vbias, rank * slab, slab, 0),
        ]
    )
    qkv = (dot(qkv_full, normed1, 0, 1) + head_bias[:, None]).astype(bf16)
    mixed, log_totals, tops = attend(qkv, mask, clips, heads)

    top_heads = jnp.max(tops.reshape(clips, heads, frames), axis=(0, 2)) / math.sqrt(HEAD_DIM)
    peak_all = lax.dynamic_update_slice_in_dim(
        jnp.full((head_count,), NEGATIVE, f32), top_heads, rank * heads, 0
    )
    logit_peak = butterfly(peak_all.reshape(1, head_count), jnp.maximum).reshape(head_count)

    span = clip_count * frames

    def token_block(v, flip, step):
        cut = v[:, flip * span : (flip + 1) * span].reshape(slab, clip_count, groups, local_frames)
        return cut[:, :, step].reshape(slab, tokens)

    def heads_to_tokens(v):
        full = jnp.zeros((width, tokens), v.dtype)
        for flip in range(2):
            for step in range(groups):
                block = token_block(v, flip, step)
                if step:
                    block = to_seq(block, step)
                if flip:
                    block = over_core(block)
                source = (core ^ flip) * groups + (seq - step) % groups
                full = lax.dynamic_update_slice_in_dim(full, block, source * slab, 0)
        return full

    def tokens_to_heads(v):
        halves = []
        for flip in range(2):
            parts = []
            for step in range(groups):
                target = (core ^ flip) * groups + (seq + step) % groups
                block = lax.dynamic_slice_in_dim(v, target * slab, slab, 0)
                if step:
                    block = to_seq(block, step)
                if flip:
                    block = over_core(block)
                parts.append((step, block))
            parts = [parts[-step % groups][1] for step in range(groups)]
            parts = [v.reshape(slab, clip_count, 1, local_frames) for v in parts]
            halves.append(jnp.concatenate(parts, axis=2).reshape(slab, span))
        return jnp.concatenate(halves, axis=1)

    def sum_to_own(near, far):
        near_mine, near_other = near[:tokens], near[tokens:].astype(bf16)
        total = near_mine + over_core(near_other).astype(f32)
        for step in range(1, groups):
            cut = far[(step - 1) * 2 * tokens : step * 2 * tokens]
            both = cut[:tokens] + over_core(cut[tokens:].astype(bf16)).astype(f32)
            total = total + to_seq(both.astype(bf16), step).astype(f32)
        return total

    mixed_own = heads_to_tokens(mixed)
    after1 = residual + (tn(mixed_own, out_full) + obias)
    plain2, scale2 = normalized(after1)
    normed2 = (plain2 * gain2 + shift2).astype(bf16)

    def near_far(own):
        mine, others = share(own)
        near = jnp.concatenate([mine[0], others[0]])
        far = jnp.concatenate([v for pair_of in zip(mine[1:], others[1:], strict=True) for v in pair_of])
        return near, far

    normed2_near, normed2_far = near_far(normed2)
    grad_near, grad_far = near_far(live_grad)
    act_near, back_near, sums_near = feed(normed2_near, grad_near, up_full, ubias, down_full)
    act_far, back_far, sums_far = feed(normed2_far, grad_far, up_full, ubias, down_full)

    grad_normed2 = sum_to_own(nt(back_near, up_full), nt(back_far, up_full))
    fed = sum_to_own(nn(act_near, down_full), nn(act_far, down_full))
    output = (after1 + (fed + dbias)).astype(bf16).reshape(clip_count, local_frames, width)

    feed_grad = jnp.concatenate(
        [
            (tn(normed2_near, back_near) + tn(normed2_far, back_far)).astype(bf16),
            (tn(act_near, grad_near) + tn(act_far, grad_far)).astype(bf16).reshape(width, -1),
        ],
        axis=1,
    )
    feed_shard = lax.psum_scatter(
        feed_grad, "fsdp", scatter_dimension=0, axis_index_groups=same_core, tiled=True
    )

    live_low = live_grad.astype(f32)
    grad_after1 = live_low + norm_back(plain2, scale2, grad_normed2 * gain2)
    grad_attn = grad_after1.astype(bf16)
    grad_mixed = tokens_to_heads(nt(out_full, grad_attn).astype(bf16))
    grad_qkv = attend_back(qkv, mask, grad_mixed, log_totals, clips, heads).reshape(3 * slab, -1)

    def reduce_spread(v):
        blocks = v.reshape(depth, 2, width // pairs, -1)
        kept = lax.dynamic_index_in_dim(blocks, xpos, 1, keepdims=False).astype(f32)
        sent = lax.dynamic_index_in_dim(blocks, 1 - xpos, 1, keepdims=False)
        both = kept + over_x(sent).astype(f32)
        total = lax.dynamic_index_in_dim(both, zpos, 0, keepdims=False)
        for step in range(1, depth):
            block = lax.dynamic_index_in_dim(both.astype(bf16), (zpos + step) % depth, 0, keepdims=False)
            total = total + over_z(block, step).astype(f32)
        return total

    qkv_grad = reduce_spread(dot(normed1, grad_qkv, 0, 1).astype(bf16)).astype(bf16)
    near_of = [0, span]
    grad_tokens = dot(grad_qkv, qkv_full, 0, 1)
    shift1_sum = jnp.sum(grad_tokens, axis=0)
    gain1_sum = jnp.sum(grad_tokens * plain1_all, axis=0)
    token_cut = grad_tokens.reshape(2, clip_count, groups, local_frames, width)
    near = token_cut[:, :, 0].reshape(2 * tokens, width)
    far = jnp.concatenate([token_cut[:, :, step].reshape(2 * tokens, width) for step in range(1, groups)])
    grad_normed1 = sum_to_own(near, far)
    plain1, scale1 = normalized(residual)
    in_grad = (grad_after1 + norm_back(plain1, scale1, grad_normed1 * gain1)).astype(bf16)

    out_blocks = tn_out = nn(mixed_own, grad_attn).reshape(pairs, 2, own_rows, width)
    out_keep = lax.dynamic_index_in_dim(out_blocks, core, 1, keepdims=False)
    out_send = lax.dynamic_index_in_dim(out_blocks, 1 - core, 1, keepdims=False).astype(bf16)
    out_sum = (out_keep + over_core(out_send).astype(f32)).reshape(pairs * own_rows, groups, width // groups)
    out_total = lax.dynamic_index_in_dim(out_sum, seq, 1, keepdims=False)
    for step in range(1, groups):
        block = lax.dynamic_index_in_dim(out_sum.astype(bf16), (seq + step) % groups, 1, keepdims=False)
        out_total = out_total + to_seq(block, step).astype(f32)
    out_blocks = out_total.astype(bf16).reshape(depth, 2, own_rows, width // groups)
    kept = lax.dynamic_index_in_dim(out_blocks, xpos, 1, keepdims=False).astype(f32)
    sent = lax.dynamic_index_in_dim(out_blocks, 1 - xpos, 1, keepdims=False)
    both = kept + over_x(sent).astype(f32)
    out_shard = lax.dynamic_index_in_dim(both, zpos, 0, keepdims=False)
    for step in range(1, depth):
        block = lax.dynamic_index_in_dim(both.astype(bf16), (zpos + step) % depth, 0, keepdims=False)
        out_shard = out_shard + over_z(block, step).astype(f32)
    out_shard = out_shard.astype(bf16)

    def along_seq(v):
        full = jnp.zeros((groups,) + v.shape, v.dtype)
        for step in range(groups):
            block = from_seq(v, step) if step else v
            full = lax.dynamic_update_index_in_dim(full, block, (seq + step) % groups, 0)
        return full

    def own_of_ranks(v):
        cut = v.reshape(2, own_rows, -1)
        keep = lax.dynamic_index_in_dim(cut, core, 0, keepdims=True)
        other = over_core(lax.dynamic_index_in_dim(cut, 1 - core, 0, keepdims=True))
        return jnp.swapaxes(along_seq(by_core(keep, other)), 0, 1)

    up_shard = feed_shard[:, :rank_hidden]
    down_shard = feed_shard[:, rank_hidden:].reshape(piece, width)
    up_weight_grad = (
        own_of_ranks(up_shard)
        .reshape(2, groups, own_rows, pairs, piece)
        .transpose(2, 3, 0, 1, 4)
        .reshape(own_rows, hidden)
        .astype(f32)
    )
    down_weight_grad = along_seq(down_shard).reshape(own_hidden, width).astype(f32)
    qkv_own_grad = (
        own_of_ranks(qkv_grad)
        .reshape(2, groups, own_rows, 3, slab)
        .transpose(3, 2, 0, 1, 4)
        .reshape(3, own_rows, width)
        .astype(f32)
    )
    o_weight_grad = along_seq(out_shard).transpose(1, 0, 2).reshape(own_rows, width).astype(f32)

    bias_cols = jnp.sum(grad_qkv.astype(f32), axis=1)

    def at_rank(v):
        return lax.dynamic_update_slice_in_dim(jnp.zeros((width,), f32), v, rank * slab, 0)

    up_sums = lax.dynamic_update_index_in_dim(
        jnp.zeros((pairs, ranks, piece), f32), (sums_near + sums_far).reshape(pairs, piece), rank, 1
    ).reshape(hidden // width, width)
    stack = jnp.concatenate(
        [
            jnp.stack(
                [
                    gain1_sum,
                    shift1_sum,
                    at_rank(bias_cols[:slab]),
                    at_rank(bias_cols[2 * slab :]),
                    jnp.sum(grad_attn.astype(f32), axis=0),
                    jnp.sum(grad_normed2 * plain2, axis=0),
                    jnp.sum(grad_normed2, axis=0),
                    jnp.sum(live_low, axis=0),
                ]
            ),
            up_sums,
        ]
    )
    stack = butterfly(stack, jnp.add)
    small_own = lax.dynamic_slice_in_dim(stack[:8], fsdp * own_rows, own_rows, 1)
    up_bias_grad = lax.dynamic_slice_in_dim(stack[8:].reshape(hidden), fsdp * own_hidden, own_hidden, 0)

    factor = jnp.sqrt(LOGIT_CAP / jnp.maximum(logit_peak, LOGIT_CAP))
    column_factor = jnp.repeat(factor, HEAD_DIM)
    q_weight_clipped = q_weight.astype(f32) * column_factor[None, :]
    k_weight_clipped = k_weight.astype(f32) * column_factor[None, :]
    q_bias_clipped = q_bias.astype(f32) * lax.dynamic_slice_in_dim(
        column_factor, fsdp * own_rows, own_rows, 0
    )
    return (
        output,
        in_grad.reshape(clip_count, local_frames, width),
        small_own[0],
        small_own[1],
        qkv_own_grad[0],
        small_own[2],
        qkv_own_grad[1],
        qkv_own_grad[2],
        small_own[3],
        o_weight_grad,
        small_own[4],
        small_own[5],
        small_own[6],
        up_weight_grad,
        up_bias_grad,
        down_weight_grad,
        small_own[7],
        logit_peak,
        q_weight_clipped,
        q_bias_clipped,
        k_weight_clipped,
    )


def solution(mesh):
    rows, vector, clip = P("fsdp", None), P("fsdp"), P("fsdp", "seq", None)
    return jax.shard_map(
        local,
        mesh=mesh,
        in_specs=(
            clip,
            vector,
            vector,
            vector,
            rows,
            vector,
            rows,
            rows,
            vector,
            rows,
            vector,
            vector,
            vector,
            rows,
            vector,
            rows,
            vector,
            clip,
        ),
        out_specs=(
            clip,
            clip,
            vector,
            vector,
            rows,
            vector,
            rows,
            rows,
            vector,
            rows,
            vector,
            vector,
            vector,
            rows,
            vector,
            rows,
            vector,
            P(),
            rows,
            vector,
            rows,
        ),
        check_vma=False,
    )
```

time: 1260 us -> 705 us (0.56)
  waiting for transfers between devices: 453 us -> 222 us
  blocking collectives: 143 us -> 0 us
  matrix products: 232 us -> 101 us
  local copies, waits for them, and re-layouts: 210 us -> 124 us
  other arithmetic: 159 us -> 73.2 us
  Pallas kernels: 0 us -> 84.6 us
  starting transfers between devices: 36 us -> 73.5 us
    reduce_scatter x1, waiting for transfers between devices: 319 us -> 0.01 us  [local(): lax.psum_scatter(feed_grad, 'fsdp', scatter_dimension=0, axis_index_group...]
    ppermute x0 -> x72, waiting for transfers between devices: none -> 221 us  [the longest x15 99.5 us: from_seq(): lax.ppermute(v, 'seq', [(i, (i - step) % groups) for i in range(groups)])]
    dot_general x26 -> x14, matrix products: 232 us -> 101 us  [dot(): lax.dot_general(left, right, (((left_dim,), (right_dim,)), ((), ())), pre...]
    pallas_call x0 -> x6, Pallas kernels: none -> 84.6 us  [the longest x1 31.7 us: attend_back(): pl.pallas_call(lambda *refs: attend_back_kernel(tile, 1.0 / math.sqrt(HEA...]
    unnamed x10 -> x4, other arithmetic: 76.6 us -> 0.01 us
    all_gather x6 -> x1, waiting for transfers between devices: 75.4 us -> 0.01 us  [local(): lax.all_gather(feed_own, 'fsdp', axis=0, axis_index_groups=same_core)]
    ppermute x0 -> x72, starting transfers between devices: none -> 73.4 us  [the longest x12 25.1 us: over_z(): return lax.ppermute(v, 'fsdp', z_way(step))]
    unnamed x1 -> x0, blocking collectives: 63.5 us -> none
  transfers between devices with their start and end apart: 16 -> 74, of which waited for: 8 -> 27; matrix products, arithmetic and copies ran while one was open for 29% -> 36% of each run, Pallas kernels for 0% -> 10%
where the time goes in v1:
time: 705 us; the launch traced here: 695 us
  waiting for transfers between devices  222 us (31%)
  local copies, waits for them, and re-layouts  124 us (18%)
  matrix products  101 us (14%)
  Pallas kernels  84.6 us (12%)
  starting transfers between devices  73.5 us (10%)
  other arithmetic  73.2 us (10%)
  between operations  16.9 us (2%)
    dot_general x14, matrix products, dot(): lax.dot_general(left, right, (((left_dim,), (right_dim,)), ((), ())), pre...  101 us
    ppermute x15, waiting for transfers between devices, from_seq(): lax.ppermute(v, 'seq', [(i, (i - step) % groups) for i in range(groups)])  99.5 us
    ppermute x12, waiting for transfers between devices, over_z(): return lax.ppermute(v, 'fsdp', z_way(step))  55.8 us
    ppermute x12, waiting for transfers between devices, over_x(): return lax.ppermute(v, 'fsdp', x_way)  54.2 us
    pallas_call x1, Pallas kernels, attend_back(): pl.pallas_call(lambda *refs: attend_back_kernel(tile, 1.0 / math.sqrt(HEA...  31.7 us
    pallas_call x2, Pallas kernels, feed(): pl.pallas_call(lambda *refs: feed_kernel(rows, *refs), grid=(hidden // ti...  30.1 us
    ppermute x12, starting transfers between devices, over_z(): return lax.ppermute(v, 'fsdp', z_way(step))  25.1 us
    unnamed x153, local copies, waits for them, and re-layouts  23.4 us
  transfers between devices with their start and end apart: 74, of which 27 were waited for; matrix products, arithmetic and copies ran while one was open for 36% of the time, Pallas kernels for 10%

profile of v1, /device:TPU:0, one launch (start us, length us, event | category | flops | bytes accessed | tf_op | source)
XLA Modules:
  0.0 694.5 jit_solution(13480294346589475013)
XLA Ops:
  7.3 6.2 concatenate.150
  29.1 4.9 dynamic-slice_reduce_fusion.1
  52.3 7.1 %collective-permute-start.3 = (bf16[176,960]{1,0:T(8,128)(2,1)S(1)}, bf16[176,960]{1,0:T(8,128)(2,1)}, u32[]{:S(2)}, u32[]{:S(2)}) collective-permute-start(bf16[176,960]{1,0:T(8,128)(2,1)S(1)} %fusion.42.refs_0_), channel_id=1, source_target_pairs={{0,8},{2,10},{4,12},{6,14},{8,16},{10,18},{12,20},{14,22},{16,24},... | collective-permute-start | bytes 1013768 | tf_op jit(solution)/shard_map/ppermute | solution.py:313
  61.8 5.6 collective-permute-start.7
  69.4 18.7 %collective-permute-done.5.refs_4_ = bf16[176,960]{1,0:T(8,128)(2,1)} collective-permute-done((bf16[176,960]{1,0:T(8,128)(2,1)S(1)}, bf16[176,960]{1,0:T(8,128)(2,1)}, u32[]{:S(2)}, u32[]{:S(2)}) %collective-permute-start.5) | collective-permute-done | bytes 337952 | tf_op jit(solution)/shard_map/ppermute | solution.py:313
  88.7 7.1 %collective-permute-done.7.refs_6_ = bf16[176,960]{1,0:T(8,128)(2,1)} collective-permute-done((bf16[176,960]{1,0:T(8,128)(2,1)S(1)}, bf16[176,960]{1,0:T(8,128)(2,1)}, u32[]{:S(2)}, u32[]{:S(2)}) %collective-permute-start.7) | collective-permute-done | bytes 337952 | tf_op jit(solution)/shard_map/ppermute | solution.py:313
  99.2 4.5 collective-permute-done.24.refs_7_
  111.4 7.8 %collective-permute-done.6.refs_5_ = bf16[176,960]{1,0:T(8,128)(2,1)} collective-permute-done((bf16[176,960]{1,0:T(8,128)(2,1)}, bf16[176,960]{1,0:T(8,128)(2,1)}, u32[]{:S(2)}, u32[]{:S(2)}) %collective-permute-start.6) | collective-permute-done | bytes 337952 | tf_op jit(solution)/shard_map/ppermute | solution.py:310
  119.2 13.7 %collective-permute-done.8.refs_7_ = bf16[176,960]{1,0:T(8,128)(2,1)} collective-permute-done((bf16[176,960]{1,0:T(8,128)(2,1)}, bf16[176,960]{1,0:T(8,128)(2,1)}, u32[]{:S(2)}, u32[]{:S(2)}) %collective-permute-start.8) | collective-permute-done | bytes 337952 | tf_op jit(solution)/shard_map/ppermute | solution.py:310
  146.8 9.4 %add_convert_fusion.refs_0_.refs_1_.refs_2_ = bf16[960,2048]{1,0:T(8,128)(2,1)} fusion(f32[960]{0:T(1024)S(1)} %pad_maximum_fusion.9, bf16[1280,960]{1,0:T(8,128)(2,1)S(1)} %bitcast.290, f32[1280]{0:T(1024)S(1)} %reshape.551, f32[1280]{0:T(1024)S(1)} %reshape.550, f32[2048]{0:T(1024)S(1)} %add_rsqrt_fusion, f32[2048]{0:T(1024)S(1)} %broadcast_multiply_fusion, ...), kind=kOutput, calls=%fused_computation.13 | convolution fusion | flops 5060689920 | bytes 11663104 | tf_op jit(solution)/shard_map/dot_general | solution.py:21
  156.2 16.4 %attend.1 = (bf16[320,2048]{1,0:T(8,128)(2,1)}, f32[8,1,1024]{2,1,0:T(1,128)}, f32[8,1,1024]{2,1,0:T(1,128)}) custom-call(bf16[960,2048]{1,0:T(8,128)(2,1)} %add_convert_fusion.refs_0_.refs_1_.refs_2_, bf16[960,2048]{1,0:T(8,128)(2,1)} %add_convert_fusion.refs_0_.refs_1_.refs_2_, bf16[960,2048]{1,0:T(8,128)(2,1)} %add_convert_fusion.refs_0_.refs_1_.refs_2_, ...), custom_call_target="tpu_custom_call" | custom-call | flops 16777216000 | bytes 5898240 | tf_op jit(solution)/shard_map/attend/pallas_call | solution.py:84
  180.9 5.8 collective-permute-done.15
  186.8 6.9 collective-permute-done.13
  193.8 5.4 fusion.75
  205.9 16.0 %collective-permute-done.32 = bf16[512,1280]{1,0:T(8,128)(2,1)} collective-permute-done((bf16[512,1280]{1,0:T(8,128)(2,1)}, bf16[512,1280]{1,0:T(8,128)(2,1)}, u32[]{:S(2)}, u32[]{:S(2)}) %collective-permute-start.32) | collective-permute-done | bytes 1310752 | tf_op jit(solution)/shard_map/ppermute | solution.py:316
  221.9 4.3 collective-permute-start.69
  229.6 3.8 collective-permute-start.70
  236.4 10.0 %collective-permute-done.71 = f32[1,16]{1,0:T(1,128)S(1)} collective-permute-done((f32[1,16]{1,0:T(1,128)S(1)}, f32[1,16]{1,0:T(1,128)S(1)}, u32[]{:S(2)}, u32[]{:S(2)}) %collective-permute-start.71) | collective-permute-done | bytes 96 | tf_op jit(solution)/shard_map/ppermute | solution.py:334
  258.1 6.1 fusion.68
  264.2 14.9 %feed.3 = (bf16[1024,1280]{1,0:T(8,128)(2,1)}, bf16[1024,1280]{1,0:T(8,128)(2,1)}, f32[1,1280]{1,0:T(1,128)}) custom-call(bf16[1024,1280]{1,0:T(8,128)(2,1)} %constant_dynamic-update-slice_fusion.4.refs_0_, bf16[1024,1280]{1,0:T(8,128)(2,1)} %constant_dynamic-update-slice_fusion.6.refs_1_, bf16[1280,1280]{1,0:T(8,128)(2,1)} %bitcast.252, ...), custom_call_target="tpu_custom_call" | custom-call | flops 6710886400 | bytes 17039360 | tf_op jit(solution)/shard_map/feed/pallas_call | solution.py:207
  279.1 5.3 fusion.79
  288.5 15.2 %feed.2 = (bf16[1024,1280]{1,0:T(8,128)(2,1)}, bf16[1024,1280]{1,0:T(8,128)(2,1)}, f32[1,1280]{1,0:T(1,128)}) custom-call(bf16[1024,1280]{1,0:T(8,128)(2,1)} %pad_maximum_fusion.2.refs_0_, bf16[1024,1280]{1,0:T(8,128)(2,1)} %pad_maximum_fusion.3.refs_1_, bf16[1280,1280]{1,0:T(8,128)(2,1)} %bitcast.253, f32[1,1280]{1,0:T(1,128)} %reshape.557.refs_3_, ...), custom_call_target="tpu_custom_call" | custom-call | flops 6710886400 | bytes 17039360 | tf_op jit(solution)/shard_map/feed/pallas_call | solution.py:207
  303.7 5.5 fusion.78
  323.0 8.3 %fusion.57 = f32[1280,1280]{0,1:T(8,128)} fusion(bf16[1024,1280]{1,0:T(8,128)(2,1)S(1)} %copy-done.60, bf16[512,1280]{1,0:T(8,128)(2,1)} %collective-permute-done.27, bf16[512,1280]{1,0:T(8,128)(2,1)} %get-tuple-element.62), kind=kOutput, calls=%fused_computation.210 | convolution fusion | flops 3360686080 | bytes 11796480 | tf_op jit(solution)/shard_map/dot_general | solution.py:21
  331.3 8.6 %fusion.9 = bf16[1280,1280]{0,1:T(8,128)(2,1)S(1)} fusion(f32[1280,1280]{0,1:T(8,128)} %fusion.57, bf16[1024,1280]{1,0:T(8,128)(2,1)} %get-tuple-element.36, bf16[1024,1280]{1,0:T(8,128)(2,1)} %constant_dynamic-update-slice_fusion.6.refs_1_), kind=kOutput, calls=%fused_computation.15 | convolution fusion | flops 3358720000 | bytes 15073280 | tf_op jit(solution)/shard_map/dot_general | solution.py:21
  339.9 8.9 %fusion.58 = f32[1280,1280]{0,1:T(8,128)} fusion(bf16[1024,1280]{1,0:T(8,128)(2,1)} %get-tuple-element.37, bf16[512,1280]{1,0:T(8,128)(2,1)} %collective-permute-done.26, bf16[512,1280]{1,0:T(8,128)(2,1)} %add_convert_fusion.1), kind=kOutput, calls=%fused_computation.211 | convolution fusion | flops 3360686080 | bytes 11796480 | tf_op jit(solution)/shard_map/dot_general | solution.py:21
  355.0 8.0 %fusion.8 = bf16[1280,1280]{0,1:T(8,128)(2,1)S(1)} fusion(f32[1280,1280]{0,1:T(8,128)} %fusion.58, bf16[1024,1280]{1,0:T(8,128)(2,1)} %constant_dynamic-update-slice_fusion.4.refs_0_, bf16[1024,1280]{1,0:T(8,128)(2,1)} %get-tuple-element.38), kind=kOutput, calls=%fused_computation.14 | convolution fusion | flops 3358720000 | bytes 15073280 | tf_op jit(solution)/shard_map/dot_general | solution.py:21
  363.0 20.4 %collective-permute-done.38 = bf16[512,1280]{1,0:T(8,128)(2,1)} collective-permute-done((bf16[512,1280]{1,0:T(8,128)(2,1)}, bf16[512,1280]{1,0:T(8,128)(2,1)}, u32[]{:S(2)}, u32[]{:S(2)}) %collective-permute-start.38) | collective-permute-done | bytes 1310752 | tf_op jit(solution)/shard_map/ppermute | solution.py:316
  386.5 24.5 %collective-permute-done.35 = bf16[512,1280]{1,0:T(8,128)(2,1)S(1)} collective-permute-done((bf16[512,1280]{1,0:T(8,128)(2,1)}, bf16[512,1280]{1,0:T(8,128)(2,1)S(1)}, u32[]{:S(2)}, u32[]{:S(2)}) %collective-permute-start.35) | collective-permute-done | bytes 1310752 | tf_op jit(solution)/shard_map/ppermute | solution.py:316
  411.1 4.1 convert_reduce_fusion.4
  415.2 4.8 convolution_convert_fusion.1
  424.7 9.6 %copy.118 = bf16[1280,2560]{1,0:T(8,128)(2,1)} copy(bf16[1280,2560]{0,1:T(8,128)(2,1)} %pad_maximum_fusion) | data formatting | bytes 13107200
  436.4 5.9 fusion.54
  447.4 31.7 %attend_back.1 = bf16[3,320,2048]{2,1,0:T(8,128)(2,1)} custom-call(bf16[960,2048]{1,0:T(8,128)(2,1)} %add_convert_fusion.refs_0_.refs_1_.refs_2_, bf16[960,2048]{1,0:T(8,128)(2,1)} %add_convert_fusion.refs_0_.refs_1_.refs_2_, bf16[960,2048]{1,0:T(8,128)(2,1)} %add_convert_fusion.refs_0_.refs_1_.refs_2_, bf16[32,1024]{1,0:T(8,128)(2,1)} %bitcast.287, ...), custom_call_target="tpu_custom_call" | custom-call | flops 33554432000 | bytes 11796480 | tf_op jit(solution)/shard_map/attend_back/pallas_call | solution.py:148
  479.2 13.7 %fusion.61 = (f32[1280]{0:T(1024)S(1)}, f32[1280]{0:T(1024)S(1)}, f32[2048,1280]{1,0:T(8,128)}) fusion(f32[2048]{0:T(1024)S(1)} %copy-done.54, f32[2048]{0:T(1024)S(1)} %copy-done.47, bf16[1024,1280]{1,0:T(8,128)(2,1)S(1)} %copy-done.8, bf16[1024,1280]{1,0:T(8,128)(2,1)S(1)} %copy-done.6, bf16[960,2048]{1,0:T(8,128)(2,1)} %bitcast.246, ...), kind=kOutput, calls=%fused_computation.212 | convolution fusion | flops 5056755712 | bytes 22145024 | tf_op jit(solution)/shard_map/dot_general | solution.py:21
  499.1 9.6 %convolution_convert_fusion = bf16[1280,960]{0,1:T(8,128)(2,1)} fusion(bf16[960,2048]{1,0:T(8,128)(2,1)} %bitcast.247, f32[1280]{0:T(1024)S(1)} %copy-done.52, f32[1280]{0:T(1024)S(1)} %copy-done.45, f32[2048]{0:T(1024)S(1)} %copy-done.54, f32[2048]{0:T(1024)S(1)} %copy-done.47, bf16[1024,1280]{1,0:T(8,128)(2,1)S(1)} %copy-done.9, ...), kind=kOutput, calls=%fused_computation.21 | convolution fusion | flops 5057986560 | bytes 11659264 | tf_op jit(solution)/shard_map/dot_general | solution.py:21
  513.5 4.6 copy.103
  518.1 4.8 collective-permute-start.49
  529.4 3.7 slice_bitcast_fusion.3
  536.8 5.5 reshape.544
  542.2 22.3 %collective-permute-done.51 = bf16[4,160,960]{2,1,0:T(8,128)(2,1)} collective-permute-done((bf16[4,160,960]{2,1,0:T(8,128)(2,1)}, bf16[4,160,960]{2,1,0:T(8,128)(2,1)}, u32[]{:S(2)}, u32[]{:S(2)}) %collective-permute-start.51) | collective-permute-done | bytes 1228832 | tf_op jit(solution)/shard_map/ppermute | solution.py:310
  564.6 3.6 fusion.65
  577.9 20.3 %collective-permute-done.53 = bf16[160,960]{1,0:T(8,128)(2,1)S(1)} collective-permute-done((bf16[160,960]{1,0:T(8,128)(2,1)S(1)}, bf16[160,960]{1,0:T(8,128)(2,1)S(1)}, u32[]{:S(2)}, u32[]{:S(2)}) %collective-permute-start.53) | collective-permute-done | bytes 307232 | tf_op jit(solution)/shard_map/ppermute | solution.py:313
  637.7 6.1 collective-permute-done.63
  647.2 3.8 fusion.62
  658.2 8.5 %collective-permute-done.66 = bf16[160,1280]{1,0:T(8,128)(2,1)S(1)} collective-permute-done((bf16[160,1280]{1,0:T(8,128)(2,1)S(1)}, bf16[160,1280]{1,0:T(8,128)(2,1)S(1)}, u32[]{:S(2)}, u32[]{:S(2)}) %collective-permute-start.66) | collective-permute-done | bytes 409632 | tf_op jit(solution)/shard_map/ppermute | solution.py:316
  668.1 6.1 collective-permute-done.65
  681.7 5.8 reshape.562
  (471 shorter events, 223.9 us)
Async XLA Ops:
  7.2 250.9 %all-gather.3.cloned.1.call-start = ((), (), s32[]{:S(2)}) async-start(), calls=%async_computation.1 | async-start | bytes 7372800 | tf_op jit(solution)/shard_map/all_gather | solution.py:394
  13.4 25.6 %collective-permute-start.1 = (bf16[1,960]{1,0:T(2,128)(2,1)S(1)}, bf16[1,960]{1,0:T(2,128)(2,1)}, u32[]{:S(2)}, u32[]{:S(2)}) collective-permute-start(bf16[1,960]{1,0:T(2,128)(2,1)S(1)} %reshape.511), channel_id=1, source_target_pairs={{0,2},{2,0},{4,6},{6,4},{8,10},{10,8},{12,14},{14,12},{16,18},{18,... | collective-permute-start | bytes 5768 | tf_op jit(solution)/shard_map/ppermute | solution.py:307
  18.1 25.8 %collective-permute-start = (bf16[80,960]{1,0:T(8,128)(2,1)}, bf16[80,960]{1,0:T(8,128)(2,1)}, u32[]{:S(2)}, u32[]{:S(2)}) collective-permute-start(bf16[80,960]{1,0:T(8,128)(2,1)} %pad_maximum_fusion.8), channel_id=1, source_target_pairs={{0,2},{2,0},{4,6},{6,4},{8,10},{10,8},{12,14},{14,12},{16,18},{18,... | collective-permute-start | bytes 460808 | tf_op jit(solution)/shard_map/ppermute | solution.py:307
  18.2 78.1 %collective-permute-start.9 = (bf16[512,1280]{1,0:T(8,128)(2,1)}, bf16[512,1280]{1,0:T(8,128)(2,1)}, u32[]{:S(2)}, u32[]{:S(2)}) collective-permute-start(bf16[512,1280]{1,0:T(8,128)(2,1)} %bitcast.231), channel_id=1, source_target_pairs={{0,1},{1,0},{2,3},{3,2},{4,5},{5,4},{6,7},{7,6},{8,9},{9,8},{10,11... | collective-permute-start | bytes 3932168 | tf_op jit(solution)/shard_map/ppermute | solution.py:316
  22.3 20.1 %collective-permute-start.12 = (f32[1,128]{1,0:T(1,128)}, f32[1,128]{1,0:T(1,128)}, u32[]{:S(2)}, u32[]{:S(2)}) collective-permute-start(f32[1,128]{1,0:T(1,128)} %broadcast_in_dim.107), channel_id=1, source_target_pairs={{0,2},{2,0},{4,6},{6,4},{8,10},{10,8},{12,14},{14,12},{16,18},{18,... | collective-permute-start | bytes 1544 | tf_op jit(solution)/shard_map/ppermute | solution.py:307
  23.9 15.9 %collective-permute-start.17 = (bf16[80,640]{1,0:T(8,128)(2,1)}, bf16[80,640]{1,0:T(8,128)(2,1)}, u32[]{:S(2)}, u32[]{:S(2)}) collective-permute-start(bf16[80,640]{1,0:T(8,128)(2,1)} %get-tuple-element.98), channel_id=1, source_target_pairs={{0,2},{2,0},{4,6},{6,4},{8,10},{10,8},{12,14},{14,12},{16,18},{18,... | collective-permute-start | bytes 307208 | tf_op jit(solution)/shard_map/ppermute | solution.py:307
  44.0 17.0 %collective-permute-start.21 = (bf16[160,640]{1,0:T(8,128)(2,1)S(1)}, bf16[160,640]{1,0:T(8,128)(2,1)S(1)}, u32[]{:S(2)}, u32[]{:S(2)}) collective-permute-start(bf16[160,640]{1,0:T(8,128)(2,1)S(1)} %maximum_select_fusion.9.refs_0_), channel_id=1, source_target_pairs={{0,16},{2,18},{4,20},{6,22},{8,24},{10,26},{12,28},{14,30},{16,0},... | collective-permute-start | bytes 614408 | tf_op jit(solution)/shard_map/ppermute | solution.py:313
  46.6 15.2 %collective-permute-start.23 = (bf16[160,640]{1,0:T(8,128)(2,1)S(1)}, bf16[160,640]{1,0:T(8,128)(2,1)S(1)}, u32[]{:S(2)}, u32[]{:S(2)}) collective-permute-start(bf16[160,640]{1,0:T(8,128)(2,1)S(1)} %maximum_select_fusion.9.refs_0_), channel_id=1, source_target_pairs={{0,24},{2,26},{4,28},{6,30},{8,0},{10,2},{12,4},{14,6},{16,8},{18,... | collective-permute-start | bytes 614408 | tf_op jit(solution)/shard_map/ppermute | solution.py:313
  49.2 18.9 %collective-permute-start.2 = (bf16[176,960]{1,0:T(8,128)(2,1)S(1)}, bf16[176,960]{1,0:T(8,128)(2,1)S(1)}, u32[]{:S(2)}, u32[]{:S(2)}) collective-permute-start(bf16[176,960]{1,0:T(8,128)(2,1)S(1)} %fusion.42.refs_0_), channel_id=1, source_target_pairs={{0,4},{2,6},{4,0},{6,2},{8,12},{10,14},{12,8},{14,10},{16,20},{18,... | collective-permute-start | bytes 1013768 | tf_op jit(solution)/shard_map/ppermute | solution.py:310
  52.3 16.6 %collective-permute-start.3 = (bf16[176,960]{1,0:T(8,128)(2,1)S(1)}, bf16[176,960]{1,0:T(8,128)(2,1)}, u32[]{:S(2)}, u32[]{:S(2)}) collective-permute-start(bf16[176,960]{1,0:T(8,128)(2,1)S(1)} %fusion.42.refs_0_), channel_id=1, source_target_pairs={{0,8},{2,10},{4,12},{6,14},{8,16},{10,18},{12,20},{14,22},{16,24},... | collective-permute-start | bytes 1013768 | tf_op jit(solution)/shard_map/ppermute | solution.py:313
  61.0 27.1 %collective-permute-start.5 = (bf16[176,960]{1,0:T(8,128)(2,1)S(1)}, bf16[176,960]{1,0:T(8,128)(2,1)}, u32[]{:S(2)}, u32[]{:S(2)}) collective-permute-start(bf16[176,960]{1,0:T(8,128)(2,1)S(1)} %fusion.42.refs_0_), channel_id=1, source_target_pairs={{0,16},{2,18},{4,20},{6,22},{8,24},{10,26},{12,28},{14,30},{16,0},... | collective-permute-start | bytes 1013768 | tf_op jit(solution)/shard_map/ppermute | solution.py:313
  61.8 33.9 %collective-permute-start.7 = (bf16[176,960]{1,0:T(8,128)(2,1)S(1)}, bf16[176,960]{1,0:T(8,128)(2,1)}, u32[]{:S(2)}, u32[]{:S(2)}) collective-permute-start(bf16[176,960]{1,0:T(8,128)(2,1)S(1)} %fusion.42.refs_0_), channel_id=1, source_target_pairs={{0,24},{2,26},{4,28},{6,30},{8,0},{10,2},{12,4},{14,6},{16,8},{18,... | collective-permute-start | bytes 1013768 | tf_op jit(solution)/shard_map/ppermute | solution.py:313
  68.1 71.5 %collective-permute-start.10 = (bf16[512,1280]{1,0:T(8,128)(2,1)S(1)}, bf16[512,1280]{1,0:T(8,128)(2,1)}, u32[]{:S(2)}, u32[]{:S(2)}) collective-permute-start(bf16[512,1280]{1,0:T(8,128)(2,1)S(1)} %bitcast.232), channel_id=1, source_target_pairs={{0,2},{2,0},{4,6},{6,4},{8,10},{10,8},{12,14},{14,12},{16,18},{18,... | collective-permute-start | bytes 3932168 | tf_op jit(solution)/shard_map/ppermute | solution.py:307
  68.9 28.1 %collective-permute-start.20 = (bf16[160,640]{1,0:T(8,128)(2,1)S(1)}, bf16[160,640]{1,0:T(8,128)(2,1)S(1)}, u32[]{:S(2)}, u32[]{:S(2)}) collective-permute-start(bf16[160,640]{1,0:T(8,128)(2,1)S(1)} %collective-permute-done.19.refs_2_), channel_id=1, source_target_pairs={{0,4},{2,6},{4,0},{6,2},{8,12},{10,14},{12,8},{14,10},{16,20},{18,... | collective-permute-start | bytes 614408 | tf_op jit(solution)/shard_map/ppermute | solution.py:310
  96.3 43.3 %collective-permute-start.11 = (bf16[512,1280]{1,0:T(8,128)(2,1)}, bf16[512,1280]{1,0:T(8,128)(2,1)}, u32[]{:S(2)}, u32[]{:S(2)}) collective-permute-start(bf16[512,1280]{1,0:T(8,128)(2,1)} %collective-permute-done.9), channel_id=1, source_target_pairs={{0,2},{2,0},{4,6},{6,4},{8,10},{10,8},{12,14},{14,12},{16,18},{18,... | collective-permute-start | bytes 3932168 | tf_op jit(solution)/shard_map/ppermute | solution.py:307
  97.1 14.3 %collective-permute-start.4 = (bf16[176,960]{1,0:T(8,128)(2,1)}, bf16[176,960]{1,0:T(8,128)(2,1)S(1)}, u32[]{:S(2)}, u32[]{:S(2)}) collective-permute-start(bf16[176,960]{1,0:T(8,128)(2,1)} %collective-permute-done.3.refs_2_), channel_id=1, source_target_pairs={{0,4},{2,6},{4,0},{6,2},{8,12},{10,14},{12,8},{14,10},{16,20},{18,... | collective-permute-start | bytes 1013768 | tf_op jit(solution)/shard_map/ppermute | solution.py:310
  98.6 20.6 %collective-permute-start.6 = (bf16[176,960]{1,0:T(8,128)(2,1)}, bf16[176,960]{1,0:T(8,128)(2,1)}, u32[]{:S(2)}, u32[]{:S(2)}) collective-permute-start(bf16[176,960]{1,0:T(8,128)(2,1)} %collective-permute-done.5.refs_4_), channel_id=1, source_target_pairs={{0,4},{2,6},{4,0},{6,2},{8,12},{10,14},{12,8},{14,10},{16,20},{18,... | collective-permute-start | bytes 1013768 | tf_op jit(solution)/shard_map/ppermute | solution.py:310
  104.3 28.6 %collective-permute-start.8 = (bf16[176,960]{1,0:T(8,128)(2,1)}, bf16[176,960]{1,0:T(8,128)(2,1)}, u32[]{:S(2)}, u32[]{:S(2)}) collective-permute-start(bf16[176,960]{1,0:T(8,128)(2,1)} %collective-permute-done.7.refs_6_), channel_id=1, source_target_pairs={{0,4},{2,6},{4,0},{6,2},{8,12},{10,14},{12,8},{14,10},{16,20},{18,... | collective-permute-start | bytes 1013768 | tf_op jit(solution)/shard_map/ppermute | solution.py:310
  106.0 546.9 %reduce-scatter.4.cloned.1.call-start = ((), (), s32[]{:S(2)}) async-start(), calls=%async_computation.2 | async-start | bytes 7372800 | tf_op jit(solution)/shard_map/reduce_scatter | solution.py:530
  111.4 82.4 %collective-permute-start.25 = (bf16[1280,640]{1,0:T(8,128)(2,1)}, bf16[1280,640]{1,0:T(8,128)(2,1)}, u32[]{:S(2)}, u32[]{:S(2)}) collective-permute-start(bf16[1280,640]{1,0:T(8,128)(2,1)} %bitcast.270), channel_id=1, source_target_pairs={{0,2},{2,0},{4,6},{6,4},{8,10},{10,8},{12,14},{14,12},{16,18},{18,... | collective-permute-start | bytes 4915208 | tf_op jit(solution)/shard_map/ppermute | solution.py:307
  177.0 16.7 %collective-permute-start.13 = (bf16[320,512]{1,0:T(8,128)(2,1)S(1)}, bf16[320,512]{1,0:T(8,128)(2,1)S(1)}, u32[]{:S(2)}, u32[]{:S(2)}) collective-permute-start(bf16[320,512]{1,0:T(8,128)(2,1)S(1)} %bitcast.282), channel_id=1, source_target_pairs={{0,1},{1,0},{2,3},{3,2},{4,5},{5,4},{6,7},{7,6},{8,9},{9,8},{10,11... | collective-permute-start | bytes 983048 | tf_op jit(solution)/shard_map/ppermute | solution.py:316
  180.5 41.4 %collective-permute-start.32 = (bf16[512,1280]{1,0:T(8,128)(2,1)}, bf16[512,1280]{1,0:T(8,128)(2,1)}, u32[]{:S(2)}, u32[]{:S(2)}) collective-permute-start(bf16[512,1280]{1,0:T(8,128)(2,1)} %get-tuple-element.62), channel_id=1, source_target_pairs={{0,1},{1,0},{2,3},{3,2},{4,5},{5,4},{6,7},{7,6},{8,9},{9,8},{10,11... | collective-permute-start | bytes 3932168 | tf_op jit(solution)/shard_map/ppermute | solution.py:316
  180.8 12.9 %collective-permute-start.14 = (bf16[320,512]{1,0:T(8,128)(2,1)S(1)}, bf16[320,512]{1,0:T(8,128)(2,1)S(1)}, u32[]{:S(2)}, u32[]{:S(2)}) collective-permute-start(bf16[320,512]{1,0:T(8,128)(2,1)S(1)} %bitcast.284), channel_id=1, source_target_pairs={{0,2},{2,0},{4,6},{6,4},{8,10},{10,8},{12,14},{14,12},{16,18},{18,... | collective-permute-start | bytes 983048 | tf_op jit(solution)/shard_map/ppermute | solution.py:307
  193.7 32.5 %collective-permute-start.27 = (bf16[512,1280]{1,0:T(8,128)(2,1)}, bf16[512,1280]{1,0:T(8,128)(2,1)}, u32[]{:S(2)}, u32[]{:S(2)}) collective-permute-start(bf16[512,1280]{1,0:T(8,128)(2,1)} %get-tuple-element.62), channel_id=1, source_target_pairs={{0,2},{2,0},{4,6},{6,4},{8,10},{10,8},{12,14},{14,12},{16,18},{18,... | collective-permute-start | bytes 3932168 | tf_op jit(solution)/shard_map/ppermute | solution.py:307
  201.2 46.4 %collective-permute-start.30 = (bf16[512,1280]{1,0:T(8,128)(2,1)}, bf16[512,1280]{1,0:T(8,128)(2,1)}, u32[]{:S(2)}, u32[]{:S(2)}) collective-permute-start(bf16[512,1280]{1,0:T(8,128)(2,1)} %add_convert_fusion.1), channel_id=1, source_target_pairs={{0,1},{1,0},{2,3},{3,2},{4,5},{5,4},{6,7},{7,6},{8,9},{9,8},{10,11... | collective-permute-start | bytes 3932168 | tf_op jit(solution)/shard_map/ppermute | solution.py:316
  205.1 16.8 %collective-permute-start.68 = (f32[1,16]{1,0:T(1,128)S(1)}, f32[1,16]{1,0:T(1,128)S(1)}, u32[]{:S(2)}, u32[]{:S(2)}) collective-permute-start(f32[1,16]{1,0:T(1,128)S(1)} %max.18), channel_id=1, source_target_pairs={{0,4},{2,6},{4,0},{6,2},{8,12},{10,14},{12,8},{14,10},{16,20},{18,... | collective-permute-start | bytes 200 | tf_op jit(solution)/shard_map/ppermute | solution.py:310
  221.9 26.7 %collective-permute-start.33 = (bf16[512,1280]{1,0:T(8,128)(2,1)}, bf16[512,1280]{1,0:T(8,128)(2,1)}, u32[]{:S(2)}, u32[]{:S(2)}) collective-permute-start(bf16[512,1280]{1,0:T(8,128)(2,1)} %collective-permute-done.32), channel_id=1, source_target_pairs={{0,2},{2,0},{4,6},{6,4},{8,10},{10,8},{12,14},{14,12},{16,18},{18,... | collective-permute-start | bytes 3932168 | tf_op jit(solution)/shard_map/ppermute | solution.py:307
  236.4 17.2 %collective-permute-start.26 = (bf16[512,1280]{1,0:T(8,128)(2,1)}, bf16[512,1280]{1,0:T(8,128)(2,1)}, u32[]{:S(2)}, u32[]{:S(2)}) collective-permute-start(bf16[512,1280]{1,0:T(8,128)(2,1)} %add_convert_fusion.1), channel_id=1, source_target_pairs={{0,2},{2,0},{4,6},{6,4},{8,10},{10,8},{12,14},{14,12},{16,18},{18,... | collective-permute-start | bytes 3932168 | tf_op jit(solution)/shard_map/ppermute | solution.py:307
  288.0 60.8 %collective-permute-start.37 = (bf16[512,1280]{1,0:T(8,128)(2,1)}, bf16[512,1280]{1,0:T(8,128)(2,1)}, u32[]{:S(2)}, u32[]{:S(2)}) collective-permute-start(bf16[512,1280]{1,0:T(8,128)(2,1)} %slice.317), channel_id=1, source_target_pairs={{0,2},{2,0},{4,6},{6,4},{8,10},{10,8},{12,14},{14,12},{16,18},{18,... | collective-permute-start | bytes 3932168 | tf_op jit(solution)/shard_map/ppermute | solution.py:307
  310.4 52.6 %collective-permute-start.36 = (bf16[512,1280]{1,0:T(8,128)(2,1)}, bf16[512,1280]{1,0:T(8,128)(2,1)S(1)}, u32[]{:S(2)}, u32[]{:S(2)}) collective-permute-start(bf16[512,1280]{1,0:T(8,128)(2,1)} %slice.318), channel_id=1, source_target_pairs={{0,2},{2,0},{4,6},{6,4},{8,10},{10,8},{12,14},{14,12},{16,18},{18,... | collective-permute-start | bytes 3932168 | tf_op jit(solution)/shard_map/ppermute | solution.py:307
  315.1 36.7 %collective-permute-start.34 = (bf16[512,1280]{1,0:T(8,128)(2,1)S(1)}, bf16[512,1280]{1,0:T(8,128)(2,1)S(1)}, u32[]{:S(2)}, u32[]{:S(2)}) collective-permute-start(bf16[512,1280]{1,0:T(8,128)(2,1)S(1)} %slice.319), channel_id=1, source_target_pairs={{0,2},{2,0},{4,6},{6,4},{8,10},{10,8},{12,14},{14,12},{16,18},{18,... | collective-permute-start | bytes 3932168 | tf_op jit(solution)/shard_map/ppermute | solution.py:307
  323.0 63.5 %collective-permute-start.29 = (bf16[512,1280]{1,0:T(8,128)(2,1)}, bf16[512,1280]{1,0:T(8,128)(2,1)}, u32[]{:S(2)}, u32[]{:S(2)}) collective-permute-start(bf16[512,1280]{1,0:T(8,128)(2,1)} %slice.320), channel_id=1, source_target_pairs={{0,2},{2,0},{4,6},{6,4},{8,10},{10,8},{12,14},{14,12},{16,18},{18,... | collective-permute-start | bytes 3932168 | tf_op jit(solution)/shard_map/ppermute | solution.py:307
  351.6 31.9 %collective-permute-start.38 = (bf16[512,1280]{1,0:T(8,128)(2,1)}, bf16[512,1280]{1,0:T(8,128)(2,1)}, u32[]{:S(2)}, u32[]{:S(2)}) collective-permute-start(bf16[512,1280]{1,0:T(8,128)(2,1)} %fusion.25), channel_id=1, source_target_pairs={{0,1},{1,0},{2,3},{3,2},{4,5},{5,4},{6,7},{7,6},{8,9},{9,8},{10,11... | collective-permute-start | bytes 3932168 | tf_op jit(solution)/shard_map/ppermute | solution.py:316
  353.2 57.8 %collective-permute-start.35 = (bf16[512,1280]{1,0:T(8,128)(2,1)}, bf16[512,1280]{1,0:T(8,128)(2,1)S(1)}, u32[]{:S(2)}, u32[]{:S(2)}) collective-permute-start(bf16[512,1280]{1,0:T(8,128)(2,1)} %fusion.27), channel_id=1, source_target_pairs={{0,1},{1,0},{2,3},{3,2},{4,5},{5,4},{6,7},{7,6},{8,9},{9,8},{10,11... | collective-permute-start | bytes 3932168 | tf_op jit(solution)/shard_map/ppermute | solution.py:316
  421.0 15.3 %collective-permute-start.41 = (bf16[320,512]{1,0:T(8,128)(2,1)S(1)}, bf16[320,512]{1,0:T(8,128)(2,1)}, u32[]{:S(2)}, u32[]{:S(2)}) collective-permute-start(bf16[320,512]{1,0:T(8,128)(2,1)S(1)} %get-tuple-element.79), channel_id=1, source_target_pairs={{0,1},{1,0},{2,3},{3,2},{4,5},{5,4},{6,7},{7,6},{8,9},{9,8},{10,11... | collective-permute-start | bytes 983048 | tf_op jit(solution)/shard_map/ppermute | solution.py:316
  434.3 11.1 %collective-permute-start.40 = (bf16[320,512]{1,0:T(8,128)(2,1)}, bf16[320,512]{1,0:T(8,128)(2,1)S(1)}, u32[]{:S(2)}, u32[]{:S(2)}) collective-permute-start(bf16[320,512]{1,0:T(8,128)(2,1)} %get-tuple-element.80), channel_id=1, source_target_pairs={{0,2},{2,0},{4,6},{6,4},{8,10},{10,8},{12,14},{14,12},{16,18},{18,... | collective-permute-start | bytes 983048 | tf_op jit(solution)/shard_map/ppermute | solution.py:307
  498.0 35.3 %collective-permute-start.57 = (bf16[8,80,1280]{2,1,0:T(8,128)(2,1)}, bf16[8,80,1280]{2,1,0:T(8,128)(2,1)}, u32[]{:S(2)}, u32[]{:S(2)}) collective-permute-start(bf16[8,80,1280]{2,1,0:T(8,128)(2,1)} %fusion.32), channel_id=1, source_target_pairs={{0,2},{2,0},{4,6},{6,4},{8,10},{10,8},{12,14},{14,12},{16,18},{18,... | collective-permute-start | bytes 4915208 | tf_op jit(solution)/shard_map/ppermute | solution.py:307
  525.5 39.0 %collective-permute-start.51 = (bf16[4,160,960]{2,1,0:T(8,128)(2,1)}, bf16[4,160,960]{2,1,0:T(8,128)(2,1)}, u32[]{:S(2)}, u32[]{:S(2)}) collective-permute-start(bf16[4,160,960]{2,1,0:T(8,128)(2,1)} %dynamic-slice_bitcast_fusion), channel_id=1, source_target_pairs={{0,4},{2,6},{4,0},{6,2},{8,12},{10,14},{12,8},{14,10},{16,20},{18,... | collective-permute-start | bytes 3686408 | tf_op jit(solution)/shard_map/ppermute | solution.py:310
  533.2 73.8 %collective-permute-start.44 = (bf16[512,1280]{1,0:T(8,128)(2,1)}, bf16[512,1280]{1,0:T(8,128)(2,1)}, u32[]{:S(2)}, u32[]{:S(2)}) collective-permute-start(bf16[512,1280]{1,0:T(8,128)(2,1)} %get-tuple-element.70), channel_id=1, source_target_pairs={{0,2},{2,0},{4,6},{6,4},{8,10},{10,8},{12,14},{14,12},{16,18},{18,... | collective-permute-start | bytes 3932168 | tf_op jit(solution)/shard_map/ppermute | solution.py:307
  569.1 29.1 %collective-permute-start.53 = (bf16[160,960]{1,0:T(8,128)(2,1)S(1)}, bf16[160,960]{1,0:T(8,128)(2,1)S(1)}, u32[]{:S(2)}, u32[]{:S(2)}) collective-permute-start(bf16[160,960]{1,0:T(8,128)(2,1)S(1)} %get-tuple-element.77), channel_id=1, source_target_pairs={{0,16},{2,18},{4,20},{6,22},{8,24},{10,26},{12,28},{14,30},{16,0},... | collective-permute-start | bytes 921608 | tf_op jit(solution)/shard_map/ppermute | solution.py:313
  570.8 27.5 %collective-permute-start.52 = (bf16[160,960]{1,0:T(8,128)(2,1)S(1)}, bf16[160,960]{1,0:T(8,128)(2,1)S(1)}, u32[]{:S(2)}, u32[]{:S(2)}) collective-permute-start(bf16[160,960]{1,0:T(8,128)(2,1)S(1)} %get-tuple-element.75), channel_id=1, source_target_pairs={{0,8},{2,10},{4,12},{6,14},{8,16},{10,18},{12,20},{14,22},{16,24},... | collective-permute-start | bytes 921608 | tf_op jit(solution)/shard_map/ppermute | solution.py:313
  573.0 32.2 %collective-permute-start.58 = (bf16[640,640]{1,0:T(8,128)(2,1)S(1)}, bf16[640,640]{1,0:T(8,128)(2,1)S(1)}, u32[]{:S(2)}, u32[]{:S(2)}) collective-permute-start(bf16[640,640]{1,0:T(8,128)(2,1)S(1)} %bitcast.275), channel_id=1, source_target_pairs={{0,1},{1,0},{2,3},{3,2},{4,5},{5,4},{6,7},{7,6},{8,9},{9,8},{10,11... | collective-permute-start | bytes 2457608 | tf_op jit(solution)/shard_map/ppermute | solution.py:316
  577.9 69.2 %collective-permute-start.43 = (bf16[512,1280]{1,0:T(8,128)(2,1)}, bf16[512,1280]{1,0:T(8,128)(2,1)}, u32[]{:S(2)}, u32[]{:S(2)}) collective-permute-start(bf16[512,1280]{1,0:T(8,128)(2,1)} %get-tuple-element.69), channel_id=1, source_target_pairs={{0,2},{2,0},{4,6},{6,4},{8,10},{10,8},{12,14},{14,12},{16,18},{18,... | collective-permute-start | bytes 3932168 | tf_op jit(solution)/shard_map/ppermute | solution.py:307
  605.4 11.6 %collective-permute-start.59 = (bf16[4,80,640]{2,1,0:T(8,128)(2,1)S(1)}, bf16[4,80,640]{2,1,0:T(8,128)(2,1)S(1)}, u32[]{:S(2)}, u32[]{:S(2)}) collective-permute-start(bf16[4,80,640]{2,1,0:T(8,128)(2,1)S(1)} %dynamic-slice_bitcast_fusion.1), channel_id=1, source_target_pairs={{0,4},{2,6},{4,0},{6,2},{8,12},{10,14},{12,8},{14,10},{16,20},{18,... | collective-permute-start | bytes 1228808 | tf_op jit(solution)/shard_map/ppermute | solution.py:310
  610.4 36.8 %collective-permute-start.45 = (bf16[512,1280]{1,0:T(8,128)(2,1)}, bf16[512,1280]{1,0:T(8,128)(2,1)}, u32[]{:S(2)}, u32[]{:S(2)}) collective-permute-start(bf16[512,1280]{1,0:T(8,128)(2,1)} %fusion.21), channel_id=1, source_target_pairs={{0,1},{1,0},{2,3},{3,2},{4,5},{5,4},{6,7},{7,6},{8,9},{9,8},{10,11... | collective-permute-start | bytes 3932168 | tf_op jit(solution)/shard_map/ppermute | solution.py:316
  629.9 13.9 %collective-permute-start.63 = (bf16[80,640]{1,0:T(8,128)(2,1)S(1)}, bf16[80,640]{1,0:T(8,128)(2,1)S(1)}, u32[]{:S(2)}, u32[]{:S(2)}) collective-permute-start(bf16[80,640]{1,0:T(8,128)(2,1)S(1)} %get-tuple-element.56), channel_id=1, source_target_pairs={{0,1},{1,0},{2,3},{3,2},{4,5},{5,4},{6,7},{7,6},{8,9},{9,8},{10,11... | collective-permute-start | bytes 307208 | tf_op jit(solution)/shard_map/ppermute | solution.py:316
  654.3 12.4 %collective-permute-start.66 = (bf16[160,1280]{1,0:T(8,128)(2,1)S(1)}, bf16[160,1280]{1,0:T(8,128)(2,1)S(1)}, u32[]{:S(2)}, u32[]{:S(2)}) collective-permute-start(bf16[160,1280]{1,0:T(8,128)(2,1)S(1)} %get-tuple-element.84), channel_id=1, source_target_pairs={{0,1},{1,0},{2,3},{3,2},{4,5},{5,4},{6,7},{7,6},{8,9},{9,8},{10,11... | collective-permute-start | bytes 1228808 | tf_op jit(solution)/shard_map/ppermute | solution.py:316
  657.7 16.5 %collective-permute-start.65 = (bf16[2,80,1280]{2,1,0:T(8,128)(2,1)S(1)}, bf16[2,80,1280]{2,1,0:T(8,128)(2,1)S(1)}, u32[]{:S(2)}, u32[]{:S(2)}) collective-permute-start(bf16[2,80,1280]{2,1,0:T(8,128)(2,1)S(1)} %maximum_select_fusion.5), channel_id=1, source_target_pairs={{0,1},{1,0},{2,3},{3,2},{4,5},{5,4},{6,7},{7,6},{8,9},{9,8},{10,11... | collective-permute-start | bytes 1228808 | tf_op jit(solution)/shard_map/ppermute | solution.py:316
  (97 other events, 1469.7 us)
Sparse Core Ops, SparseCore 0:
  106.1 107.2 all-gather.2
  434.4 130.7 reduce-scatter.3

commit v2 on v1

v2 whole, which is shorter than its diff:
```python
import math

import jax
import jax.numpy as jnp
from jax import lax
from jax.experimental import pallas as pl
from jax.experimental.pallas import tpu as pltpu
from jax.sharding import PartitionSpec as P

HEAD_DIM = 80
NEGATIVE = -1000000000.0
EPSILON = 1e-05
LOGIT_CAP = 10.0
LOG2E = 1.4426950408889634
VMEM_LIMIT = 56 * 1024 * 1024
f32 = jnp.float32
bf16 = jnp.bfloat16


def dot(left, right, left_dim, right_dim):
    return lax.dot_general(
        left, right, (((left_dim,), (right_dim,)), ((), ())), preferred_element_type=f32
    )


def nt(a, b):
    return dot(a, b, 1, 1)


def nn(a, b):
    return dot(a, b, 1, 0)


def tn(a, b):
    return dot(a, b, 0, 0)


def normalized(rows):
    centred = rows - jnp.mean(rows, axis=-1, keepdims=True)
    spread = jnp.mean(centred * centred, axis=-1, keepdims=True)
    scale = lax.rsqrt(spread + EPSILON)
    return centred * scale, scale


def norm_back(plain, scale, grad):
    first = jnp.mean(grad, axis=-1, keepdims=True)
    second = jnp.mean(grad * plain, axis=-1, keepdims=True)
    return scale * (grad - first - plain * second)


def tie(value, *after):
    return lax.optimization_barrier((value,) + after)[0]


def params(**more):
    return pltpu.CompilerParams(vmem_limit_bytes=VMEM_LIMIT, **more)


def vmem(count):
    return [pl.BlockSpec(memory_space=pltpu.VMEM)] * count


def smem():
    return pl.BlockSpec(memory_space=pltpu.SMEM)


def sds(shape, dtype):
    return jax.ShapeDtypeStruct(shape, dtype)


def one_row(width):
    return jnp.where(lax.broadcasted_iota(jnp.int32, (16, width), 0) == 0, 1.0, 0.0).astype(bf16)


def attend_kernel(scale2, span, q_ref, k_ref, v_ref, mask_ref, near_ref, far_ref, lse_ref, peak_ref):
    frames = q_ref.shape[1]
    mask_rows = mask_ref[...]
    keys = jnp.concatenate([k_ref[...], mask_rows], axis=0).T
    values = jnp.concatenate([v_ref[...], one_row(frames)], axis=0)
    s = nn(keys, jnp.concatenate([q_ref[...], one_row(frames)], axis=0))
    top = jnp.max(s, axis=0, keepdims=True)
    p = jnp.exp2(s * scale2 - top * scale2).astype(bf16)
    mixed = nn(values, p)
    total = mixed[HEAD_DIM : HEAD_DIM + 1, :]
    mixed = (mixed[:HEAD_DIM, :] * (1.0 / total)).astype(bf16)
    near_ref[0] = mixed[:, :span]
    for step in range(1, frames // span):
        far_ref[step - 1, 0] = mixed[:, step * span : (step + 1) * span]
    lse_ref[0] = top * scale2 + jnp.log2(total)
    peak_ref[0] = jnp.where(mask_rows[0:1, :].astype(f32) == 0.0, top, NEGATIVE)


def head_rows(frames, heads, half):
    return [
        pl.BlockSpec((HEAD_DIM, frames), lambda b, h, i=i: ((3 * half + i) * heads + h, b))
        for i in range(3)
    ]


def attend(qkv, mask, clips, heads, half, halves, groups):
    frames = qkv.shape[1] // clips
    span = frames // groups
    vec = pl.BlockSpec((1, 1, frames), lambda b, h: (b * heads + h, 0, 0))
    return pl.pallas_call(
        lambda *refs: attend_kernel(LOG2E / math.sqrt(HEAD_DIM), span, *refs),
        grid=(clips, heads),
        in_specs=head_rows(frames, heads, half) + [pl.BlockSpec((16, frames), lambda b, h: (b, 0))],
        out_specs=[
            pl.BlockSpec((1, HEAD_DIM, span), lambda b, h: (b, h, 0)),
            pl.BlockSpec((groups - 1, 1, HEAD_DIM, span), lambda b, h: (0, b, h, 0)),
            vec,
            vec,
        ],
        out_shape=[
            sds((clips, heads * HEAD_DIM, span), bf16),
            sds((groups - 1, clips, heads * HEAD_DIM, span), bf16),
            sds((clips * heads, 1, frames), f32),
            sds((clips * heads, 1, frames), f32),
        ],
        compiler_params=params(),
        cost_estimate=pl.CostEstimate(
            flops=clips * heads * frames * frames * 2000,
            bytes_accessed=qkv.size * 3 // halves,
            transcendentals=clips * heads * frames * frames,
        ),
        name="attend",
    )(qkv, qkv, qkv, mask)


def attend_back_kernel(span, scale, *refs):
    q_ref, k_ref, v_ref, mask_ref, lse_ref = refs[:5]
    groups = q_ref.shape[1] // span
    grads = refs[5 : 5 + 2 * groups]
    out_ref, gk, gv, gs = refs[5 + 2 * groups :]
    scale2 = LOG2E * scale
    key_rows = k_ref[...]
    keys = jnp.concatenate([key_rows, mask_ref[...]], axis=0).T
    values = v_ref[...].T
    ones = one_row(span)
    for flip in range(2):

        @pl.when(pl.program_id(0) == flip)
        def _(flip=flip):
            for at in range(groups):
                gs[:, at * span : (at + 1) * span] = grads[flip * groups + at][...].reshape(HEAD_DIM, span)

    for at in range(groups):
        cols = pl.ds(at * span, span)
        q = q_ref[:, cols]
        g = gs[:, cols]
        s = nn(keys, jnp.concatenate([q, ones], axis=0))
        p = jnp.exp2(s * scale2 - lse_ref[0, :, cols])
        t = p * nn(values, g)
        inner = jnp.sum(t, axis=0, keepdims=True)
        ds = (t - p * inner).astype(bf16)
        out_ref[0, :, cols] = (nn(key_rows, ds) * scale).astype(bf16)
        dk = nt(q, ds)
        dv = nt(g, p.astype(bf16))
        if at == 0:
            gk[...] = dk
            gv[...] = dv
        else:
            gk[...] += dk
            gv[...] += dv
    out_ref[1] = (gk[...] * scale).astype(bf16)
    out_ref[2] = gv[...].astype(bf16)


def attend_back(qkv, mask, grads, lse, clips, heads, half, halves, groups):
    frames = qkv.shape[1] // clips
    span = frames // groups
    vec = pl.BlockSpec((1, 1, frames), lambda b, h: (b * heads + h, 0, 0))

    def block(v, place):
        if v.ndim == 3:
            return pl.BlockSpec((1, HEAD_DIM, span), lambda b, h: (place, h, 0))
        return pl.BlockSpec((HEAD_DIM, span), lambda b, h: (place + h, 0))

    grads = grads[0] + grads[1]
    return pl.pallas_call(
        lambda *refs: attend_back_kernel(span, 1.0 / math.sqrt(HEAD_DIM), *refs),
        grid=(clips, heads),
        in_specs=head_rows(frames, heads, half)
        + [pl.BlockSpec((16, frames), lambda b, h: (b, 0)), vec]
        + [block(*g) for g in grads],
        out_specs=pl.BlockSpec((3, HEAD_DIM, frames), lambda b, h: (0, h, b)),
        out_shape=sds((3, heads * HEAD_DIM, clips * frames), bf16),
        scratch_shapes=[
            pltpu.VMEM((HEAD_DIM, frames), f32),
            pltpu.VMEM((HEAD_DIM, frames), f32),
            pltpu.VMEM((HEAD_DIM, frames), bf16),
        ],
        compiler_params=params(),
        cost_estimate=pl.CostEstimate(
            flops=clips * heads * frames * frames * 4000,
            bytes_accessed=qkv.size * 6 // halves,
            transcendentals=clips * heads * frames * frames,
        ),
        name="attend_back",
    )(qkv, qkv, qkv, mask, lse, *[v for v, _ in grads])


def gelu_parts(v):
    bell = jnp.exp2(v * v * (-0.5 * LOG2E))
    t = 1.0 / (1.0 + (0.3275911 / math.sqrt(2.0)) * jnp.abs(v))
    poly = t * (
        0.5 * 0.254829592
        + t * (0.5 * -0.284496736 + t * (0.5 * 1.421413741 + t * (0.5 * -1.453152027 + t * (0.5 * 1.061405429))))
    )
    tail = poly * bell
    return jnp.where(v < 0.0, tail, 1.0 - tail), bell * (1.0 / math.sqrt(2.0 * math.pi))


def feed_kernel(count, own, tile, refs):
    ns, gs = refs[:count], refs[count : 2 * count]
    up_ref, down_ref, bias_ref = refs[2 * count : 2 * count + 3]
    act_ref, back_ref, grad_own, grad_other, out_own, out_other, sum_ref, n_now, g_now = refs[2 * count + 3 :]
    width = n_now.shape[1]
    hidden = act_ref.shape[1]
    rows = ns[0].shape[0]
    for j in range(count):
        n_now[j * rows : (j + 1) * rows, :] = ns[j][...]
        g_now[j * rows : (j + 1) * rows, :] = gs[j][...]
    up = up_ref[...].reshape(width, hidden)
    down = down_ref[...].reshape(hidden, width)
    for low in range(0, hidden, tile):
        cols = slice(low, low + tile)
        before = nn(n_now[...], up[:, cols]) + bias_ref[:, cols]
        grad_act = nt(g_now[...], down[cols, :])
        cumulative, density = gelu_parts(before)
        act_ref[:, cols] = (before * cumulative).astype(bf16)
        grad = ((cumulative + before * density) * grad_act).astype(bf16)
        back_ref[:, cols] = grad
        sum_ref[:, cols] = jnp.sum(grad.astype(f32), axis=0, keepdims=True)
    mine = own * rows
    grad_own[...] = nt(back_ref[:mine, :], up)
    grad_other[...] = nt(back_ref[mine:, :], up).astype(bf16)
    out_own[...] = nn(act_ref[:mine, :], down)
    out_other[...] = nn(act_ref[mine:, :], down).astype(bf16)


def feed(normed, grad, own, rows, weights, bias):
    count = len(normed)
    width = normed[0][0].shape[1]
    hidden = bias.shape[1]
    tile = 256 if hidden % 256 == 0 else hidden

    def whole(shape):
        return pl.BlockSpec(shape, lambda i: (0,) * len(shape))

    if len(weights) == 1:
        pairs = weights[0].shape[0]
        weights = weights * 2
        weight_specs = [pl.BlockSpec((pairs, hidden // pairs, width), lambda i, j=j: (0, j, 0)) for j in range(2)]
    else:
        weight_specs = [whole(w.shape) for w in weights]
    shapes = [
        sds((count * rows, hidden), bf16),
        sds((count * rows, hidden), bf16),
        sds((own * rows, width), f32),
        sds(((count - own) * rows, width), bf16),
        sds((own * rows, width), f32),
        sds(((count - own) * rows, width), bf16),
        sds((1, hidden), f32),
    ]
    return pl.pallas_call(
        lambda *refs: feed_kernel(count, own, tile, refs),
        grid=(1,),
        in_specs=[pl.BlockSpec((rows, width), lambda i, at=at: (at, 0)) for _, at in normed + grad]
        + weight_specs
        + [whole((1, hidden))],
        out_specs=[whole(v.shape) for v in shapes],
        out_shape=shapes,
        scratch_shapes=[pltpu.VMEM((count * rows, width), bf16)] * 2,
        compiler_params=params(),
        cost_estimate=pl.CostEstimate(
            flops=8 * count * rows * width * hidden,
            bytes_accessed=4 * width * hidden + 16 * count * rows * width,
            transcendentals=count * rows * hidden,
        ),
        name="feed",
    )(*[v for v, _ in normed + grad], *weights, bias)


def project(rank, blocks, small, weight, halves):
    count = len(blocks)
    rows, width = blocks[0].shape
    shards, lines_count, features = small.shape
    own_rows = width // shards
    slab = features // 3
    cut = slab // halves
    sub = math.gcd(rows, 256)

    def kernel(rank_ref, small_ref, w_ref, *refs):
        xs = refs[:count]
        normed_ref, qkv_ref, lines_ref, turned, bias, now = refs[count:]
        at = pl.program_id(0)

        @pl.when(at == 0)
        def _():
            lines_ref[...] = jnp.concatenate(
                [small_ref[f, :, :own_rows].astype(f32) for f in range(shards)], axis=1
            )
            turned[...] = w_ref[...].T
            for r in range(count):

                @pl.when(rank_ref[0] == r)
                def _(r=r):
                    parts = []
                    for h in range(halves):
                        cols = slice(r * slab + h * cut, r * slab + (h + 1) * cut)
                        parts += [lines_ref[2:3, cols], jnp.zeros((1, cut), f32), lines_ref[3:4, cols]]
                    row = jnp.concatenate(parts, axis=1)
                    bias[...] = jnp.broadcast_to(row, (8, features)).T

        for j in range(count):

            @pl.when(at == j)
            def _(j=j):
                now[...] = xs[j][...]

        for t in range(0, rows, sub):
            plain, _ = normalized(now[t : t + sub, :].astype(f32))
            normed = (plain * lines_ref[0:1, :] + lines_ref[1:2, :]).astype(bf16)
            normed_ref[t : t + sub, :] = normed
            qkv_ref[:, t : t + sub] = (nt(turned[...], normed) + bias[:, 0:1]).astype(bf16)

    return pl.pallas_call(
        kernel,
        grid=(count,),
        in_specs=[
            smem(),
            pl.BlockSpec(small.shape, lambda i: (0, 0, 0)),
            pl.BlockSpec(weight.shape, lambda i: (0, 0)),
        ]
        + [pl.BlockSpec((rows, width), lambda i: (0, 0))] * count,
        out_specs=[
            pl.BlockSpec((rows, width), lambda i: (i, 0)),
            pl.BlockSpec((features, rows), lambda i: (0, i)),
            pl.BlockSpec((lines_count, width), lambda i: (0, 0)),
        ],
        out_shape=[
            sds((count * rows, width), bf16),
            sds((features, count * rows), bf16),
            sds((lines_count, width), f32),
        ],
        scratch_shapes=[
            pltpu.VMEM((features, width), bf16),
            pltpu.VMEM((features, 8), f32),
            pltpu.VMEM((rows, width), bf16),
        ],
        compiler_params=params(),
        cost_estimate=pl.CostEstimate(
            flops=2 * count * rows * width * features,
            bytes_accessed=2 * width * features + 6 * count * rows * width,
            transcendentals=count * rows,
        ),
        name="project",
    )(rank, small, weight, *blocks)


def project_back(grads, weight, blocks, places, groups):
    count, halves = len(blocks), len(grads)
    rows, width = blocks[0].shape
    features = weight.shape[1]
    own = count // 2
    sub = math.gcd(rows, 256)

    def kernel(w_ref, *refs):
        g_refs, xs = refs[:halves], refs[halves : halves + count]
        own_ref, other_ref, sums_ref, bias_ref, now = refs[halves + count :]
        at = pl.program_id(0)
        for j in range(count):

            @pl.when(at == j)
            def _(j=j):
                now[...] = xs[j][...]

        @pl.when(at == 0)
        def _():
            sums_ref[...] = jnp.zeros(sums_ref.shape, f32)
            bias_ref[...] = jnp.zeros(bias_ref.shape, f32)

        for t in range(0, rows, sub):
            cut = slice(t, t + sub)
            turned = jnp.concatenate([g[:, cut] for g in g_refs], axis=0).T
            grad = nt(turned, w_ref[...])
            plain, _ = normalized(now[cut, :].astype(f32))
            sums_ref[0:1, :] += jnp.sum(grad * plain, axis=0, keepdims=True)
            sums_ref[1:2, :] += jnp.sum(grad, axis=0, keepdims=True)
            bias_ref[...] += nn(jnp.ones((8, sub), bf16), turned)

            @pl.when(at < own)
            def _(cut=cut, grad=grad):
                own_ref[cut, :] = grad

            @pl.when(at >= own)
            def _(cut=cut, grad=grad):
                other_ref[cut, :] = grad.astype(bf16)

    return pl.pallas_call(
        kernel,
        grid=(count,),
        in_specs=[pl.BlockSpec(weight.shape, lambda i: (0, 0))]
        + [
            pl.BlockSpec((g.shape[0], rows), lambda i: (0, i // own * groups + i % own + places[0])) for g in grads
        ]
        + [pl.BlockSpec((rows, width), lambda i: (0, 0))] * count,
        out_specs=[
            pl.BlockSpec((rows, width), lambda i: (jnp.minimum(i, own - 1), 0)),
            pl.BlockSpec((rows, width), lambda i: (jnp.maximum(i - own, 0), 0)),
            pl.BlockSpec((8, width), lambda i: (0, 0)),
            pl.BlockSpec((8, features), lambda i: (0, 0)),
        ],
        out_shape=[
            sds((own * rows, width), f32),
            sds((own * rows, width), bf16),
            sds((8, width), f32),
            sds((8, features), f32),
        ],
        scratch_shapes=[pltpu.VMEM((rows, width), bf16)],
        compiler_params=params(),
        cost_estimate=pl.CostEstimate(
            flops=2 * count * rows * width * features,
            bytes_accessed=2 * width * features + 8 * count * rows * width,
            transcendentals=count * rows,
        ),
        name="project_back",
    )(weight, *grads, *blocks)


def by_source(r, groups):
    return [((src % groups - r % groups) % groups, (src // groups) ^ (r // groups)) for src in range(2 * groups)]


def finish_heads(rank, blocks, halves, groups):
    _, rows, features = blocks[0].shape
    ranks = 2 * groups
    slab = features // 4
    cut = slab // halves
    width = slab * ranks
    starts = [0] + [slab + 3 * cut * h for h in range(1, halves)]

    def kernel(rank_ref, *refs):
        ins, outs = refs[:-4], refs[-4:]
        for r in range(ranks):

            @pl.when(rank_ref[0] == r)
            def _(r=r):
                order = by_source(r, groups)
                for i in range(3):
                    outs[i][...] = jnp.concatenate(
                        [
                            ins[step][flip, :, low + i * cut : low + (i + 1) * cut]
                            for step, flip in order
                            for low in starts
                        ],
                        axis=1,
                    ).astype(f32)
                outs[3][...] = jnp.concatenate(
                    [ins[step][flip, :, 3 * cut : 3 * cut + slab] for step, flip in order], axis=1
                ).astype(f32)

    return pl.pallas_call(
        kernel,
        in_specs=[smem()] + vmem(groups),
        out_specs=vmem(4),
        out_shape=[sds((rows, width), f32)] * 4,
        compiler_params=params(),
        cost_estimate=pl.CostEstimate(flops=0, bytes_accessed=24 * rows * width, transcendentals=0),
        name="finish_heads",
    )(rank, *blocks)


def finish_feed(rank, ups, downs, pairs, groups):
    _, rows, rank_hidden = ups[0].shape
    piece, width = downs[0].shape
    ranks = 2 * groups

    def kernel(rank_ref, *refs):
        up_refs, down_refs, up_out, down_out = refs[:groups], refs[groups : 2 * groups], refs[-2], refs[-1]
        for r in range(ranks):

            @pl.when(rank_ref[0] == r)
            def _(r=r):
                for zx in range(pairs):
                    up_out[:, zx * ranks * piece : (zx + 1) * ranks * piece] = jnp.concatenate(
                        [
                            up_refs[step][flip, :, zx * piece : (zx + 1) * piece]
                            for step, flip in by_source(r, groups)
                        ],
                        axis=1,
                    ).astype(f32)
                for step in range(groups):
                    at = (r + step) % groups * piece
                    down_out[at : at + piece, :] = down_refs[step][...].astype(f32)

    return pl.pallas_call(
        kernel,
        in_specs=[smem()] + vmem(2 * groups),
        out_specs=vmem(2),
        out_shape=[sds((rows, rank_hidden * ranks), f32), sds((groups * piece, width), f32)],
        compiler_params=params(),
        cost_estimate=pl.CostEstimate(flops=0, bytes_accessed=12 * rows * rank_hidden * ranks, transcendentals=0),
        name="finish_feed",
    )(rank, *ups, *downs)


def pick(where, q, k, v, up, o, small, ranks, halves, pairs):
    own_rows, width = q.shape
    slab = width // ranks
    cut = slab // halves
    piece = up.shape[1] // (ranks * pairs)
    base = -(-own_rows // 16) * 16
    extra = small.shape[0]

    def kernel(where_ref, q_ref, k_ref, v_ref, up_ref, o_ref, small_ref, *outs):
        for side in range(2):
            pay, ups, half = outs[3 * side : 3 * side + 3]
            pay[base:, :] = jnp.zeros((extra, 3 * slab), bf16)
            pay[base:, : small.shape[1]] = small_ref[...]
            for r in range(ranks):

                @pl.when(where_ref[side] == r)
                def _(pay=pay, ups=ups, r=r):
                    parts = [
                        w[:, r * slab + h * cut : r * slab + (h + 1) * cut]
                        for h in range(halves)
                        for w in (q_ref, k_ref, v_ref)
                    ]
                    pay[:own_rows, :] = jnp.concatenate(parts, axis=1)
                    ups[...] = jnp.concatenate(
                        [up_ref[:, (c * ranks + r) * piece : (c * ranks + r + 1) * piece] for c in range(pairs)],
                        axis=1,
                    )

            for c in range(2):

                @pl.when(where_ref[2] == (c ^ side))
                def _(half=half, c=c):
                    half[...] = o_ref[:, c * width // 2 : (c + 1) * width // 2]

    shapes = [
        sds((base + extra, 3 * slab), bf16),
        sds((own_rows, piece * pairs), bf16),
        sds((own_rows, width // 2), bf16),
    ]
    return pl.pallas_call(
        kernel,
        in_specs=[smem()] + vmem(6),
        out_specs=vmem(6),
        out_shape=shapes * 2,
        compiler_params=params(),
        cost_estimate=pl.CostEstimate(flops=0, bytes_accessed=10 * up.size, transcendentals=0),
        name="pick",
    )(where, q, k, v, up, o, small)


def place(blocks, slots, pieces):
    count, (_, width) = len(blocks), blocks[0].shape

    def kernel(slots_ref, *refs):
        for i in range(count):
            for target, spans in zip(refs[count:], pieces, strict=True):
                for j, (low, high) in enumerate(spans):
                    target[slots_ref[i] * len(spans) + j] = refs[i][low:high, :]

    return pl.pallas_call(
        kernel,
        in_specs=[smem()] + vmem(count),
        out_specs=vmem(len(pieces)),
        out_shape=[
            sds((count * len(spans), spans[0][1] - spans[0][0], width), blocks[0].dtype) for spans in pieces
        ],
        compiler_params=params(),
        cost_estimate=pl.CostEstimate(
            flops=0, bytes_accessed=4 * count * blocks[0].size, transcendentals=0
        ),
        name="place",
    )(slots, *blocks)


def merge(slots, x, out_full, lines, blocks, halves, token_parts):
    tokens, width = x.shape
    count = len(blocks)
    hs = blocks[0][0].shape[0]
    slab = hs * halves
    rows = tokens // token_parts

    def kernel(slots_ref, x_ref, w_ref, lines_ref, *refs):
        ins, mixed, after = refs[: count * halves], refs[count * halves], refs[count * halves + 1]
        outs = refs[count * halves + 2 :]
        for i in range(count):
            for h in range(halves):
                at = pl.multiple_of(slots_ref[i] * slab + h * hs, 16)
                mixed[pl.ds(at, hs), :] = ins[i * halves + h][...]
        for t in range(token_parts):
            cols = slice(t * rows, (t + 1) * rows)
            total = nn(mixed[:, cols].T, w_ref[...]) + lines_ref[4:5, :] + x_ref[cols, :].astype(f32)
            after[cols, :] = total
            plain, _ = normalized(total)
            outs[t][...] = (plain * lines_ref[5:6, :] + lines_ref[6:7, :]).astype(bf16)

    made = pl.pallas_call(
        kernel,
        in_specs=[smem()] + vmem(3 + count * halves),
        out_specs=vmem(2 + token_parts),
        out_shape=[sds((width, tokens), bf16), sds((tokens, width), f32)]
        + [sds((rows, width), bf16)] * token_parts,
        compiler_params=params(),
        cost_estimate=pl.CostEstimate(
            flops=2 * tokens * width * width, bytes_accessed=2 * width * width + 12 * tokens * width, transcendentals=tokens
        ),
        name="merge",
    )(slots, x, out_full, lines, *[b for source in blocks for b in source])
    return made[0], made[1], list(made[2:])


def turn(slots, after1, near, fars, live_grad, lines, out_full, halves, groups):
    tokens, width = after1.shape
    ranks = 2 * groups
    slab = width // ranks
    hs = slab // halves
    parts = len(fars)
    rows = tokens // parts
    per = len(fars[0])

    def kernel(slots_ref, after_ref, near_ref, live_ref, g_ref, w_ref, *refs):
        far_refs = refs[: parts * per]
        grad_ref, low_ref, sums_ref = refs[parts * per : parts * per + 3]
        outs = refs[parts * per + 3 :]
        sums = [jnp.zeros((1, width), f32) for _ in range(4)]
        for t in range(parts):
            cut = slice(t * rows, (t + 1) * rows)
            grad = near_ref[cut, :]
            for j in range(per):
                grad = grad + far_refs[t * per + j][...].astype(f32)
            plain, scale = normalized(after_ref[cut, :])
            live = live_ref[cut, :].astype(f32)
            total = live + norm_back(plain, scale, grad * g_ref[5:6, :])
            grad_ref[cut, :] = total
            low = total.astype(bf16)
            low_ref[cut, :] = low
            for i, term in enumerate((grad * plain, grad, low.astype(f32), live)):
                sums[i] = sums[i] + jnp.sum(term, axis=0, keepdims=True)
        for i in range(4):
            sums_ref[i : i + 1, :] = sums[i]
        low = low_ref[...]

        def of_rank(flip, step, h):
            at = pl.multiple_of(slots_ref[flip * groups + step] * slab + h * hs, 16)
            return nt(w_ref[pl.ds(at, hs), :], low).astype(bf16)

        for h in range(halves):
            for step in range(1, groups):
                for flip in range(2):
                    outs[h * (groups - 1) + step - 1][flip] = of_rank(flip, step, h)
        near_outs = outs[halves * (groups - 1) :]
        for h in range(halves):
            near_outs[0][h * hs : (h + 1) * hs, :] = of_rank(0, 0, h)
            near_outs[1][h * hs : (h + 1) * hs, :] = of_rank(1, 0, h)

    fars_count = halves * (groups - 1)
    made = pl.pallas_call(
        kernel,
        in_specs=[smem()] + vmem(5 + parts * per),
        out_specs=vmem(3 + fars_count + 2),
        out_shape=[sds((tokens, width), f32), sds((tokens, width), bf16), sds((4, width), f32)]
        + [sds((2, hs, tokens), bf16)] * fars_count
        + [sds((slab, tokens), bf16)] * 2,
        compiler_params=params(),
        cost_estimate=pl.CostEstimate(
            flops=2 * tokens * width * width, bytes_accessed=2 * width * width + 16 * tokens * width, transcendentals=tokens
        ),
        name="turn",
    )(slots, after1, near, live_grad, lines, out_full, *[v for part in fars for v in part])
    sent = [[made[3 + h * (groups - 1) + step] for step in range(groups - 1)] for h in range(halves)]
    return made[0], made[1], made[2], sent, made[-2], made[-1]


def part_ways(x_ref, value, kept, sent):
    depth, rows = kept.shape[:2]
    for flip in range(2):

        @pl.when(x_ref[0] == flip)
        def _(flip=flip):
            for z in range(depth):
                low, other = (2 * z + flip) * rows, (2 * z + 1 - flip) * rows
                kept[z] = value[low : low + rows, :]
                sent[z] = value[other : other + rows, :]


def weight_grad(lefts, rights, wide=1, into=None):
    rows = lefts[0][0].shape[1]
    cols = rights[0][0].shape[1]
    tile = 256 if cols % 256 == 0 else cols
    count, right_count = len(lefts), len(rights)

    def ends_of(parts):
        return [sum(size for _, _, size in parts[:i]) for i in range(len(parts) + 1)]

    left_ends, right_ends = ends_of(lefts), ends_of(rights)
    tokens = left_ends[-1]

    def kernel(*refs):
        left_refs, right_refs = refs[:count], refs[count : count + right_count]
        out_ref, turned, joined = refs[-3:]

        @pl.when(pl.program_id(0) == 0)
        def _():
            for i in range(count):
                turned[:, left_ends[i] : left_ends[i + 1]] = left_refs[i][...].T

        for i in range(right_count):
            joined[right_ends[i] : right_ends[i + 1], :] = right_refs[i][...]
        out_ref[...] = nn(turned[...], joined[...]).astype(bf16)

    whole = [pl.BlockSpec((size, rows), lambda i, at=at: (at, 0)) for _, at, size in lefts]
    strips = [pl.BlockSpec((size, tile), lambda i, at=at: (at, i)) for _, at, size in rights]
    shift = 0 if into is None else cols // tile
    return pl.pallas_call(
        kernel,
        grid=(cols // tile,),
        in_specs=whole + strips + ([] if into is None else [pl.BlockSpec(memory_space=pl.ANY)]),
        out_specs=pl.BlockSpec((rows, tile), lambda i: (0, i + shift)),
        out_shape=sds((rows, wide * cols), bf16),
        input_output_aliases={} if into is None else {count + right_count: 0},
        scratch_shapes=[pltpu.VMEM((rows, tokens), bf16), pltpu.VMEM((tokens, tile), bf16)],
        compiler_params=params(),
        cost_estimate=pl.CostEstimate(
            flops=2 * tokens * rows * cols, bytes_accessed=2 * (tokens * (rows + cols) + rows * cols), transcendentals=0
        ),
        name="weight_grad",
    )(*[v for v, _, _ in lefts + rights], *([] if into is None else [into]))


def head_grad(x_at, normed, grad_heads, depth, extra=()):
    tokens, width = normed.shape
    features = grad_heads.shape[0]
    tile = 512 if tokens % 512 == 0 else tokens
    share = width // (2 * depth)
    cols = features + (extra[0].shape[1] if extra else 0)

    def kernel(x_ref, n_ref, g_ref, *refs):
        kept, sent, total = refs[-3:]
        part = nn(g_ref[...], n_ref[...])

        @pl.when(pl.program_id(0) == 0)
        def _():
            total[...] = part

        @pl.when(pl.program_id(0) > 0)
        def _():
            total[...] += part

        @pl.when(pl.program_id(0) == pl.num_programs(0) - 1)
        def _():
            value = total[...].astype(bf16).T
            if extra:
                more = refs[0][...].astype(f32)
                for v in refs[1:-3]:
                    more = more + v[...].astype(f32)
                value = jnp.concatenate([value, more.astype(bf16)], axis=1)
            part_ways(x_ref, value, kept, sent)

    return pl.pallas_call(
        kernel,
        grid=(tokens // tile,),
        in_specs=[
            smem(),
            pl.BlockSpec((tile, width), lambda i: (i, 0)),
            pl.BlockSpec((features, tile), lambda i: (0, i)),
        ]
        + [pl.BlockSpec(v.shape, lambda i: (0, 0)) for v in extra],
        out_specs=[pl.BlockSpec((depth, share, cols), lambda i: (0, 0, 0))] * 2,
        out_shape=[sds((depth, share, cols), bf16)] * 2,
        scratch_shapes=[pltpu.VMEM((features, width), f32)],
        compiler_params=params(),
        cost_estimate=pl.CostEstimate(
            flops=2 * tokens * width * features, bytes_accessed=2 * tokens * (width + features), transcendentals=0
        ),
        name="head_grad",
    )(x_at, normed, grad_heads, *extra)


def out_grad_halves(core_at, mixed, grad):
    rows, tokens = mixed.shape
    width = grad.shape[1]
    half = width // 2

    def kernel(core_ref, m_ref, g_ref, kept, sent):
        value = nn(m_ref[...], g_ref[...]).astype(bf16)
        for core in range(2):

            @pl.when(core_ref[0] == core)
            def _(core=core):
                kept[...] = value[:, core * half : (core + 1) * half]
                sent[...] = value[:, (1 - core) * half : (2 - core) * half]

    return pl.pallas_call(
        kernel,
        in_specs=[smem()] + vmem(2),
        out_specs=vmem(2),
        out_shape=[sds((rows, half), bf16)] * 2,
        compiler_params=params(),
        cost_estimate=pl.CostEstimate(
            flops=2 * rows * tokens * width, bytes_accessed=4 * rows * width, transcendentals=0
        ),
        name="out_grad_halves",
    )(core_at, mixed, grad)


def out_grad_parts(seq_at, kept, came, groups):
    rows, half = kept.shape
    slab = half // groups

    def kernel(seq_ref, a_ref, b_ref, *outs):
        value = (a_ref[...].astype(f32) + b_ref[...].astype(f32)).astype(bf16)
        for at in range(groups):

            @pl.when(seq_ref[0] == at)
            def _(at=at):
                for step in range(groups):
                    low = (at + step) % groups * slab
                    outs[step][...] = value[:, low : low + slab]

    return pl.pallas_call(
        kernel,
        in_specs=[smem()] + vmem(2),
        out_specs=vmem(groups),
        out_shape=[sds((rows, slab), bf16)] * groups,
        compiler_params=params(),
        cost_estimate=pl.CostEstimate(flops=0, bytes_accessed=6 * rows * half, transcendentals=0),
        name="out_grad_parts",
    )(seq_at, kept, came)


def local(
    frames_in,
    clip_lengths,
    norm1_gain,
    norm1_bias,
    q_weight,
    q_bias,
    k_weight,
    v_weight,
    v_bias,
    o_weight,
    o_bias,
    norm2_gain,
    norm2_bias,
    up_weight,
    up_bias,
    down_weight,
    down_bias,
    out_grad,
):
    clip_count, local_frames, width = frames_in.shape
    hidden = up_weight.shape[1]
    groups = lax.axis_size("seq")
    shards = lax.axis_size("fsdp")
    pairs = shards // 2
    depth = pairs // 2
    ranks = groups * 2
    frames = local_frames * groups
    assert clip_count == 1
    tokens = clip_count * local_frames
    head_count = width // HEAD_DIM
    heads = head_count // ranks
    halves = 2 if heads % 2 == 0 else 1
    slab = heads * HEAD_DIM
    cut = slab // halves
    own_rows = width // shards
    own_hidden = hidden // shards
    piece = own_hidden * 2 // ranks
    rank_hidden = piece * pairs
    clips = 2 * clip_count
    token_parts = 2
    part_rows = tokens // token_parts
    fsdp = lax.axis_index("fsdp")
    seq = lax.axis_index("seq")
    core, pair = fsdp % 2, fsdp // 2
    xpos, zpos = pair % 2, pair // 2
    rank = core * groups + seq
    peer = (1 - core) * groups + seq

    core_way = [(i, i ^ 1) for i in range(shards)]
    x_way = [(i, i ^ 2) for i in range(shards)]

    def over_core(v):
        return lax.ppermute(v, "fsdp", core_way)

    def over_x(v):
        return lax.ppermute(v, "fsdp", x_way)

    def over_z(v, step):
        return lax.ppermute(v, "fsdp", [(i, (i + 4 * step) % shards) for i in range(shards)])

    def from_seq(v, step):
        return lax.ppermute(v, "seq", [(i, (i - step) % groups) for i in range(groups)])

    def to_seq(v, step):
        return from_seq(v, -step % groups)

    steps = range(1, groups)

    def by_core(mine, other):
        return jnp.where(
            core == 0, jnp.concatenate([mine, other]), jnp.concatenate([other, mine])
        )

    slots = []
    for step in range(depth):
        for flip in range(2):
            slots.append(((zpos - step) % depth) * 2 + (xpos ^ flip))
    slots = jnp.stack(slots).astype(jnp.int32)

    def spread_z(payload):
        return [payload] + [over_z(payload, step) for step in range(1, depth)]

    def spread_x(blocks):
        return [v for block in blocks for v in (block, over_x(block))]

    small = [norm1_gain, norm1_bias, q_bias, v_bias, o_bias, norm2_gain, norm2_bias, down_bias]
    small = jnp.concatenate([jnp.stack(small), up_bias.reshape(hidden // width, own_rows)])
    small_rows = -(-small.shape[0] // 16) * 16
    small = jnp.pad(small, ((0, small_rows - small.shape[0]), (0, 0)))
    where = jnp.stack([rank, peer, core]).astype(jnp.int32)
    pay, up_mine, out_mine, pay_other, up_other, out_other = pick(
        where, q_weight, k_weight, v_weight, up_weight, o_weight, small, ranks, halves, pairs
    )
    base = -(-own_rows // 16) * 16
    pay_rows = base + small_rows
    frames_own = frames_in.reshape(tokens, width)
    pay_full = by_core(pay, over_core(pay_other))
    pay_z = spread_z(pay_full)
    frames_side = [from_seq(tie(frames_own, pay_full), step) for step in steps]

    up_own = by_core(up_mine, over_core(up_other))
    down_own = lax.dynamic_slice_in_dim(down_weight, seq * piece, piece, 0)
    out_own = by_core(out_mine, over_core(out_other))
    same_core = [[i for i in range(shards) if i % 2 == c] for c in range(2)]

    def over_chips(v):
        return lax.all_gather(v, "fsdp", axis=0, axis_index_groups=same_core)

    out_half = over_chips(out_own).reshape(width, width // 2)
    feed_own = jnp.concatenate([up_own.reshape(-1, width), down_own])
    gathered = over_chips(tie(feed_own, *pay_z[1:]))
    up_rows = up_own.size // width
    if rank_hidden == width:
        feed_weights = [gathered]
    else:
        feed_weights = [
            gathered[:, :up_rows].reshape(width, rank_hidden),
            gathered[:, up_rows:].reshape(rank_hidden, width),
        ]

    pay_z[depth // 2] = tie(pay_z[depth // 2], *frames_side)
    pay_all = spread_x(pay_z)
    frames_near = over_core(tie(frames_own, *pay_all))
    lengths_sent = jnp.broadcast_to(clip_lengths.astype(f32)[:, None], (clip_count, 128))
    lengths_near = over_core(tie(lengths_sent, *pay_z[1:]))
    frames_cross = [over_core(tie(v, *pay_all)) for v in frames_side]

    positions = jnp.concatenate(
        [
            ((seq + step) % groups) * local_frames + jnp.arange(local_frames, dtype=jnp.int32)
            for step in range(groups)
        ]
    )
    lengths = jnp.concatenate([clip_lengths, lengths_near[:, 0].astype(jnp.int32)])
    live = positions[None, :] < lengths[:, None]
    live_own = live[:clip_count, :local_frames].reshape(tokens, 1)
    mask = jnp.where(live, 0.0, NEGATIVE).astype(bf16)
    mask = jnp.pad(mask[:, None, :], ((0, 0), (0, 15), (0, 0))).reshape(clips * 16, frames)
    live_grad = jnp.where(live_own, out_grad.reshape(tokens, width), 0.0).astype(bf16)

    grad_side = [from_seq(tie(live_grad, *frames_side), step) for step in steps]

    qkv_part, small_part = place(
        pay_all,
        slots,
        [
            [(0, own_rows), (pay_rows, pay_rows + own_rows)],
            [(base, pay_rows), (pay_rows + base, 2 * pay_rows)],
        ],
    )
    qkv_full = qkv_part.reshape(width, 3 * slab)
    ubias = small_part[:, 8 : 8 + hidden // width, :own_rows].astype(f32).reshape(pairs, ranks, piece)
    ubias = lax.dynamic_index_in_dim(ubias, rank, 1, keepdims=False).reshape(1, rank_hidden)


    def to_z(both):
        blocks = [
            lax.dynamic_index_in_dim(both, (zpos + step) % depth, 0, keepdims=False) for step in range(depth)
        ]
        return blocks[0], [v.astype(bf16) for v in blocks[1:]]

    def reduce_z(kept, sent, parted=True):
        both = kept.astype(f32) + over_x(sent).astype(f32)
        return to_z(both) if parted else both

    def reduce_end(own, sent):
        total = own
        for step in range(1, depth):
            total = total + over_z(sent[step - 1], step).astype(f32)
        return total.astype(bf16)

    def along_seq(v):
        return [v] + [from_seq(v, step) for step in steps]

    def own_of_ranks(v):
        blocks = v.reshape(2, own_rows, -1)
        keep = lax.dynamic_index_in_dim(blocks, core, 0, keepdims=False)
        other = over_core(lax.dynamic_index_in_dim(blocks, 1 - core, 0, keepdims=False))
        return jnp.stack([keep, other])

    rank_at = rank.reshape(1).astype(jnp.int32)
    seq_at = seq.reshape(1).astype(jnp.int32)
    frames_all = [frames_own] + frames_side + [frames_near] + frames_cross
    normed1, qkv, lines = project(rank_at, frames_all, small_part, qkv_full, halves)
    grad_cross_near = over_core(tie(live_grad, lines))
    grad_cross = [over_core(tie(v, lines)) for v in grad_side]
    grad_near = [(v, t) for v in (live_grad, grad_cross_near) for t in range(token_parts)]
    grad_far = [[(v, t) for v in grad_side + grad_cross] for t in range(token_parts)]

    out_half = out_half.reshape(width, width // 2)
    out_rest = over_core(out_half)
    out_full = jnp.where(
        core == 0,
        jnp.concatenate([out_half, out_rest], axis=1),
        jnp.concatenate([out_rest, out_half], axis=1),
    )
    half_heads = heads // halves
    logs, tops, sources = [], [], []
    mixed_blocks = [[] for _ in range(ranks)]

    def flat(v):
        return jnp.swapaxes(v, 0, 1).reshape(v.shape[1], tokens)

    for half in range(halves):
        if half:
            qkv = tie(qkv, grad_cross_near, *grad_cross)
        near, far, log_half, top_half = attend(qkv, mask, clips, half_heads, half, halves, groups)
        logs.append(log_half)
        tops.append(top_half)
        came = [near] + [to_seq(far[step - 1], step) for step in steps]
        for step, v in enumerate(came):
            mixed_blocks[step].append(flat(v[:clip_count]))
            mixed_blocks[groups + step].append(flat(over_core(v[clip_count:])))
    sources = [
        (core ^ flip) * groups + (seq - step) % groups for flip in range(2) for step in range(groups)
    ]
    sources = jnp.stack(sources).astype(jnp.int32)
    mixed_own, after1, normed2_own = merge(
        sources, frames_own, out_full, lines, mixed_blocks, halves, token_parts
    )

    normed2_side = [[from_seq(v, step) for step in steps] for v in normed2_own]
    normed2_near = normed2_own + [over_core(v) for v in normed2_own]

    def parts_of(arrays):
        return [(v, 0) for v in arrays]

    act_near, back_near, grad2_own, grad2_other, fed_own, fed_other, sums = feed(
        parts_of(normed2_near), grad_near, token_parts, part_rows, feed_weights, ubias
    )
    normed2_side = [[tie(v, sums) for v in side] for side in normed2_side]
    normed2_far = [side + [over_core(v) for v in side] for side in normed2_side]
    normed2_far[0][0] = tie(normed2_far[0][0], *sum(normed2_side, []))
    act_far, back_far, grad2_sent, fed_parts = [], [], [], []

    def far_sums(own, other):
        both = (own + over_core(other).astype(f32)).astype(bf16)
        return [both[i * part_rows : (i + 1) * part_rows] for i in range(len(steps))]

    for t in range(token_parts):
        if t:
            normed2_far[t][0] = tie(normed2_far[t][0], *grad2_sent[t - 1])
        act, back, far_own, far_other, out_own_far, out_other_far, sums_far = feed(
            parts_of(normed2_far[t]), grad_far[t], len(steps), part_rows, feed_weights, ubias
        )
        act_far.append(act)
        back_far.append(back)
        grad2_sent.append(far_sums(far_own, far_other))
        fed_parts.append((out_own_far, out_other_far))
        sums = sums + sums_far

    grad2_far = [[to_seq(v, step) for v, step in zip(part, steps)] for part in grad2_sent]
    grad2_near = grad2_own + over_core(grad2_other).astype(f32)

    def with_sizes(parts):
        return [(v, at, part_rows) for v, at in parts]

    def wholes(arrays):
        return [(v, 0, v.shape[0]) for v in arrays]

    x_at = xpos.reshape(1).astype(jnp.int32)
    lefts = with_sizes(parts_of(normed2_near + sum(normed2_far, [])))
    lefts[0] = (tie(lefts[0][0], grad2_near, *grad2_sent[-1]),) + lefts[0][1:]

    def over_chips_sum(v):
        return lax.psum_scatter(v, "fsdp", scatter_dimension=0, axis_index_groups=same_core, tiled=True)

    rights = wholes([back_near] + back_far)
    acts, cotangents = wholes([act_near] + act_far), with_sizes(grad_near + sum(grad_far, []))
    if rank_hidden == width:
        feed_sum = weight_grad(acts, cotangents, 2, weight_grad(lefts, rights, 2))
        feed_shard = over_chips_sum(feed_sum)
        up_shard, down_shard = feed_shard[:, :width], feed_shard[:, width:]
    else:
        feed_sum = weight_grad(acts, cotangents)
        up_shard, down_shard = over_chips_sum(weight_grad(lefts, rights)), over_chips_sum(feed_sum)

    targets = [
        (core ^ flip) * groups + (seq + step) % groups for flip in range(2) for step in range(groups)
    ]
    targets = jnp.stack(targets).astype(jnp.int32)
    grad_after1, grad_attn, sums2, grad_sent, heads_own, heads_other = turn(
        targets, after1, tie(grad2_near, feed_sum), grad2_far, live_grad, lines, out_full, halves, groups
    )
    half_rows = heads // halves
    heads_cross = over_core(heads_other)
    head_grads, arrived, sides = [], [], []
    for half in range(halves):
        came = [to_seq(v, step) for v, step in zip(grad_sent[half], steps)]
        came = [came[groups - step - 1] for step in steps]
        cross = [over_core(v) for v in came]
        sides.append(came)
        arrived += cross
        head_grads.append(
            [
                [(heads_own, half * half_rows)] + [(v, 0) for v in came],
                [(heads_cross, half * half_rows)] + [(v, 1) for v in cross],
            ]
        )

    out_kept, out_other_half = out_grad_halves(where[2:], mixed_own, grad_attn)
    out_parts = out_grad_parts(seq_at, out_kept, over_core(out_other_half), groups)
    out_sent = list(out_parts[1:])
    out_came = [to_seq(v, step) for v, step in zip(out_sent, steps)]
    def fed_sums(after):
        both = [(mine + over_core(tie(other, after)).astype(f32)).astype(bf16) for mine, other in fed_parts]
        sent = [jnp.concatenate([v[i * part_rows : (i + 1) * part_rows] for v in both]) for i in range(len(steps))]
        return sent, fed_own + over_core(tie(fed_other, after)).astype(f32)

    grad_qkv, x_parts = [], []
    for half in range(halves):
        if half:
            fed_sent, fed_near = fed_sums(x_parts[0][1])
            fed_far = [to_seq(v, step) for v, step in zip(fed_sent, steps)]
            after = [x_parts[0][1], fed_near] + fed_sent
        else:
            after = out_sent + arrived
        own = head_grads[half][0]
        own[0] = (tie(own[0][0], *after), own[0][1])
        grads = attend_back(qkv, mask, head_grads[half], logs[half], clips, half_heads, half, halves, groups)
        grads = grads.reshape(3 * cut, -1)
        if half:
            grads = tie(grads, *fed_far)
        grad_qkv.append(grads)
        x_parts.append(head_grad(x_at, normed1, grads, depth, () if half else [out_parts[0]] + out_came))
    if halves == 1:
        fed_sent, fed_near = fed_sums(x_parts[0][1])
        fed_far = [to_seq(v, step) for v, step in zip(fed_sent, steps)]
    fed = tie(fed_near, x_parts[-1][1])
    for v in fed_far:
        fed = fed + v.astype(f32)
    output = (after1 + (fed + lines[7:8])).astype(bf16).reshape(clip_count, local_frames, width)
    kept, sent = x_parts[0]
    z_parts = [reduce_z(tie(kept, grad_qkv[-1]), sent)]
    feed_last = jnp.concatenate(
        [own_of_ranks(up_shard).reshape(2 * own_rows, rank_hidden), down_shard.reshape(-1, rank_hidden)]
    )
    grad_qkv[-1] = tie(grad_qkv[-1], x_parts[-1][1], *z_parts[0][1])
    far_own, far_other, far_sums1, far_bias = project_back(grad_qkv, qkv_full, frames_side + frames_cross, steps, groups)
    far_cross = over_core(far_other).astype(f32)
    far1 = (far_own + far_cross).astype(bf16)
    far1 = [far1[i * tokens : (i + 1) * tokens] for i in range(len(steps))]
    near_own, near_other, near_sums1, near_bias = project_back(
        [tie(grad_qkv[0], *far1)] + grad_qkv[1:], qkv_full, [frames_own, frames_near], [0], groups
    )
    feed_lasts = along_seq(tie(feed_last, near_other))
    sums1, bias_sums = far_sums1 + near_sums1, far_bias + near_bias
    shard_parts = [reduce_end(tie(z_parts[0][0], near_other), z_parts[0][1])]
    x_sums = [reduce_z(tie(kept, near_other), sent, False) for kept, sent in x_parts[1:]]
    grad_normed1 = near_own + over_core(near_other).astype(f32)
    for v, step in zip(far1, steps):
        grad_normed1 = grad_normed1 + to_seq(v, step).astype(f32)
    plain1, scale1 = normalized(frames_own.astype(f32))
    in_grad = (grad_after1 + norm_back(plain1, scale1, grad_normed1 * lines[0:1])).astype(bf16)

    for both in x_sums:
        shard_parts.append(reduce_end(*to_z(both)))
    heads_last = own_of_ranks(jnp.concatenate(shard_parts, axis=1))

    up_weight_grad, down_weight_grad = finish_feed(
        rank_at,
        [v[: 2 * own_rows].reshape(2, own_rows, rank_hidden) for v in feed_lasts],
        [v[2 * own_rows :].reshape(piece, width) for v in feed_lasts],
        pairs,
        groups,
    )
    q_weight_grad, k_weight_grad, v_weight_grad, o_weight_grad = finish_heads(
        rank_at, along_seq(heads_last), halves, groups
    )

    bias_cols = bias_sums[0].reshape(halves, 3, cut)

    def at_rank(v):
        return lax.dynamic_update_slice_in_dim(jnp.zeros((width,), f32), v, rank * slab, 0)

    up_sums = lax.dynamic_update_index_in_dim(
        jnp.zeros((pairs, ranks, piece), f32), sums.reshape(pairs, piece), rank, 1
    ).reshape(hidden // width, width)
    tops = jnp.stack([jnp.max(v.reshape(clips, half_heads, frames), axis=(0, 2)) for v in tops])
    tops = tops.reshape(heads) / math.sqrt(HEAD_DIM)
    peak_row = lax.dynamic_update_slice_in_dim(
        jnp.full((width,), NEGATIVE, f32), tops, rank * heads, 0
    )
    added = 8 + hidden // width
    stack = jnp.concatenate(
        [
            sums1[:2],
            at_rank(bias_cols[:, 0].reshape(slab))[None],
            at_rank(bias_cols[:, 2].reshape(slab))[None],
            sums2[2:3],
            sums2[:2],
            sums2[3:4],
            up_sums,
            peak_row[None],
        ]
    )
    is_sum = (jnp.arange(added + 1) < added)[:, None]

    def combine(a, b):
        return jnp.where(is_sum, a + b, jnp.maximum(a, b))

    stack = combine(stack, over_core(stack))
    stack = combine(stack, over_x(stack))
    step = 4
    while step < shards:
        stack = combine(stack, lax.ppermute(stack, "fsdp", [(i, i ^ step) for i in range(shards)]))
        step *= 2
    stack = tie(stack, grad_normed1)
    step = 1
    while step < groups:
        stack = combine(stack, lax.ppermute(stack, "seq", [(i, i ^ step) for i in range(groups)]))
        step *= 2
    small_own = lax.dynamic_slice_in_dim(stack[:8], fsdp * own_rows, own_rows, 1)
    up_bias_grad = lax.dynamic_slice_in_dim(stack[8:added].reshape(hidden), fsdp * own_hidden, own_hidden, 0)
    logit_peak = stack[added, :head_count]

    factor = jnp.sqrt(LOGIT_CAP / jnp.maximum(logit_peak, LOGIT_CAP))
    column_factor = jnp.repeat(factor, HEAD_DIM)
    q_weight_clipped = q_weight.astype(f32) * column_factor[None, :]
    k_weight_clipped = k_weight.astype(f32) * column_factor[None, :]
    q_bias_clipped = q_bias.astype(f32) * lax.dynamic_slice_in_dim(
        column_factor, fsdp * own_rows, own_rows, 0
    )
    return (
        output,
        in_grad.reshape(clip_count, local_frames, width),
        small_own[0],
        small_own[1],
        q_weight_grad,
        small_own[2],
        k_weight_grad,
        v_weight_grad,
        small_own[3],
        o_weight_grad,
        small_own[4],
        small_own[5],
        small_own[6],
        up_weight_grad,
        up_bias_grad,
        down_weight_grad,
        small_own[7],
        logit_peak,
        q_weight_clipped,
        q_bias_clipped,
        k_weight_clipped,
    )


def solution(mesh):
    rows, vector, clip = P("fsdp", None), P("fsdp"), P("fsdp", "seq", None)
    return jax.shard_map(
        local,
        mesh=mesh,
        in_specs=(
            clip,
            vector,
            vector,
            vector,
            rows,
            vector,
            rows,
            rows,
            vector,
            rows,
            vector,
            vector,
            vector,
            rows,
            vector,
            rows,
            vector,
            clip,
        ),
        out_specs=(
            clip,
            clip,
            vector,
            vector,
            rows,
            vector,
            rows,
            rows,
            vector,
            rows,
            vector,
            vector,
            vector,
            rows,
            vector,
            rows,
            vector,
            P(),
            rows,
            vector,
            rows,
        ),
        check_vma=False,
    )
```

time: 705 us -> 550 us (0.78)
  Pallas kernels: 84.6 us -> 219 us
  matrix products: 101 us -> 0 us
  local copies, waits for them, and re-layouts: 124 us -> 26.9 us
  other arithmetic: 73.2 us -> 33.8 us
  waiting for transfers between devices: 222 us -> 184 us
  starting transfers between devices: 73.5 us -> 61.5 us
    pallas_call x6 -> x22, Pallas kernels: 84.6 us -> 219 us  [the longest x3 47.2 us: feed(): pl.pallas_call(lambda *refs: feed_kernel(count, own, tile, refs), grid=(1...]
    dot_general x14 -> x0, matrix products: 101 us -> none  [dot(): lax.dot_general(left, right, (((left_dim,), (right_dim,)), ((), ())), pre...]
    ppermute x12 -> x7, waiting for transfers between devices: 54.2 us -> 20.5 us  [over_x(): return lax.ppermute(v, 'fsdp', x_way)]
    convert_element_type x17 -> x2, local copies, waits for them, and re-layouts: 29 us -> 1.02 us  [to_z(): return (blocks[0], [v.astype(bf16) for v in blocks[1:]])]
    ppermute x18 -> x12, waiting for transfers between devices: 65.8 us -> 47.8 us  [the longest x9 37.2 us: over_z(): lax.ppermute(v, 'fsdp', [(i, (i + 4 * step) % shards) for i in range(shar...]
    unnamed x153 -> x100, local copies, waits for them, and re-layouts: 23.4 us -> 6.94 us
    convert_element_type x14 -> x7, other arithmetic: 19.2 us -> 3.44 us  [the longest x2 1.58 us: far_sums(): both = (own + over_core(other).astype(f32)).astype(bf16)]
    dynamic_slice x10 -> x4, local copies, waits for them, and re-layouts: 14.1 us -> 0.76 us  [the longest x1 0.65 us: local(): lax.dynamic_slice_in_dim(stack[8:added].reshape(hidden), fsdp * own_hidde...]
  transfers between devices with their start and end apart: 74 -> 69, of which waited for: 27 -> 31; matrix products, arithmetic and copies ran while one was open for 36% -> 8% of each run, Pallas kernels for 10% -> 32%
where the time goes in v2:
time: 550 us; the launch traced here: 541 us
  Pallas kernels  219 us (40%)
  waiting for transfers between devices  184 us (33%)
  starting transfers between devices  61.5 us (11%)
  other arithmetic  33.8 us (6%)
  local copies, waits for them, and re-layouts  26.9 us (5%)
  between operations  16 us (3%)
    ppermute x15, waiting for transfers between devices, from_seq(): lax.ppermute(v, 'seq', [(i, (i - step) % groups) for i in range(groups)])  90.3 us
    pallas_call x3, Pallas kernels, feed(): pl.pallas_call(lambda *refs: feed_kernel(count, own, tile, refs), grid=(1...  47.2 us
    ppermute x9, waiting for transfers between devices, over_z(): lax.ppermute(v, 'fsdp', [(i, (i + 4 * step) % shards) for i in range(shar...  37.2 us
    pallas_call x2, Pallas kernels, attend_back(): pl.pallas_call(lambda *refs: attend_back_kernel(span, 1.0 / math.sqrt(HEA...  35.6 us
    ppermute x9, starting transfers between devices, over_z(): lax.ppermute(v, 'fsdp', [(i, (i + 4 * step) % shards) for i in range(shar...  27.1 us
    pallas_call x2, Pallas kernels, weight_grad(): pl.pallas_call(kernel, grid=(cols // tile,), in_specs=whole + strips + ([...  27 us
    pallas_call x2, Pallas kernels, project_back(): pl.pallas_call(kernel, grid=(count,), in_specs=[pl.BlockSpec(weight.shape...  20.5 us
    ppermute x7, waiting for transfers between devices, over_x(): return lax.ppermute(v, 'fsdp', x_way)  20.5 us
  transfers between devices with their start and end apart: 69, of which 31 were waited for; matrix products, arithmetic and copies ran while one was open for 8% of the time, Pallas kernels for 32%

profile of v2, /device:TPU:0, one launch (start us, length us, event | category | flops | bytes accessed | tf_op | source)
XLA Modules:
  0.0 541.3 jit_solution(8941861749235479593)
XLA Ops:
  10.1 2.8 pick.1
  19.3 3.0 collective-permute-start.4
  22.3 2.6 collective-permute-start.6
  28.5 8.3 %collective-permute-done.4.refs_2_ = bf16[192,960]{1,0:T(8,128)(2,1)S(1)} collective-permute-done((bf16[192,960]{1,0:T(8,128)(2,1)S(1)}, bf16[192,960]{1,0:T(8,128)(2,1)S(1)}, u32[]{:S(2)}, u32[]{:S(2)}) %collective-permute-start.4) | collective-permute-done | bytes 368672 | tf_op jit(solution)/shard_map/ppermute | solution.py:897
  36.8 20.5 %collective-permute-done.6.refs_4_ = bf16[192,960]{1,0:T(8,128)(2,1)S(1)} collective-permute-done((bf16[192,960]{1,0:T(8,128)(2,1)S(1)}, bf16[192,960]{1,0:T(8,128)(2,1)S(1)}, u32[]{:S(2)}, u32[]{:S(2)}) %collective-permute-start.6) | collective-permute-done | bytes 368672 | tf_op jit(solution)/shard_map/ppermute | solution.py:897
  62.5 25.7 %collective-permute-done.7.refs_1_.refs_2_ = bf16[512,1280]{1,0:T(8,128)(2,1)} collective-permute-done((bf16[512,1280]{1,0:T(8,128)(2,1)S(1)}, bf16[512,1280]{1,0:T(8,128)(2,1)}, u32[]{:S(2)}, u32[]{:S(2)}) %collective-permute-start.7) | collective-permute-done | bytes 1310752 | tf_op jit(solution)/shard_map/ppermute | solution.py:900
  91.7 4.9 collective-permute-done.10.refs_7_
  96.6 9.6 %collective-permute-done.8.refs_5_ = bf16[192,960]{1,0:T(8,128)(2,1)S(1)} collective-permute-done((bf16[192,960]{1,0:T(8,128)(2,1)S(1)}, bf16[192,960]{1,0:T(8,128)(2,1)S(1)}, u32[]{:S(2)}, u32[]{:S(2)}) %collective-permute-start.8) | collective-permute-done | bytes 368672 | tf_op jit(solution)/shard_map/ppermute | solution.py:894
  109.4 3.8 place.1
  113.2 14.2 %project.1 = (bf16[2048,1280]{1,0:T(8,128)(2,1)}, bf16[960,2048]{1,0:T(8,128)(2,1)}, f32[16,1280]{1,0:T(8,128)}) custom-call(s32[1]{0:T(128)} %bitcast.5.rank_ref, bf16[16,16,960]{2,1,0:T(8,128)(2,1)} %get-tuple-element.130.small_ref, bf16[1280,960]{1,0:T(8,128)(2,1)} %bitcast.155, bf16[512,1280]{1,0:T(8,128)(2,1)} %bitcast.118, ...), custom_call_target="tpu_custom_call" | custom-call | flops 5033164800 | bytes 18186240 | tf_op jit(solution)/shard_map/project/pallas_call | solution.py:328
  127.9 12.0 %collective-permute-done.15.refs_2_.refs_7_.refs_9_ = bf16[512,1280]{1,0:T(8,128)(2,1)} collective-permute-done((bf16[512,1280]{1,0:T(8,128)(2,1)S(1)}, bf16[512,1280]{1,0:T(8,128)(2,1)}, u32[]{:S(2)}, u32[]{:S(2)}) %collective-permute-start.15) | collective-permute-done | bytes 1310752 | tf_op jit(solution)/shard_map/ppermute | solution.py:900
  141.7 9.0 %attend.2 = (bf16[2,160,512]{2,1,0:T(8,128)(2,1)}, bf16[1,2,160,512]{3,2,1,0:T(8,128)(2,1)}, f32[4,1,1024]{2,1,0:T(1,128)}, f32[4,1,1024]{2,1,0:T(1,128)}) custom-call(bf16[960,2048]{1,0:T(8,128)(2,1)} %get-tuple-element.141.refs_0_.refs_1_.refs_2_, bf16[960,2048]{1,0:T(8,128)(2,1)} %get-tuple-element.141.refs_0_.refs_1_.refs_2_, ...), custom_call_target="tpu_custom_call" | custom-call | flops 8388608000 | bytes 2949120 | tf_op jit(solution)/shard_map/attend/pallas_call | solution.py:104
  152.7 9.5 %attend.3 = (bf16[2,160,512]{2,1,0:T(8,128)(2,1)}, bf16[1,2,160,512]{3,2,1,0:T(8,128)(2,1)}, f32[4,1,1024]{2,1,0:T(1,128)}, f32[4,1,1024]{2,1,0:T(1,128)}) custom-call(bf16[960,2048]{1,0:T(8,128)(2,1)} %get-tuple-element.141.refs_0_.refs_1_.refs_2_, bf16[960,2048]{1,0:T(8,128)(2,1)} %get-tuple-element.141.refs_0_.refs_1_.refs_2_, ...), custom_call_target="tpu_custom_call" | custom-call | flops 8388608000 | bytes 2949120 | tf_op jit(solution)/shard_map/attend/pallas_call | solution.py:104
  166.9 5.7 %collective-permute-done.18 = bf16[2,160,512]{2,1,0:T(8,128)(2,1)S(1)} collective-permute-done((bf16[2,160,512]{2,1,0:T(8,128)(2,1)}, bf16[2,160,512]{2,1,0:T(8,128)(2,1)S(1)}, u32[]{:S(2)}, u32[]{:S(2)}) %collective-permute-start.18) | collective-permute-done | bytes 327712 | tf_op jit(solution)/shard_map/ppermute | solution.py:900
  173.3 2.6 maximum_select_fusion.w_ref
  176.7 6.6 %merge.1 = (bf16[1280,512]{1,0:T(8,128)(2,1)}, f32[512,1280]{1,0:T(8,128)}, bf16[256,1280]{1,0:T(8,128)(2,1)}, bf16[256,1280]{1,0:T(8,128)(2,1)}) custom-call(s32[4]{0:T(128)} %pad_add_fusion.1.slots_ref, bf16[512,1280]{1,0:T(8,128)(2,1)} %bitcast.119, bf16[1280,1280]{1,0:T(8,128)(2,1)} %maximum_select_fusion.w_ref, ...), custom_call_target="tpu_custom_call" | custom-call | flops 1677721600 | bytes 11141120 | tf_op jit(solution)/shard_map/merge/pallas_call | solution.py:604
  187.5 6.9 %all-gather.6.cloned.1.call-done = bf16[2560,1280]{1,0:T(8,128)(2,1)} async-done(((bf16[320,1280]{1,0:T(8,128)(2,1)}), bf16[2560,1280]{1,0:T(8,128)(2,1)}) %all-gather.6.cloned.1.call-update) | async-done | bytes 6553616 | tf_op jit(solution)/shard_map/all_gather | solution.py:945
  194.3 21.8 %feed.3 = (bf16[1024,1280]{1,0:T(8,128)(2,1)}, bf16[1024,1280]{1,0:T(8,128)(2,1)}, f32[512,1280]{1,0:T(8,128)}, bf16[512,1280]{1,0:T(8,128)(2,1)}, f32[512,1280]...) custom-call(bf16[256,1280]{1,0:T(8,128)(2,1)} %get-tuple-element.169.refs_0_, ...), custom_call_target="tpu_custom_call" | custom-call | flops 13421772800 | bytes 27525120 | tf_op jit(solution)/shard_map/feed/pallas_call | solution.py:266
  219.2 12.6 %feed.4 = (bf16[512,1280]{1,0:T(8,128)(2,1)}, bf16[512,1280]{1,0:T(8,128)(2,1)}, f32[256,1280]{1,0:T(8,128)}, bf16[256,1280]{1,0:T(8,128)(2,1)}, f32[256,1280]{1...) custom-call(bf16[256,1280]{1,0:T(8,128)(2,1)} %copy-done.42, bf16[256,1280]{1,0:T(8,128)(2,1)} %copy-done.43, ...), custom_call_target="tpu_custom_call" | custom-call | flops 6710886400 | bytes 17039360 | tf_op jit(solution)/shard_map/feed/pallas_call | solution.py:266
  237.9 12.8 %feed.5 = (bf16[512,1280]{1,0:T(8,128)(2,1)}, bf16[512,1280]{1,0:T(8,128)(2,1)}, f32[256,1280]{1,0:T(8,128)}, bf16[256,1280]{1,0:T(8,128)(2,1)}, f32[256,1280]{1...) custom-call(bf16[256,1280]{1,0:T(8,128)(2,1)} %collective-permute-done.28.refs_0_.refs_6_, ...), custom_call_target="tpu_custom_call" | custom-call | flops 6710886400 | bytes 17039360 | tf_op jit(solution)/shard_map/feed/pallas_call | solution.py:266
  254.5 13.1 %weight_grad.2.refs_11_ = bf16[1280,2560]{1,0:T(8,128)(2,1)} custom-call(bf16[256,1280]{1,0:T(8,128)(2,1)} %get-tuple-element.169.refs_0_, bf16[256,1280]{1,0:T(8,128)(2,1)} %get-tuple-element.147.refs_1_, bf16[256,1280]{1,0:T(8,128)(2,1)} %copy-done.40, bf16[256,1280]{1,0:T(8,128)(2,1)} %copy-done.41, bf16[256,1280]{1,0:T(8,128)(2,1)} %copy-done.42, ...), custom_call_target="tpu_custom_call" | custom-call | flops 6710886400 | bytes 13762560 | tf_op jit(solution)/shard_map/weight_grad/pallas_call | solution.py:721
  267.7 13.8 %weight_grad.3 = bf16[1280,2560]{1,0:T(8,128)(2,1)} custom-call(bf16[1024,1280]{1,0:T(8,128)(2,1)} %get-tuple-element.157.refs_0_, bf16[512,1280]{1,0:T(8,128)(2,1)} %get-tuple-element.162.refs_1_, bf16[512,1280]{1,0:T(8,128)(2,1)} %get-tuple-element.166.refs_2_, bf16[512,1280]{1,0:T(8,128)(2,1)} %copy-done.2, ...), custom_call_target="tpu_custom_call", output_to_operand_aliasing={{}: (11, {})} | custom-call | flops 6710886400 | bytes 13762560 | tf_op jit(solution)/shard_map/weight_grad/pallas_call | solution.py:721
  282.6 10.7 %turn.1 = (f32[512,1280]{1,0:T(8,128)}, bf16[512,1280]{1,0:T(8,128)(2,1)}, f32[4,1280]{1,0:T(4,128)}, bf16[2,160,512]{2,1,0:T(8,128)(2,1)}, bf16[2,160,512]{2,1,...) custom-call(s32[4]{0:T(128)} %pad_add_fusion.4.slots_ref, f32[512,1280]{1,0:T(8,128)} %get-tuple-element.145.after_ref, ...), custom_call_target="tpu_custom_call" | custom-call | flops 1677721600 | bytes 13762560 | tf_op jit(solution)/shard_map/turn/pallas_call | solution.py:664
  293.3 5.7 %out_grad_halves.1 = (bf16[1280,640]{1,0:T(8,128)(2,1)}, bf16[1280,640]{1,0:T(8,128)(2,1)}) custom-call(s32[1]{0:T(128)} %bitcast.7.core_ref, bf16[1280,512]{1,0:T(8,128)(2,1)} %get-tuple-element.175.m_ref, bf16[512,1280]{1,0:T(8,128)(2,1)} %get-tuple-element.176.g_ref), custom_call_target="tpu_custom_call" | custom-call | flops 1677721600 | bytes 6553600 | tf_op jit(solution)/shard_map/out_grad_halves/pallas_call | solution.py:800
  301.4 8.5 %collective-permute-done.36.refs_6_ = bf16[2,160,512]{2,1,0:T(8,128)(2,1)} collective-permute-done((bf16[2,160,512]{2,1,0:T(8,128)(2,1)}, bf16[2,160,512]{2,1,0:T(8,128)(2,1)}, u32[]{:S(2)}, u32[]{:S(2)}) %collective-permute-start.36) | collective-permute-done | bytes 327712 | tf_op jit(solution)/shard_map/ppermute | solution.py:900
  309.9 6.5 %collective-permute-done.38.refs_6_ = bf16[2,160,512]{2,1,0:T(8,128)(2,1)S(1)} collective-permute-done((bf16[2,160,512]{2,1,0:T(8,128)(2,1)}, bf16[2,160,512]{2,1,0:T(8,128)(2,1)S(1)}, u32[]{:S(2)}, u32[]{:S(2)}) %collective-permute-start.38) | collective-permute-done | bytes 327712 | tf_op jit(solution)/shard_map/ppermute | solution.py:900
  318.1 4.2 out_grad_parts.1
  324.7 17.6 %attend_back.2 = bf16[3,160,2048]{2,1,0:T(8,128)(2,1)} custom-call(bf16[960,2048]{1,0:T(8,128)(2,1)} %get-tuple-element.141.refs_0_.refs_1_.refs_2_, bf16[960,2048]{1,0:T(8,128)(2,1)} %get-tuple-element.141.refs_0_.refs_1_.refs_2_, bf16[960,2048]{1,0:T(8,128)(2,1)} %get-tuple-element.141.refs_0_.refs_1_.refs_2_, bf16[32,1024]{1,0:T(8,128)(2,1)} %bitcast.136, ...), custom_call_target="tpu_custom_call" | custom-call | flops 16777216000 | bytes 5898240 | tf_op jit(solution)/shard_map/attend_back/pallas_call | solution.py:180
  346.0 8.9 %head_grad.2 = (bf16[4,160,800]{2,1,0:T(8,128)(2,1)}, bf16[4,160,800]{2,1,0:T(8,128)(2,1)}) custom-call(s32[1]{0:T(128)} %bitcast.43.x_ref, bf16[2048,1280]{1,0:T(8,128)(2,1)} %get-tuple-element.153.n_ref, bf16[480,2048]{1,0:T(8,128)(2,1)} %bitcast.165, bf16[1280,320]{1,0:T(8,128)(2,1)} %get-tuple-element.184.refs_0_, bf16[1280,320]{1,0:T(8,128)(2,1)} %copy.46.refs_1_), custom_call_target="tpu_custom_call" | custom-call | flops 2516582400 | bytes 7208960 | tf_op jit(solution)/shard_map/head_grad/pallas_call | solution.py:766
  362.9 17.9 %attend_back.3 = bf16[3,160,2048]{2,1,0:T(8,128)(2,1)} custom-call(bf16[960,2048]{1,0:T(8,128)(2,1)} %get-tuple-element.141.refs_0_.refs_1_.refs_2_, bf16[960,2048]{1,0:T(8,128)(2,1)} %get-tuple-element.141.refs_0_.refs_1_.refs_2_, bf16[960,2048]{1,0:T(8,128)(2,1)} %get-tuple-element.141.refs_0_.refs_1_.refs_2_, bf16[32,1024]{1,0:T(8,128)(2,1)} %bitcast.137, ...), custom_call_target="tpu_custom_call" | custom-call | flops 16777216000 | bytes 5898240 | tf_op jit(solution)/shard_map/attend_back/pallas_call | solution.py:180
  380.9 10.2 %collective-permute-done.45 = bf16[512,1280]{1,0:T(8,128)(2,1)S(1)} collective-permute-done((bf16[512,1280]{1,0:T(8,128)(2,1)S(1)}, bf16[512,1280]{1,0:T(8,128)(2,1)S(1)}, u32[]{:S(2)}, u32[]{:S(2)}) %collective-permute-start.45) | collective-permute-done | bytes 1310752 | tf_op jit(solution)/shard_map/ppermute | solution.py:900
  391.1 3.3 collective-permute-done.46
  397.2 7.6 %head_grad.3 = (bf16[4,160,480]{2,1,0:T(8,128)(2,1)}, bf16[4,160,480]{2,1,0:T(8,128)(2,1)}) custom-call(s32[1]{0:T(128)} %bitcast.43.x_ref, bf16[2048,1280]{1,0:T(8,128)(2,1)} %get-tuple-element.153.n_ref, bf16[480,2048]{1,0:T(8,128)(2,1)} %bitcast.168), custom_call_target="tpu_custom_call" | custom-call | flops 2516582400 | bytes 7208960 | tf_op jit(solution)/shard_map/head_grad/pallas_call | solution.py:766
  404.8 10.3 %project_back.2 = (f32[512,1280]{1,0:T(8,128)}, bf16[512,1280]{1,0:T(8,128)(2,1)}, f32[8,1280]{1,0:T(8,128)}, f32[8,960]{1,0:T(8,128)}) custom-call(bf16[1280,960]{1,0:T(8,128)(2,1)} %bitcast.156, bf16[480,2048]{1,0:T(8,128)(2,1)} %bitcast.166, bf16[480,2048]{1,0:T(8,128)(2,1)} %bitcast.169, bf16[512,1280]{1,0:T(8,128)(2,1)} %collective-permute-done.7.refs_1_.refs_2_, ...), custom_call_target="tpu_custom_call" | custom-call | flops 2516582400 | bytes 12943360 | tf_op jit(solution)/shard_map/project_back/pallas_call | solution.py:401
  416.5 10.9 %collective-permute-start.57 = (bf16[160,800]{1,0:T(8,128)(2,1)}, bf16[160,800]{1,0:T(8,128)(2,1)}, u32[]{:S(2)}, u32[]{:S(2)}) collective-permute-start(bf16[160,800]{1,0:T(8,128)(2,1)} %get-tuple-element.236), channel_id=1, source_target_pairs={{0,24},{2,26},{4,28},{6,30},{8,0},{10,2},{12,4},{14,6},{16,8},{18,... | collective-permute-start | bytes 768008 | tf_op jit(solution)/shard_map/ppermute | solution.py:897
  428.2 3.0 fusion.10
  432.1 10.2 %project_back.3 = (f32[512,1280]{1,0:T(8,128)}, bf16[512,1280]{1,0:T(8,128)(2,1)}, f32[8,1280]{1,0:T(8,128)}, f32[8,960]{1,0:T(8,128)}) custom-call(bf16[1280,960]{1,0:T(8,128)(2,1)} %bitcast.157, bf16[480,2048]{1,0:T(8,128)(2,1)} %bitcast.167, bf16[480,2048]{1,0:T(8,128)(2,1)} %bitcast.170, bf16[512,1280]{1,0:T(8,128)(2,1)} %bitcast.120, ...), custom_call_target="tpu_custom_call" | custom-call | flops 2516582400 | bytes 12943360 | tf_op jit(solution)/shard_map/project_back/pallas_call | solution.py:401
  447.0 7.9 %collective-permute-start.61 = (bf16[160,480]{1,0:T(8,128)(2,1)S(1)}, bf16[160,480]{1,0:T(8,128)(2,1)S(1)}, u32[]{:S(2)}, u32[]{:S(2)}) collective-permute-start(bf16[160,480]{1,0:T(8,128)(2,1)S(1)} %get-tuple-element.240), channel_id=1, source_target_pairs={{0,24},{2,26},{4,28},{6,30},{8,0},{10,2},{12,4},{14,6},{16,8},{18,... | collective-permute-start | bytes 460808 | tf_op jit(solution)/shard_map/ppermute | solution.py:897
  454.8 2.5 collective-permute-done.56
  459.1 2.6 collective-permute-done.51
  462.6 2.8 collective-permute-start.52
  465.4 5.9 %collective-permute-done.60 = bf16[160,480]{1,0:T(8,128)(2,1)S(1)} collective-permute-done((bf16[160,480]{1,0:T(8,128)(2,1)S(1)}, bf16[160,480]{1,0:T(8,128)(2,1)S(1)}, u32[]{:S(2)}, u32[]{:S(2)}) %collective-permute-start.60) | collective-permute-done | bytes 153632 | tf_op jit(solution)/shard_map/ppermute | solution.py:897
  474.7 8.4 %collective-permute-done.53 = f32[13,1280]{1,0:T(8,128)S(1)} collective-permute-done((f32[13,1280]{1,0:T(8,128)S(1)}, f32[13,1280]{1,0:T(8,128)S(1)}, u32[]{:S(2)}, u32[]{:S(2)}) %collective-permute-start.53) | collective-permute-done | bytes 66592 | tf_op jit(solution)/shard_map/ppermute | solution.py:1244
  485.5 2.6 finish_heads.1
  488.2 2.5 multiply_reduce_fusion
  497.6 9.1 %reduce-scatter.2.cloned.1.call-done = bf16[160,2560]{1,0:T(8,128)(2,1)} async-done(((bf16[1280,2560]{1,0:T(8,128)(2,1)}), bf16[160,2560]{1,0:T(8,128)(2,1)}) %reduce-scatter.2.cloned.1.call-update) | async-done | bytes 819216 | tf_op jit(solution)/shard_map/reduce_scatter | solution.py:1104
  512.7 17.2 %collective-permute-done.65 = bf16[320,1280]{1,0:T(8,128)(2,1)S(1)} collective-permute-done((bf16[320,1280]{1,0:T(8,128)(2,1)S(1)}, bf16[320,1280]{1,0:T(8,128)(2,1)S(1)}, u32[]{:S(2)}, u32[]{:S(2)}) %collective-permute-start.65) | collective-permute-done | bytes 819232 | tf_op jit(solution)/shard_map/ppermute | solution.py:900
  530.8 3.5 finish_feed.1
  (326 shorter events, 103.0 us)
Async XLA Ops:
  7.2 134.0 %all-gather.4.cloned.1.call-start = ((), (), s32[]{:S(2)}) async-start(), calls=%async_computation.1 | async-start | bytes 1843200 | tf_op jit(solution)/shard_map/all_gather | solution.py:945
  16.3 178.1 %all-gather.6.cloned.1.call-start = ((), (), s32[]{:S(2)}) async-start(), calls=%async_computation.3 | async-start | bytes 7372800 | tf_op jit(solution)/shard_map/all_gather | solution.py:945
  16.7 9.5 %collective-permute-start.25 = (bf16[80,1280]{1,0:T(8,128)(2,1)}, bf16[80,1280]{1,0:T(8,128)(2,1)}, u32[]{:S(2)}, u32[]{:S(2)}) collective-permute-start(bf16[80,1280]{1,0:T(8,128)(2,1)} %get-tuple-element.149), channel_id=1, source_target_pairs={{0,2},{2,0},{4,6},{6,4},{8,10},{10,8},{12,14},{14,12},{16,18},{18,... | collective-permute-start | bytes 614408 | tf_op jit(solution)/shard_map/ppermute | solution.py:891
  19.3 17.5 %collective-permute-start.4 = (bf16[192,960]{1,0:T(8,128)(2,1)S(1)}, bf16[192,960]{1,0:T(8,128)(2,1)S(1)}, u32[]{:S(2)}, u32[]{:S(2)}) collective-permute-start(bf16[192,960]{1,0:T(8,128)(2,1)S(1)} %maximum_select_fusion.2.refs_0_), channel_id=1, source_target_pairs={{0,8},{2,10},{4,12},{6,14},{8,16},{10,18},{12,20},{14,22},{16,24},... | collective-permute-start | bytes 1105928 | tf_op jit(solution)/shard_map/ppermute | solution.py:897
  22.3 35.0 %collective-permute-start.6 = (bf16[192,960]{1,0:T(8,128)(2,1)S(1)}, bf16[192,960]{1,0:T(8,128)(2,1)S(1)}, u32[]{:S(2)}, u32[]{:S(2)}) collective-permute-start(bf16[192,960]{1,0:T(8,128)(2,1)S(1)} %maximum_select_fusion.2.refs_0_), channel_id=1, source_target_pairs={{0,16},{2,18},{4,20},{6,22},{8,24},{10,26},{12,28},{14,30},{16,0},... | collective-permute-start | bytes 1105928 | tf_op jit(solution)/shard_map/ppermute | solution.py:897
  24.8 32.4 %collective-permute-start.9 = (bf16[192,960]{1,0:T(8,128)(2,1)S(1)}, bf16[192,960]{1,0:T(8,128)(2,1)S(1)}, u32[]{:S(2)}, u32[]{:S(2)}) collective-permute-start(bf16[192,960]{1,0:T(8,128)(2,1)S(1)} %maximum_select_fusion.2.refs_0_), channel_id=1, source_target_pairs={{0,24},{2,26},{4,28},{6,30},{8,0},{10,2},{12,4},{14,6},{16,8},{18,... | collective-permute-start | bytes 1105928 | tf_op jit(solution)/shard_map/ppermute | solution.py:897
  57.3 449.4 %reduce-scatter.2.cloned.1.call-start = ((), (), s32[]{:S(2)}) async-start(), calls=%async_computation.2 | async-start | bytes 7372800 | tf_op jit(solution)/shard_map/reduce_scatter | solution.py:1104
  57.4 30.8 %collective-permute-start.7 = (bf16[512,1280]{1,0:T(8,128)(2,1)S(1)}, bf16[512,1280]{1,0:T(8,128)(2,1)}, u32[]{:S(2)}, u32[]{:S(2)}) collective-permute-start(bf16[512,1280]{1,0:T(8,128)(2,1)S(1)} %bitcast.121), channel_id=1, source_target_pairs={{0,1},{1,0},{2,3},{3,2},{4,5},{5,4},{6,7},{7,6},{8,9},{9,8},{10,11... | collective-permute-start | bytes 3932168 | tf_op jit(solution)/shard_map/ppermute | solution.py:900
  59.0 32.7 %collective-permute-start.3 = (bf16[192,960]{1,0:T(8,128)(2,1)S(1)}, bf16[192,960]{1,0:T(8,128)(2,1)S(1)}, u32[]{:S(2)}, u32[]{:S(2)}) collective-permute-start(bf16[192,960]{1,0:T(8,128)(2,1)S(1)} %maximum_select_fusion.2.refs_0_), channel_id=1, source_target_pairs={{0,4},{2,6},{4,0},{6,2},{8,12},{10,14},{12,8},{14,10},{16,20},{18,... | collective-permute-start | bytes 1105928 | tf_op jit(solution)/shard_map/ppermute | solution.py:894
  60.5 31.2 %collective-permute-start.5 = (bf16[192,960]{1,0:T(8,128)(2,1)S(1)}, bf16[192,960]{1,0:T(8,128)(2,1)S(1)}, u32[]{:S(2)}, u32[]{:S(2)}) collective-permute-start(bf16[192,960]{1,0:T(8,128)(2,1)S(1)} %collective-permute-done.4.refs_2_), channel_id=1, source_target_pairs={{0,4},{2,6},{4,0},{6,2},{8,12},{10,14},{12,8},{14,10},{16,20},{18,... | collective-permute-start | bytes 1105928 | tf_op jit(solution)/shard_map/ppermute | solution.py:894
  61.0 35.6 %collective-permute-start.10 = (bf16[192,960]{1,0:T(8,128)(2,1)S(1)}, bf16[192,960]{1,0:T(8,128)(2,1)S(1)}, u32[]{:S(2)}, u32[]{:S(2)}) collective-permute-start(bf16[192,960]{1,0:T(8,128)(2,1)S(1)} %collective-permute-done.9.refs_6_), channel_id=1, source_target_pairs={{0,4},{2,6},{4,0},{6,2},{8,12},{10,14},{12,8},{14,10},{16,20},{18,... | collective-permute-start | bytes 1105928 | tf_op jit(solution)/shard_map/ppermute | solution.py:894
  88.2 18.1 %collective-permute-start.8 = (bf16[192,960]{1,0:T(8,128)(2,1)S(1)}, bf16[192,960]{1,0:T(8,128)(2,1)S(1)}, u32[]{:S(2)}, u32[]{:S(2)}) collective-permute-start(bf16[192,960]{1,0:T(8,128)(2,1)S(1)} %collective-permute-done.6.refs_4_), channel_id=1, source_target_pairs={{0,4},{2,6},{4,0},{6,2},{8,12},{10,14},{12,8},{14,10},{16,20},{18,... | collective-permute-start | bytes 1105928 | tf_op jit(solution)/shard_map/ppermute | solution.py:894
  108.5 31.4 %collective-permute-start.15 = (bf16[512,1280]{1,0:T(8,128)(2,1)S(1)}, bf16[512,1280]{1,0:T(8,128)(2,1)}, u32[]{:S(2)}, u32[]{:S(2)}) collective-permute-start(bf16[512,1280]{1,0:T(8,128)(2,1)S(1)} %bitcast_select_fusion.refs_4_.refs_5_.refs_3_.live_ref), channel_id=1, source_target_pairs={{0,1},{1,0},{2,3},{3,2},{4,5},{5,4},{6,7},{7,6},{8,9},{9,8},{10,11... | collective-permute-start | bytes 3932168 | tf_op jit(solution)/shard_map/ppermute | solution.py:900
  127.4 25.3 %collective-permute-start.14 = (bf16[512,1280]{1,0:T(8,128)(2,1)S(1)}, bf16[512,1280]{1,0:T(8,128)(2,1)S(1)}, u32[]{:S(2)}, u32[]{:S(2)}) collective-permute-start(bf16[512,1280]{1,0:T(8,128)(2,1)S(1)} %bitcast_select_fusion.refs_4_.refs_5_.refs_3_.live_ref), channel_id=1, source_target_pairs={{0,2},{2,0},{4,6},{6,4},{8,10},{10,8},{12,14},{14,12},{16,18},{18,... | collective-permute-start | bytes 3932168 | tf_op jit(solution)/shard_map/ppermute | solution.py:891
  139.9 12.8 %collective-permute-start.16 = (bf16[512,1280]{1,0:T(8,128)(2,1)}, bf16[512,1280]{1,0:T(8,128)(2,1)}, u32[]{:S(2)}, u32[]{:S(2)}) collective-permute-start(bf16[512,1280]{1,0:T(8,128)(2,1)} %collective-permute-done.15.refs_2_.refs_7_.refs_9_), channel_id=1, source_target_pairs={{0,2},{2,0},{4,6},{6,4},{8,10},{10,8},{12,14},{14,12},{16,18},{18,... | collective-permute-start | bytes 3932168 | tf_op jit(solution)/shard_map/ppermute | solution.py:891
  141.2 32.1 %collective-permute-start.1 = (bf16[1280,640]{1,0:T(8,128)(2,1)}, bf16[1280,640]{1,0:T(8,128)(2,1)S(1)}, u32[]{:S(2)}, u32[]{:S(2)}) collective-permute-start(bf16[1280,640]{1,0:T(8,128)(2,1)} %bitcast.128), channel_id=1, source_target_pairs={{0,2},{2,0},{4,6},{6,4},{8,10},{10,8},{12,14},{14,12},{16,18},{18,... | collective-permute-start | bytes 4915208 | tf_op jit(solution)/shard_map/ppermute | solution.py:891
  150.7 13.3 %collective-permute-start.17 = (bf16[2,160,512]{2,1,0:T(8,128)(2,1)}, bf16[2,160,512]{2,1,0:T(8,128)(2,1)S(1)}, u32[]{:S(2)}, u32[]{:S(2)}) collective-permute-start(bf16[2,160,512]{2,1,0:T(8,128)(2,1)} %bitcast.158), channel_id=1, source_target_pairs={{0,1},{1,0},{2,3},{3,2},{4,5},{5,4},{6,7},{7,6},{8,9},{9,8},{10,11... | collective-permute-start | bytes 983048 | tf_op jit(solution)/shard_map/ppermute | solution.py:900
  152.7 23.2 %collective-permute-start.19 = (bf16[1,160,512]{2,1,0:T(8,128)(2,1)S(1)}, bf16[1,160,512]{2,1,0:T(8,128)(2,1)S(1)}, u32[]{:S(2)}, u32[]{:S(2)}) collective-permute-start(bf16[1,160,512]{2,1,0:T(8,128)(2,1)S(1)} %get-tuple-element.258), channel_id=1, source_target_pairs={{0,2},{2,0},{4,6},{6,4},{8,10},{10,8},{12,14},{14,12},{16,18},{18,... | collective-permute-start | bytes 491528 | tf_op jit(solution)/shard_map/ppermute | solution.py:891
  162.2 10.4 %collective-permute-start.18 = (bf16[2,160,512]{2,1,0:T(8,128)(2,1)}, bf16[2,160,512]{2,1,0:T(8,128)(2,1)S(1)}, u32[]{:S(2)}, u32[]{:S(2)}) collective-permute-start(bf16[2,160,512]{2,1,0:T(8,128)(2,1)} %bitcast.159), channel_id=1, source_target_pairs={{0,1},{1,0},{2,3},{3,2},{4,5},{5,4},{6,7},{7,6},{8,9},{9,8},{10,11... | collective-permute-start | bytes 983048 | tf_op jit(solution)/shard_map/ppermute | solution.py:900
  164.7 11.2 %collective-permute-start.21 = (bf16[1,160,512]{2,1,0:T(8,128)(2,1)S(1)}, bf16[1,160,512]{2,1,0:T(8,128)(2,1)S(1)}, u32[]{:S(2)}, u32[]{:S(2)}) collective-permute-start(bf16[1,160,512]{2,1,0:T(8,128)(2,1)S(1)} %get-tuple-element.254), channel_id=1, source_target_pairs={{0,2},{2,0},{4,6},{6,4},{8,10},{10,8},{12,14},{14,12},{16,18},{18,... | collective-permute-start | bytes 491528 | tf_op jit(solution)/shard_map/ppermute | solution.py:891
  166.6 9.3 %collective-permute-start.20 = (bf16[1,160,512]{2,1,0:T(8,128)(2,1)S(1)}, bf16[1,160,512]{2,1,0:T(8,128)(2,1)S(1)}, u32[]{:S(2)}, u32[]{:S(2)}) collective-permute-start(bf16[1,160,512]{2,1,0:T(8,128)(2,1)S(1)} %get-tuple-element.256), channel_id=1, source_target_pairs={{0,2},{2,0},{4,6},{6,4},{8,10},{10,8},{12,14},{14,12},{16,18},{18,... | collective-permute-start | bytes 491528 | tf_op jit(solution)/shard_map/ppermute | solution.py:891
  185.4 30.7 %collective-permute-start.27 = (bf16[256,1280]{1,0:T(8,128)(2,1)}, bf16[256,1280]{1,0:T(8,128)(2,1)S(1)}, u32[]{:S(2)}, u32[]{:S(2)}) collective-permute-start(bf16[256,1280]{1,0:T(8,128)(2,1)} %get-tuple-element.169.refs_0_), channel_id=1, source_target_pairs={{0,1},{1,0},{2,3},{3,2},{4,5},{5,4},{6,7},{7,6},{8,9},{9,8},{10,11... | collective-permute-start | bytes 1966088 | tf_op jit(solution)/shard_map/ppermute | solution.py:900
  187.2 29.7 %collective-permute-start.28 = (bf16[256,1280]{1,0:T(8,128)(2,1)}, bf16[256,1280]{1,0:T(8,128)(2,1)}, u32[]{:S(2)}, u32[]{:S(2)}) collective-permute-start(bf16[256,1280]{1,0:T(8,128)(2,1)} %get-tuple-element.147.refs_1_), channel_id=1, source_target_pairs={{0,1},{1,0},{2,3},{3,2},{4,5},{5,4},{6,7},{7,6},{8,9},{9,8},{10,11... | collective-permute-start | bytes 1966088 | tf_op jit(solution)/shard_map/ppermute | solution.py:900
  231.9 18.8 %collective-permute-start.26 = (bf16[512,1280]{1,0:T(8,128)(2,1)}, bf16[512,1280]{1,0:T(8,128)(2,1)S(1)}, u32[]{:S(2)}, u32[]{:S(2)}) collective-permute-start(bf16[512,1280]{1,0:T(8,128)(2,1)} %get-tuple-element.156), channel_id=1, source_target_pairs={{0,2},{2,0},{4,6},{6,4},{8,10},{10,8},{12,14},{14,12},{16,18},{18,... | collective-permute-start | bytes 3932168 | tf_op jit(solution)/shard_map/ppermute | solution.py:891
  235.5 46.0 %collective-permute-start.33 = (bf16[256,1280]{1,0:T(8,128)(2,1)S(1)}, bf16[256,1280]{1,0:T(8,128)(2,1)S(1)}, u32[]{:S(2)}, u32[]{:S(2)}) collective-permute-start(bf16[256,1280]{1,0:T(8,128)(2,1)S(1)} %add_convert_fusion.5), channel_id=1, source_target_pairs={{0,1},{1,0},{2,3},{3,2},{4,5},{5,4},{6,7},{7,6},{8,9},{9,8},{10,11... | collective-permute-start | bytes 1966088 | tf_op jit(solution)/shard_map/ppermute | solution.py:900
  253.2 28.4 %collective-permute-start.34 = (bf16[256,1280]{1,0:T(8,128)(2,1)S(1)}, bf16[256,1280]{1,0:T(8,128)(2,1)S(1)}, u32[]{:S(2)}, u32[]{:S(2)}) collective-permute-start(bf16[256,1280]{1,0:T(8,128)(2,1)S(1)} %add_convert_fusion.4), channel_id=1, source_target_pairs={{0,1},{1,0},{2,3},{3,2},{4,5},{5,4},{6,7},{7,6},{8,9},{9,8},{10,11... | collective-permute-start | bytes 1966088 | tf_op jit(solution)/shard_map/ppermute | solution.py:900
  299.0 17.9 %collective-permute-start.35 = (bf16[1280,640]{1,0:T(8,128)(2,1)}, bf16[1280,640]{1,0:T(8,128)(2,1)S(1)}, u32[]{:S(2)}, u32[]{:S(2)}) collective-permute-start(bf16[1280,640]{1,0:T(8,128)(2,1)} %get-tuple-element.178), channel_id=1, source_target_pairs={{0,2},{2,0},{4,6},{6,4},{8,10},{10,8},{12,14},{14,12},{16,18},{18,... | collective-permute-start | bytes 4915208 | tf_op jit(solution)/shard_map/ppermute | solution.py:891
  299.0 10.8 %collective-permute-start.36 = (bf16[2,160,512]{2,1,0:T(8,128)(2,1)}, bf16[2,160,512]{2,1,0:T(8,128)(2,1)}, u32[]{:S(2)}, u32[]{:S(2)}) collective-permute-start(bf16[2,160,512]{2,1,0:T(8,128)(2,1)} %get-tuple-element.180), channel_id=1, source_target_pairs={{0,1},{1,0},{2,3},{3,2},{4,5},{5,4},{6,7},{7,6},{8,9},{9,8},{10,11... | collective-permute-start | bytes 983048 | tf_op jit(solution)/shard_map/ppermute | solution.py:900
  299.8 16.6 %collective-permute-start.38 = (bf16[2,160,512]{2,1,0:T(8,128)(2,1)}, bf16[2,160,512]{2,1,0:T(8,128)(2,1)S(1)}, u32[]{:S(2)}, u32[]{:S(2)}) collective-permute-start(bf16[2,160,512]{2,1,0:T(8,128)(2,1)} %get-tuple-element.181), channel_id=1, source_target_pairs={{0,1},{1,0},{2,3},{3,2},{4,5},{5,4},{6,7},{7,6},{8,9},{9,8},{10,11... | collective-permute-start | bytes 983048 | tf_op jit(solution)/shard_map/ppermute | solution.py:900
  301.3 23.4 %collective-permute-start.40 = (bf16[320,512]{1,0:T(8,128)(2,1)}, bf16[320,512]{1,0:T(8,128)(2,1)}, u32[]{:S(2)}, u32[]{:S(2)}) collective-permute-start(bf16[320,512]{1,0:T(8,128)(2,1)} %get-tuple-element.183), channel_id=1, source_target_pairs={{0,2},{2,0},{4,6},{6,4},{8,10},{10,8},{12,14},{14,12},{16,18},{18,... | collective-permute-start | bytes 983048 | tf_op jit(solution)/shard_map/ppermute | solution.py:891
  309.9 14.1 %collective-permute-start.37 = (bf16[2,160,512]{2,1,0:T(8,128)(2,1)}, bf16[2,160,512]{2,1,0:T(8,128)(2,1)}, u32[]{:S(2)}, u32[]{:S(2)}) collective-permute-start(bf16[2,160,512]{2,1,0:T(8,128)(2,1)} %collective-permute-done.36.refs_6_), channel_id=1, source_target_pairs={{0,2},{2,0},{4,6},{6,4},{8,10},{10,8},{12,14},{14,12},{16,18},{18,... | collective-permute-start | bytes 983048 | tf_op jit(solution)/shard_map/ppermute | solution.py:891
  324.0 20.7 %collective-permute-start.41 = (bf16[1280,320]{0,1:T(8,128)(2,1)S(1)}, bf16[1280,320]{0,1:T(8,128)(2,1)S(1)}, u32[]{:S(2)}, u32[]{:S(2)}) collective-permute-start(bf16[1280,320]{0,1:T(8,128)(2,1)S(1)} %copy.45), channel_id=1, source_target_pairs={{0,1},{1,0},{2,3},{3,2},{4,5},{5,4},{6,7},{7,6},{8,9},{9,8},{10,11... | collective-permute-start | bytes 2457608 | tf_op jit(solution)/shard_map/ppermute | solution.py:900
  358.1 36.3 %collective-permute-start.46 = (bf16[4,160,800]{2,1,0:T(8,128)(2,1)}, bf16[4,160,800]{2,1,0:T(8,128)(2,1)}, u32[]{:S(2)}, u32[]{:S(2)}) collective-permute-start(bf16[4,160,800]{2,1,0:T(8,128)(2,1)} %get-tuple-element.185), channel_id=1, source_target_pairs={{0,4},{2,6},{4,0},{6,2},{8,12},{10,14},{12,8},{14,10},{16,20},{18,... | collective-permute-start | bytes 3072008 | tf_op jit(solution)/shard_map/ppermute | solution.py:894
  359.8 31.2 %collective-permute-start.45 = (bf16[512,1280]{1,0:T(8,128)(2,1)S(1)}, bf16[512,1280]{1,0:T(8,128)(2,1)S(1)}, u32[]{:S(2)}, u32[]{:S(2)}) collective-permute-start(bf16[512,1280]{1,0:T(8,128)(2,1)S(1)} %pad_maximum_fusion), channel_id=1, source_target_pairs={{0,1},{1,0},{2,3},{3,2},{4,5},{5,4},{6,7},{7,6},{8,9},{9,8},{10,11... | collective-permute-start | bytes 3932168 | tf_op jit(solution)/shard_map/ppermute | solution.py:900
  415.0 16.1 %collective-permute-start.47 = (bf16[512,1280]{1,0:T(8,128)(2,1)}, bf16[512,1280]{1,0:T(8,128)(2,1)S(1)}, u32[]{:S(2)}, u32[]{:S(2)}) collective-permute-start(bf16[512,1280]{1,0:T(8,128)(2,1)} %get-tuple-element.203), channel_id=1, source_target_pairs={{0,2},{2,0},{4,6},{6,4},{8,10},{10,8},{12,14},{14,12},{16,18},{18,... | collective-permute-start | bytes 3932168 | tf_op jit(solution)/shard_map/ppermute | solution.py:891
  415.1 29.5 %collective-permute-start.58 = (bf16[4,160,480]{2,1,0:T(8,128)(2,1)}, bf16[4,160,480]{2,1,0:T(8,128)(2,1)}, u32[]{:S(2)}, u32[]{:S(2)}) collective-permute-start(bf16[4,160,480]{2,1,0:T(8,128)(2,1)} %get-tuple-element.196), channel_id=1, source_target_pairs={{0,4},{2,6},{4,0},{6,2},{8,12},{10,14},{12,8},{14,10},{16,20},{18,... | collective-permute-start | bytes 1843208 | tf_op jit(solution)/shard_map/ppermute | solution.py:894
  416.5 30.5 %collective-permute-start.57 = (bf16[160,800]{1,0:T(8,128)(2,1)}, bf16[160,800]{1,0:T(8,128)(2,1)}, u32[]{:S(2)}, u32[]{:S(2)}) collective-permute-start(bf16[160,800]{1,0:T(8,128)(2,1)} %get-tuple-element.236), channel_id=1, source_target_pairs={{0,24},{2,26},{4,28},{6,30},{8,0},{10,2},{12,4},{14,6},{16,8},{18,... | collective-permute-start | bytes 768008 | tf_op jit(solution)/shard_map/ppermute | solution.py:897
  427.5 29.9 %collective-permute-start.56 = (bf16[160,800]{1,0:T(8,128)(2,1)}, bf16[160,800]{1,0:T(8,128)(2,1)}, u32[]{:S(2)}, u32[]{:S(2)}) collective-permute-start(bf16[160,800]{1,0:T(8,128)(2,1)} %get-tuple-element.237), channel_id=1, source_target_pairs={{0,16},{2,18},{4,20},{6,22},{8,24},{10,26},{12,28},{14,30},{16,0},... | collective-permute-start | bytes 768008 | tf_op jit(solution)/shard_map/ppermute | solution.py:897
  427.5 29.9 %collective-permute-start.55 = (bf16[160,800]{1,0:T(8,128)(2,1)}, bf16[160,800]{1,0:T(8,128)(2,1)}, u32[]{:S(2)}, u32[]{:S(2)}) collective-permute-start(bf16[160,800]{1,0:T(8,128)(2,1)} %get-tuple-element.238), channel_id=1, source_target_pairs={{0,8},{2,10},{4,12},{6,14},{8,16},{10,18},{12,20},{14,22},{16,24},... | collective-permute-start | bytes 768008 | tf_op jit(solution)/shard_map/ppermute | solution.py:897
  431.4 56.7 %collective-permute-start.49 = (bf16[512,1280]{1,0:T(8,128)(2,1)S(1)}, bf16[512,1280]{1,0:T(8,128)(2,1)S(1)}, u32[]{:S(2)}, u32[]{:S(2)}) collective-permute-start(bf16[512,1280]{1,0:T(8,128)(2,1)S(1)} %add_convert_fusion), channel_id=1, source_target_pairs={{0,1},{1,0},{2,3},{3,2},{4,5},{5,4},{6,7},{7,6},{8,9},{9,8},{10,11... | collective-permute-start | bytes 3932168 | tf_op jit(solution)/shard_map/ppermute | solution.py:900
  446.3 41.8 %collective-permute-start.48 = (bf16[512,1280]{1,0:T(8,128)(2,1)}, bf16[512,1280]{1,0:T(8,128)(2,1)}, u32[]{:S(2)}, u32[]{:S(2)}) collective-permute-start(bf16[512,1280]{1,0:T(8,128)(2,1)} %get-tuple-element.206), channel_id=1, source_target_pairs={{0,2},{2,0},{4,6},{6,4},{8,10},{10,8},{12,14},{14,12},{16,18},{18,... | collective-permute-start | bytes 3932168 | tf_op jit(solution)/shard_map/ppermute | solution.py:891
  447.0 15.6 %collective-permute-start.61 = (bf16[160,480]{1,0:T(8,128)(2,1)S(1)}, bf16[160,480]{1,0:T(8,128)(2,1)S(1)}, u32[]{:S(2)}, u32[]{:S(2)}) collective-permute-start(bf16[160,480]{1,0:T(8,128)(2,1)S(1)} %get-tuple-element.240), channel_id=1, source_target_pairs={{0,24},{2,26},{4,28},{6,30},{8,0},{10,2},{12,4},{14,6},{16,8},{18,... | collective-permute-start | bytes 460808 | tf_op jit(solution)/shard_map/ppermute | solution.py:897
  457.3 14.0 %collective-permute-start.60 = (bf16[160,480]{1,0:T(8,128)(2,1)S(1)}, bf16[160,480]{1,0:T(8,128)(2,1)S(1)}, u32[]{:S(2)}, u32[]{:S(2)}) collective-permute-start(bf16[160,480]{1,0:T(8,128)(2,1)S(1)} %get-tuple-element.241), channel_id=1, source_target_pairs={{0,16},{2,18},{4,20},{6,22},{8,24},{10,26},{12,28},{14,30},{16,0},... | collective-permute-start | bytes 460808 | tf_op jit(solution)/shard_map/ppermute | solution.py:897
  461.8 9.5 %collective-permute-start.59 = (bf16[160,480]{1,0:T(8,128)(2,1)S(1)}, bf16[160,480]{1,0:T(8,128)(2,1)S(1)}, u32[]{:S(2)}, u32[]{:S(2)}) collective-permute-start(bf16[160,480]{1,0:T(8,128)(2,1)S(1)} %get-tuple-element.239), channel_id=1, source_target_pairs={{0,8},{2,10},{4,12},{6,14},{8,16},{10,18},{12,20},{14,22},{16,24},... | collective-permute-start | bytes 460808 | tf_op jit(solution)/shard_map/ppermute | solution.py:897
  462.6 10.4 %collective-permute-start.52 = (f32[13,1280]{1,0:T(8,128)S(1)}, f32[13,1280]{1,0:T(8,128)S(1)}, u32[]{:S(2)}, u32[]{:S(2)}) collective-permute-start(f32[13,1280]{1,0:T(8,128)S(1)} %maximum_select_fusion.7), channel_id=1, source_target_pairs={{0,8},{2,10},{4,12},{6,14},{8,0},{10,2},{12,4},{14,6},{16,24},{18,... | collective-permute-start | bytes 199688 | tf_op jit(solution)/shard_map/ppermute | solution.py:1244
  473.0 10.1 %collective-permute-start.53 = (f32[13,1280]{1,0:T(8,128)S(1)}, f32[13,1280]{1,0:T(8,128)S(1)}, u32[]{:S(2)}, u32[]{:S(2)}) collective-permute-start(f32[13,1280]{1,0:T(8,128)S(1)} %maximum_select_fusion.6), channel_id=1, source_target_pairs={{0,16},{2,18},{4,20},{6,22},{8,24},{10,26},{12,28},{14,30},{16,0},... | collective-permute-start | bytes 199688 | tf_op jit(solution)/shard_map/ppermute | solution.py:1244
  473.2 11.6 %collective-permute-start.63 = (bf16[2,80,1280]{2,1,0:T(8,128)(2,1)S(1)}, bf16[2,80,1280]{2,1,0:T(8,128)(2,1)S(1)}, u32[]{:S(2)}, u32[]{:S(2)}) collective-permute-start(bf16[2,80,1280]{2,1,0:T(8,128)(2,1)S(1)} %pad_maximum_fusion.4.refs_0_), channel_id=1, source_target_pairs={{0,1},{1,0},{2,3},{3,2},{4,5},{5,4},{6,7},{7,6},{8,9},{9,8},{10,11... | collective-permute-start | bytes 1228808 | tf_op jit(solution)/shard_map/ppermute | solution.py:900
  509.5 20.4 %collective-permute-start.65 = (bf16[320,1280]{1,0:T(8,128)(2,1)S(1)}, bf16[320,1280]{1,0:T(8,128)(2,1)S(1)}, u32[]{:S(2)}, u32[]{:S(2)}) collective-permute-start(bf16[320,1280]{1,0:T(8,128)(2,1)S(1)} %pad_maximum_fusion.2), channel_id=1, source_target_pairs={{0,1},{1,0},{2,3},{3,2},{4,5},{5,4},{6,7},{7,6},{8,9},{9,8},{10,11... | collective-permute-start | bytes 2457608 | tf_op jit(solution)/shard_map/ppermute | solution.py:900
  (71 other events, 708.8 us)
Sparse Core Ops, SparseCore 0:
  16.4 73.5 all-gather.3
  92.8 101.5 all-gather.5
  357.6 149.0 reduce-scatter.1

commit v3 on v2

--- a/solution.py
+++ b/solution.py
@@ -50,6 +50,12 @@
 
 def tie(value, *after):
     return lax.optimization_barrier((value,) + after)[0]
+
+
+def cost(flops, bytes_accessed, transcendentals):
+    return pl.CostEstimate(
+        flops=flops // 4, bytes_accessed=bytes_accessed // 4, transcendentals=transcendentals // 4
+    )
 
 
 def params(**more):
@@ -191,7 +197,7 @@
             pltpu.VMEM((HEAD_DIM, frames), bf16),
         ],
         compiler_params=params(),
-        cost_estimate=pl.CostEstimate(
+        cost_estimate=cost(
             flops=clips * heads * frames * frames * 4000,
             bytes_accessed=qkv.size * 6 // halves,
             transcendentals=clips * heads * frames * frames,
@@ -273,7 +279,7 @@
         out_shape=shapes,
         scratch_shapes=[pltpu.VMEM((count * rows, width), bf16)] * 2,
         compiler_params=params(),
-        cost_estimate=pl.CostEstimate(
+        cost_estimate=cost(
             flops=8 * count * rows * width * hidden,
             bytes_accessed=4 * width * hidden + 16 * count * rows * width,
             transcendentals=count * rows * hidden,
@@ -420,7 +426,7 @@
         ],
         scratch_shapes=[pltpu.VMEM((rows, width), bf16)],
         compiler_params=params(),
-        cost_estimate=pl.CostEstimate(
+        cost_estimate=cost(
             flops=2 * count * rows * width * features,
             bytes_accessed=2 * width * features + 8 * count * rows * width,
             transcendentals=count * rows,
@@ -669,7 +675,7 @@
         + [sds((2, hs, tokens), bf16)] * fars_count
         + [sds((slab, tokens), bf16)] * 2,
         compiler_params=params(),
-        cost_estimate=pl.CostEstimate(
+        cost_estimate=cost(
             flops=2 * tokens * width * width, bytes_accessed=2 * width * width + 16 * tokens * width, transcendentals=tokens
         ),
         name="turn",
@@ -690,7 +696,7 @@
                 sent[z] = value[other : other + rows, :]
 
 
-def weight_grad(lefts, rights, wide=1, into=None):
+def weight_grad(x_at, lefts, rights, depth):
     rows = lefts[0][0].shape[1]
     cols = rights[0][0].shape[1]
     tile = 256 if cols % 256 == 0 else cols
@@ -701,10 +707,11 @@
 
     left_ends, right_ends = ends_of(lefts), ends_of(rights)
     tokens = left_ends[-1]
-
-    def kernel(*refs):
+    share = rows // (2 * depth)
+
+    def kernel(x_ref, *refs):
         left_refs, right_refs = refs[:count], refs[count : count + right_count]
-        out_ref, turned, joined = refs[-3:]
+        kept, sent, turned, joined = refs[-4:]
 
         @pl.when(pl.program_id(0) == 0)
         def _():
@@ -713,25 +720,23 @@
 
         for i in range(right_count):
             joined[right_ends[i] : right_ends[i + 1], :] = right_refs[i][...]
-        out_ref[...] = nn(turned[...], joined[...]).astype(bf16)
+        part_ways(x_ref, nn(turned[...], joined[...]).astype(bf16), kept, sent)
 
     whole = [pl.BlockSpec((size, rows), lambda i, at=at: (at, 0)) for _, at, size in lefts]
     strips = [pl.BlockSpec((size, tile), lambda i, at=at: (at, i)) for _, at, size in rights]
-    shift = 0 if into is None else cols // tile
     return pl.pallas_call(
         kernel,
         grid=(cols // tile,),
-        in_specs=whole + strips + ([] if into is None else [pl.BlockSpec(memory_space=pl.ANY)]),
-        out_specs=pl.BlockSpec((rows, tile), lambda i: (0, i + shift)),
-        out_shape=sds((rows, wide * cols), bf16),
-        input_output_aliases={} if into is None else {count + right_count: 0},
+        in_specs=[smem()] + whole + strips,
+        out_specs=[pl.BlockSpec((depth, share, tile), lambda i: (0, 0, i))] * 2,
+        out_shape=[sds((depth, share, cols), bf16)] * 2,
         scratch_shapes=[pltpu.VMEM((rows, tokens), bf16), pltpu.VMEM((tokens, tile), bf16)],
         compiler_params=params(),
-        cost_estimate=pl.CostEstimate(
+        cost_estimate=cost(
             flops=2 * tokens * rows * cols, bytes_accessed=2 * (tokens * (rows + cols) + rows * cols), transcendentals=0
         ),
         name="weight_grad",
-    )(*[v for v, _, _ in lefts + rights], *([] if into is None else [into]))
+    )(x_at, *[v for v, _, _ in lefts + rights])
 
 
 def head_grad(x_at, normed, grad_heads, depth, extra=()):
@@ -776,7 +781,7 @@
         out_shape=[sds((depth, share, cols), bf16)] * 2,
         scratch_shapes=[pltpu.VMEM((features, width), f32)],
         compiler_params=params(),
-        cost_estimate=pl.CostEstimate(
+        cost_estimate=cost(
             flops=2 * tokens * width * features, bytes_accessed=2 * tokens * (width + features), transcendentals=0
         ),
         name="head_grad",
@@ -803,7 +808,7 @@
         out_specs=vmem(2),
         out_shape=[sds((rows, half), bf16)] * 2,
         compiler_params=params(),
-        cost_estimate=pl.CostEstimate(
+        cost_estimate=cost(
             flops=2 * rows * tokens * width, bytes_accessed=4 * rows * width, transcendentals=0
         ),
         name="out_grad_halves",
@@ -830,7 +835,7 @@
         out_specs=vmem(groups),
         out_shape=[sds((rows, slab), bf16)] * groups,
         compiler_params=params(),
-        cost_estimate=pl.CostEstimate(flops=0, bytes_accessed=6 * rows * half, transcendentals=0),
+        cost_estimate=cost(flops=0, bytes_accessed=6 * rows * half, transcendentals=0),
         name="out_grad_parts",
     )(seq_at, kept, came)
 
@@ -1100,25 +1105,15 @@
     lefts = with_sizes(parts_of(normed2_near + sum(normed2_far, [])))
     lefts[0] = (tie(lefts[0][0], grad2_near, *grad2_sent[-1]),) + lefts[0][1:]
 
-    def over_chips_sum(v):
-        return lax.psum_scatter(v, "fsdp", scatter_dimension=0, axis_index_groups=same_core, tiled=True)
-
     rights = wholes([back_near] + back_far)
-    acts, cotangents = wholes([act_near] + act_far), with_sizes(grad_near + sum(grad_far, []))
-    if rank_hidden == width:
-        feed_sum = weight_grad(acts, cotangents, 2, weight_grad(lefts, rights, 2))
-        feed_shard = over_chips_sum(feed_sum)
-        up_shard, down_shard = feed_shard[:, :width], feed_shard[:, width:]
-    else:
-        feed_sum = weight_grad(acts, cotangents)
-        up_shard, down_shard = over_chips_sum(weight_grad(lefts, rights)), over_chips_sum(feed_sum)
+    up_kept, up_sent = weight_grad(x_at, lefts, rights, depth)
 
     targets = [
         (core ^ flip) * groups + (seq + step) % groups for flip in range(2) for step in range(groups)
     ]
     targets = jnp.stack(targets).astype(jnp.int32)
     grad_after1, grad_attn, sums2, grad_sent, heads_own, heads_other = turn(
-        targets, after1, tie(grad2_near, feed_sum), grad2_far, live_grad, lines, out_full, halves, groups
+        targets, after1, tie(grad2_near, up_sent), grad2_far, live_grad, lines, out_full, halves, groups
     )
     half_rows = heads // halves
     heads_cross = over_core(heads_other)
@@ -1136,10 +1131,13 @@
             ]
         )
 
-    out_kept, out_other_half = out_grad_halves(where[2:], mixed_own, grad_attn)
+    acts = wholes([tie(act_near, grad_attn)] + act_far)
+    down_kept, down_sent = weight_grad(x_at, acts, with_sizes(grad_near + sum(grad_far, [])), depth)
+    out_kept, out_other_half = out_grad_halves(where[2:], mixed_own, tie(grad_attn, down_sent, *sum(sides, [])))
     out_parts = out_grad_parts(seq_at, out_kept, over_core(out_other_half), groups)
     out_sent = list(out_parts[1:])
     out_came = [to_seq(v, step) for v, step in zip(out_sent, steps)]
+
     def fed_sums(after):
         both = [(mine + over_core(tie(other, after)).astype(f32)).astype(bf16) for mine, other in fed_parts]
         sent = [jnp.concatenate([v[i * part_rows : (i + 1) * part_rows] for v in both]) for i in range(len(steps))]
@@ -1150,15 +1148,16 @@
         if half:
             fed_sent, fed_near = fed_sums(x_parts[0][1])
             fed_far = [to_seq(v, step) for v, step in zip(fed_sent, steps)]
-            after = [x_parts[0][1], fed_near] + fed_sent
+            up_shard = reduce_end(tie(up_z[0], x_parts[0][1]), up_z[1])
+            down_z = reduce_z(tie(down_kept, x_parts[0][1]), down_sent)
+            after = [x_parts[0][1], up_shard, fed_near] + down_z[1] + fed_sent
         else:
-            after = out_sent + arrived
+            up_z = reduce_z(tie(up_kept, down_sent), up_sent)
+            after = up_z[1] + out_sent + arrived
         own = head_grads[half][0]
         own[0] = (tie(own[0][0], *after), own[0][1])
         grads = attend_back(qkv, mask, head_grads[half], logs[half], clips, half_heads, half, halves, groups)
         grads = grads.reshape(3 * cut, -1)
-        if half:
-            grads = tie(grads, *fed_far)
         grad_qkv.append(grads)
         x_parts.append(head_grad(x_at, normed1, grads, depth, () if half else [out_parts[0]] + out_came))
     if halves == 1:
@@ -1168,44 +1167,47 @@
     for v in fed_far:
         fed = fed + v.astype(f32)
     output = (after1 + (fed + lines[7:8])).astype(bf16).reshape(clip_count, local_frames, width)
-    kept, sent = x_parts[0]
-    z_parts = [reduce_z(tie(kept, grad_qkv[-1]), sent)]
-    feed_last = jnp.concatenate(
-        [own_of_ranks(up_shard).reshape(2 * own_rows, rank_hidden), down_shard.reshape(-1, rank_hidden)]
-    )
-    grad_qkv[-1] = tie(grad_qkv[-1], x_parts[-1][1], *z_parts[0][1])
+    if halves == 1:
+        up_shard = reduce_end(tie(up_z[0], x_parts[0][1]), up_z[1])
+        down_z = reduce_z(tie(down_kept, x_parts[0][1]), down_sent)
+    down_shard = reduce_end(tie(down_z[0], x_parts[-1][1]), down_z[1])
+    ups = along_seq(tie(own_of_ranks(up_shard), x_parts[-1][1]))
+    x_sums = [reduce_z(tie(kept, x_parts[-1][1]), sent, False) for kept, sent in x_parts[: halves - 1]]
+    grad_qkv[-1] = tie(grad_qkv[-1], x_parts[-1][1], *x_sums, *fed_far)
+
     far_own, far_other, far_sums1, far_bias = project_back(grad_qkv, qkv_full, frames_side + frames_cross, steps, groups)
     far_cross = over_core(far_other).astype(f32)
     far1 = (far_own + far_cross).astype(bf16)
     far1 = [far1[i * tokens : (i + 1) * tokens] for i in range(len(steps))]
+    kept, sent = x_parts[-1]
+    x_sums.append(reduce_z(tie(kept, far_other), sent, False))
+    heads_z = to_z(jnp.concatenate(x_sums, axis=2))
     near_own, near_other, near_sums1, near_bias = project_back(
-        [tie(grad_qkv[0], *far1)] + grad_qkv[1:], qkv_full, [frames_own, frames_near], [0], groups
-    )
-    feed_lasts = along_seq(tie(feed_last, near_other))
+        [tie(grad_qkv[0], down_shard, *far1, *heads_z[1], *ups[1:])] + grad_qkv[1:],
+        qkv_full,
+        [frames_own, frames_near],
+        [0],
+        groups,
+    )
     sums1, bias_sums = far_sums1 + near_sums1, far_bias + near_bias
-    shard_parts = [reduce_end(tie(z_parts[0][0], near_other), z_parts[0][1])]
-    x_sums = [reduce_z(tie(kept, near_other), sent, False) for kept, sent in x_parts[1:]]
-    grad_normed1 = near_own + over_core(near_other).astype(f32)
-    for v, step in zip(far1, steps):
-        grad_normed1 = grad_normed1 + to_seq(v, step).astype(f32)
+    near_cross = over_core(near_other)
+    grad_normed1 = near_own + near_cross.astype(f32)
+    far1_came = [to_seq(v, step) for v, step in zip(far1, steps)]
+    downs = along_seq(tie(down_shard.reshape(piece, width), near_other, *far1_came))
+    for v in far1_came:
+        grad_normed1 = grad_normed1 + v.astype(f32)
     plain1, scale1 = normalized(frames_own.astype(f32))
     in_grad = (grad_after1 + norm_back(plain1, scale1, grad_normed1 * lines[0:1])).astype(bf16)
 
-    for both in x_sums:
-        shard_parts.append(reduce_end(*to_z(both)))
-    heads_last = own_of_ranks(jnp.concatenate(shard_parts, axis=1))
+    heads_last = own_of_ranks(reduce_end(tie(heads_z[0], near_other), heads_z[1]))
 
     up_weight_grad, down_weight_grad = finish_feed(
         rank_at,
-        [v[: 2 * own_rows].reshape(2, own_rows, rank_hidden) for v in feed_lasts],
-        [v[2 * own_rows :].reshape(piece, width) for v in feed_lasts],
+        ups,
+        downs,
         pairs,
         groups,
     )
-    q_weight_grad, k_weight_grad, v_weight_grad, o_weight_grad = finish_heads(
-        rank_at, along_seq(heads_last), halves, groups
-    )
-
     bias_cols = bias_sums[0].reshape(halves, 3, cut)
 
     def at_rank(v):
@@ -1237,8 +1239,9 @@
     def combine(a, b):
         return jnp.where(is_sum, a + b, jnp.maximum(a, b))
 
+    stack = tie(stack, near_cross)
     stack = combine(stack, over_core(stack))
-    stack = combine(stack, over_x(stack))
+    stack = combine(tie(stack, heads_last), over_x(stack))
     step = 4
     while step < shards:
         stack = combine(stack, lax.ppermute(stack, "fsdp", [(i, i ^ step) for i in range(shards)]))
@@ -1251,6 +1254,10 @@
     small_own = lax.dynamic_slice_in_dim(stack[:8], fsdp * own_rows, own_rows, 1)
     up_bias_grad = lax.dynamic_slice_in_dim(stack[8:added].reshape(hidden), fsdp * own_hidden, own_hidden, 0)
     logit_peak = stack[added, :head_count]
+
+    q_weight_grad, k_weight_grad, v_weight_grad, o_weight_grad = finish_heads(
+        rank_at, [tie(v, stack) if i == 0 else v for i, v in enumerate(along_seq(heads_last))], halves, groups
+    )
 
     factor = jnp.sqrt(LOGIT_CAP / jnp.maximum(logit_peak, LOGIT_CAP))
     column_factor = jnp.repeat(factor, HEAD_DIM)

time: 550 us -> 527 us (0.958)
  waiting for transfers between devices: 184 us -> 146 us
  other arithmetic: 33.8 us -> 45.8 us
    ppermute x15 -> x16, waiting for transfers between devices: 90.3 us -> 51.7 us  [from_seq(): lax.ppermute(v, 'seq', [(i, (i - step) % groups) for i in range(groups)])]
    ppermute x9 -> x12, waiting for transfers between devices: 37.2 us -> 52.8 us  [over_z(): lax.ppermute(v, 'fsdp', [(i, (i + 4 * step) % shards) for i in range(shar...]
    reduce_scatter x1 -> x0, waiting for transfers between devices: 9.08 us -> none  [over_chips_sum(): lax.psum_scatter(v, 'fsdp', scatter_dimension=0, axis_index_groups=same_c...]
    ppermute x7 -> x9, waiting for transfers between devices: 20.5 us -> 14.5 us  [over_x(): return lax.ppermute(v, 'fsdp', x_way)]
    ppermute x15 -> x16, starting transfers between devices: 16.1 us -> 19 us  [from_seq(): lax.ppermute(v, 'seq', [(i, (i - step) % groups) for i in range(groups)])]
    ppermute x9 -> x12, starting transfers between devices: 27.1 us -> 24.4 us  [over_z(): lax.ppermute(v, 'fsdp', [(i, (i + 4 * step) % shards) for i in range(shar...]
  transfers between devices with their start and end apart: 69 -> 74, of which waited for: 31 -> 23; matrix products, arithmetic and copies ran while one was open for 8% -> 12% of each run, Pallas kernels for 32% -> 39%
where the time goes in v3:
time: 527 us; the launch traced here: 518 us
  Pallas kernels  220 us (42%)
  waiting for transfers between devices  146 us (28%)
  starting transfers between devices  63.9 us (12%)
  other arithmetic  45.8 us (9%)
  local copies, waits for them, and re-layouts  26.2 us (5%)
  between operations  16.4 us (3%)
    ppermute x12, waiting for transfers between devices, over_z(): lax.ppermute(v, 'fsdp', [(i, (i + 4 * step) % shards) for i in range(shar...  52.8 us
    ppermute x16, waiting for transfers between devices, from_seq(): lax.ppermute(v, 'seq', [(i, (i - step) % groups) for i in range(groups)])  51.7 us
    pallas_call x3, Pallas kernels, feed(): pl.pallas_call(lambda *refs: feed_kernel(count, own, tile, refs), grid=(1...  47.3 us
    pallas_call x2, Pallas kernels, attend_back(): pl.pallas_call(lambda *refs: attend_back_kernel(span, 1.0 / math.sqrt(HEA...  35.3 us
    pallas_call x2, Pallas kernels, weight_grad(): pl.pallas_call(kernel, grid=(cols // tile,), in_specs=[smem()] + whole +...  27.7 us
    ppermute x12, starting transfers between devices, over_z(): lax.ppermute(v, 'fsdp', [(i, (i + 4 * step) % shards) for i in range(shar...  24.4 us
    pallas_call x2, Pallas kernels, project_back(): pl.pallas_call(kernel, grid=(count,), in_specs=[pl.BlockSpec(weight.shape...  20 us
    ppermute x16, starting transfers between devices, from_seq(): lax.ppermute(v, 'seq', [(i, (i - step) % groups) for i in range(groups)])  19 us
  transfers between devices with their start and end apart: 74, of which 23 were waited for; matrix products, arithmetic and copies ran while one was open for 12% of the time, Pallas kernels for 39%

profile of v3, /device:TPU:0, one launch (start us, length us, event | category | flops | bytes accessed | tf_op | source)
XLA Modules:
  0.0 517.6 jit_solution(15034896547999431570)
XLA Ops:
  10.1 2.8 pick.1
  19.3 3.0 collective-permute-start.4
  22.3 2.6 collective-permute-start.6
  28.5 8.3 %collective-permute-done.4.refs_2_ = bf16[192,960]{1,0:T(8,128)(2,1)S(1)} collective-permute-done((bf16[192,960]{1,0:T(8,128)(2,1)S(1)}, bf16[192,960]{1,0:T(8,128)(2,1)S(1)}, u32[]{:S(2)}, u32[]{:S(2)}) %collective-permute-start.4) | collective-permute-done | bytes 368672 | tf_op jit(solution)/shard_map/ppermute | solution.py:902
  36.8 20.5 %collective-permute-done.6.refs_4_ = bf16[192,960]{1,0:T(8,128)(2,1)S(1)} collective-permute-done((bf16[192,960]{1,0:T(8,128)(2,1)S(1)}, bf16[192,960]{1,0:T(8,128)(2,1)S(1)}, u32[]{:S(2)}, u32[]{:S(2)}) %collective-permute-start.6) | collective-permute-done | bytes 368672 | tf_op jit(solution)/shard_map/ppermute | solution.py:902
  62.4 25.7 %collective-permute-done.7.refs_1_.refs_2_ = bf16[512,1280]{1,0:T(8,128)(2,1)} collective-permute-done((bf16[512,1280]{1,0:T(8,128)(2,1)S(1)}, bf16[512,1280]{1,0:T(8,128)(2,1)}, u32[]{:S(2)}, u32[]{:S(2)}) %collective-permute-start.7) | collective-permute-done | bytes 1310752 | tf_op jit(solution)/shard_map/ppermute | solution.py:905
  91.7 4.9 collective-permute-done.10.refs_7_
  96.6 9.6 %collective-permute-done.8.refs_5_ = bf16[192,960]{1,0:T(8,128)(2,1)S(1)} collective-permute-done((bf16[192,960]{1,0:T(8,128)(2,1)S(1)}, bf16[192,960]{1,0:T(8,128)(2,1)S(1)}, u32[]{:S(2)}, u32[]{:S(2)}) %collective-permute-start.8) | collective-permute-done | bytes 368672 | tf_op jit(solution)/shard_map/ppermute | solution.py:899
  109.4 3.7 place.1
  113.1 14.2 %project.1 = (bf16[2048,1280]{1,0:T(8,128)(2,1)}, bf16[960,2048]{1,0:T(8,128)(2,1)}, f32[16,1280]{1,0:T(8,128)}) custom-call(s32[1]{0:T(128)} %bitcast.5.rank_ref, bf16[16,16,960]{2,1,0:T(8,128)(2,1)} %get-tuple-element.143.small_ref, bf16[1280,960]{1,0:T(8,128)(2,1)} %bitcast.134, bf16[512,1280]{1,0:T(8,128)(2,1)} %bitcast.123, ...), custom_call_target="tpu_custom_call" | custom-call | flops 5033164800 | bytes 18186240 | tf_op jit(solution)/shard_map/project/pallas_call | solution.py:334
  127.8 12.0 %collective-permute-done.15.refs_2_.refs_7_.refs_9_ = bf16[512,1280]{1,0:T(8,128)(2,1)} collective-permute-done((bf16[512,1280]{1,0:T(8,128)(2,1)S(1)}, bf16[512,1280]{1,0:T(8,128)(2,1)}, u32[]{:S(2)}, u32[]{:S(2)}) %collective-permute-start.15) | collective-permute-done | bytes 1310752 | tf_op jit(solution)/shard_map/ppermute | solution.py:905
  141.6 9.0 %attend.2 = (bf16[2,160,512]{2,1,0:T(8,128)(2,1)}, bf16[1,2,160,512]{3,2,1,0:T(8,128)(2,1)}, f32[4,1,1024]{2,1,0:T(1,128)}, f32[4,1,1024]{2,1,0:T(1,128)}) custom-call(bf16[960,2048]{1,0:T(8,128)(2,1)} %get-tuple-element.154.refs_0_.refs_1_.refs_2_, bf16[960,2048]{1,0:T(8,128)(2,1)} %get-tuple-element.154.refs_0_.refs_1_.refs_2_, ...), custom_call_target="tpu_custom_call" | custom-call | flops 8388608000 | bytes 2949120 | tf_op jit(solution)/shard_map/attend/pallas_call | solution.py:110
  152.6 9.5 %attend.3 = (bf16[2,160,512]{2,1,0:T(8,128)(2,1)}, bf16[1,2,160,512]{3,2,1,0:T(8,128)(2,1)}, f32[4,1,1024]{2,1,0:T(1,128)}, f32[4,1,1024]{2,1,0:T(1,128)}) custom-call(bf16[960,2048]{1,0:T(8,128)(2,1)} %get-tuple-element.154.refs_0_.refs_1_.refs_2_, bf16[960,2048]{1,0:T(8,128)(2,1)} %get-tuple-element.154.refs_0_.refs_1_.refs_2_, ...), custom_call_target="tpu_custom_call" | custom-call | flops 8388608000 | bytes 2949120 | tf_op jit(solution)/shard_map/attend/pallas_call | solution.py:110
  166.8 5.7 %collective-permute-done.18 = bf16[2,160,512]{2,1,0:T(8,128)(2,1)S(1)} collective-permute-done((bf16[2,160,512]{2,1,0:T(8,128)(2,1)}, bf16[2,160,512]{2,1,0:T(8,128)(2,1)S(1)}, u32[]{:S(2)}, u32[]{:S(2)}) %collective-permute-start.18) | collective-permute-done | bytes 327712 | tf_op jit(solution)/shard_map/ppermute | solution.py:905
  173.2 2.6 maximum_select_fusion.w_ref
  176.6 6.8 %merge.1 = (bf16[1280,512]{1,0:T(8,128)(2,1)}, f32[512,1280]{1,0:T(8,128)}, bf16[256,1280]{1,0:T(8,128)(2,1)}, bf16[256,1280]{1,0:T(8,128)(2,1)}) custom-call(s32[4]{0:T(128)} %pad_add_fusion.1.slots_ref, bf16[512,1280]{1,0:T(8,128)(2,1)} %bitcast.124, bf16[1280,1280]{1,0:T(8,128)(2,1)} %maximum_select_fusion.w_ref, ...), custom_call_target="tpu_custom_call" | custom-call | flops 1677721600 | bytes 11141120 | tf_op jit(solution)/shard_map/merge/pallas_call | solution.py:610
  187.6 6.8 %all-gather.6.cloned.1.call-done = bf16[2560,1280]{1,0:T(8,128)(2,1)} async-done(((bf16[320,1280]{1,0:T(8,128)(2,1)}), bf16[2560,1280]{1,0:T(8,128)(2,1)}) %all-gather.6.cloned.1.call-update) | async-done | bytes 6553616 | tf_op jit(solution)/shard_map/all_gather | solution.py:950
  194.4 21.9 %feed.3 = (bf16[1024,1280]{1,0:T(8,128)(2,1)}, bf16[1024,1280]{1,0:T(8,128)(2,1)}, f32[512,1280]{1,0:T(8,128)}, bf16[512,1280]{1,0:T(8,128)(2,1)}, f32[512,1280]...) custom-call(bf16[256,1280]{1,0:T(8,128)(2,1)} %get-tuple-element.179.refs_0_, ...), custom_call_target="tpu_custom_call" | custom-call | flops 3355443200 | bytes 6881280 | tf_op jit(solution)/shard_map/feed/pallas_call | solution.py:272
  219.3 12.6 %feed.4 = (bf16[512,1280]{1,0:T(8,128)(2,1)}, bf16[512,1280]{1,0:T(8,128)(2,1)}, f32[256,1280]{1,0:T(8,128)}, bf16[256,1280]{1,0:T(8,128)(2,1)}, f32[256,1280]{1...) custom-call(bf16[256,1280]{1,0:T(8,128)(2,1)} %copy-done.13, bf16[256,1280]{1,0:T(8,128)(2,1)} %copy-done.14, ...), custom_call_target="tpu_custom_call" | custom-call | flops 1677721600 | bytes 4259840 | tf_op jit(solution)/shard_map/feed/pallas_call | solution.py:272
  236.9 12.8 %feed.5 = (bf16[512,1280]{1,0:T(8,128)(2,1)}, bf16[512,1280]{1,0:T(8,128)(2,1)}, f32[256,1280]{1,0:T(8,128)}, bf16[256,1280]{1,0:T(8,128)(2,1)}, f32[256,1280]{1...) custom-call(bf16[256,1280]{1,0:T(8,128)(2,1)} %collective-permute-done.27.refs_0_.refs_6_, ...), custom_call_target="tpu_custom_call" | custom-call | flops 1677721600 | bytes 4259840 | tf_op jit(solution)/shard_map/feed/pallas_call | solution.py:272
  254.9 3.1 convert_add_fusion.4.near_ref
  258.0 13.9 %weight_grad.2 = (bf16[4,160,1280]{2,1,0:T(8,128)(2,1)}, bf16[4,160,1280]{2,1,0:T(8,128)(2,1)}) custom-call(s32[1]{0:T(128)} %bitcast.43.x_ref, bf16[256,1280]{1,0:T(8,128)(2,1)} %get-tuple-element.179.refs_0_, bf16[256,1280]{1,0:T(8,128)(2,1)} %get-tuple-element.160.refs_1_, bf16[256,1280]{1,0:T(8,128)(2,1)} %copy-done.11, bf16[256,1280]{1,0:T(8,128)(2,1)} %copy-done.12, ...), custom_call_target="tpu_custom_call" | custom-call | flops 1677721600 | bytes 3440640 | tf_op jit(solution)/shard_map/weight_grad/pallas_call | solution.py:727
  273.2 8.0 %collective-permute-done.34.refs_1_ = bf16[256,1280]{1,0:T(8,128)(2,1)S(1)} collective-permute-done((bf16[256,1280]{1,0:T(8,128)(2,1)S(1)}, bf16[256,1280]{1,0:T(8,128)(2,1)S(1)}, u32[]{:S(2)}, u32[]{:S(2)}) %collective-permute-start.34) | collective-permute-done | bytes 655392 | tf_op jit(solution)/shard_map/ppermute | solution.py:905
  282.0 10.8 %turn.1 = (f32[512,1280]{1,0:T(8,128)}, bf16[512,1280]{1,0:T(8,128)(2,1)}, f32[4,1280]{1,0:T(4,128)}, bf16[2,160,512]{2,1,0:T(8,128)(2,1)}, bf16[2,160,512]{2,1,...) custom-call(s32[4]{0:T(128)} %pad_add_fusion.4.slots_ref, f32[512,1280]{1,0:T(8,128)} %get-tuple-element.158.after_ref, ...), custom_call_target="tpu_custom_call" | custom-call | flops 419430400 | bytes 3440640 | tf_op jit(solution)/shard_map/turn/pallas_call | solution.py:670
  295.4 13.7 %weight_grad.3 = (bf16[4,160,1280]{2,1,0:T(8,128)(2,1)}, bf16[4,160,1280]{2,1,0:T(8,128)(2,1)}) custom-call(s32[1]{0:T(128)} %bitcast.43.x_ref, bf16[1024,1280]{1,0:T(8,128)(2,1)} %get-tuple-element.189.refs_0_, bf16[512,1280]{1,0:T(8,128)(2,1)} %get-tuple-element.190.refs_1_, bf16[512,1280]{1,0:T(8,128)(2,1)} %get-tuple-element.191.refs_2_, ...), custom_call_target="tpu_custom_call" | custom-call | flops 1677721600 | bytes 3440640 | tf_op jit(solution)/shard_map/weight_grad/pallas_call | solution.py:727
  309.5 5.6 %out_grad_halves.1 = (bf16[1280,640]{1,0:T(8,128)(2,1)}, bf16[1280,640]{1,0:T(8,128)(2,1)}) custom-call(s32[1]{0:T(128)} %bitcast.7.core_ref, bf16[1280,512]{1,0:T(8,128)(2,1)} %get-tuple-element.194.m_ref, bf16[512,1280]{1,0:T(8,128)(2,1)} %get-tuple-element.197.g_ref), custom_call_target="tpu_custom_call" | custom-call | flops 419430400 | bytes 1638400 | tf_op jit(solution)/shard_map/out_grad_halves/pallas_call | solution.py:805
  318.7 2.2 convert_add_fusion.1
  321.0 4.2 out_grad_parts.1
  330.9 8.5 %collective-permute-start.46 = (bf16[160,1280]{1,0:T(8,128)(2,1)}, bf16[160,1280]{1,0:T(8,128)(2,1)S(1)}, u32[]{:S(2)}, u32[]{:S(2)}) collective-permute-start(bf16[160,1280]{1,0:T(8,128)(2,1)} %get-tuple-element.268), channel_id=1, source_target_pairs={{0,24},{2,26},{4,28},{6,30},{8,0},{10,2},{12,4},{14,6},{16,8},{18,... | collective-permute-start | bytes 1228808 | tf_op jit(solution)/shard_map/ppermute | solution.py:902
  340.3 17.6 %attend_back.2 = bf16[3,160,2048]{2,1,0:T(8,128)(2,1)} custom-call(bf16[960,2048]{1,0:T(8,128)(2,1)} %get-tuple-element.154.refs_0_.refs_1_.refs_2_, bf16[960,2048]{1,0:T(8,128)(2,1)} %get-tuple-element.154.refs_0_.refs_1_.refs_2_, bf16[960,2048]{1,0:T(8,128)(2,1)} %get-tuple-element.154.refs_0_.refs_1_.refs_2_, bf16[32,1024]{1,0:T(8,128)(2,1)} %bitcast.147, ...), custom_call_target="tpu_custom_call" | custom-call | flops 4194304000 | bytes 1474560 | tf_op jit(solution)/shard_map/attend_back/pallas_call | solution.py:186
  357.9 2.2 copy.45.refs_1_
  360.1 8.9 %head_grad.2 = (bf16[4,160,800]{2,1,0:T(8,128)(2,1)}, bf16[4,160,800]{2,1,0:T(8,128)(2,1)}) custom-call(s32[1]{0:T(128)} %bitcast.43.x_ref, bf16[2048,1280]{1,0:T(8,128)(2,1)} %get-tuple-element.166.n_ref, bf16[480,2048]{1,0:T(8,128)(2,1)} %bitcast.131, bf16[1280,320]{1,0:T(8,128)(2,1)} %get-tuple-element.203.refs_0_, bf16[1280,320]{1,0:T(8,128)(2,1)} %copy.45.refs_1_), custom_call_target="tpu_custom_call" | custom-call | flops 629145600 | bytes 1802240 | tf_op jit(solution)/shard_map/head_grad/pallas_call | solution.py:771
  370.6 4.2 collective-permute-done.45
  378.9 2.5 collective-permute-start.52
  381.6 2.3 collective-permute-start.51
  386.9 17.7 %attend_back.3 = bf16[3,160,2048]{2,1,0:T(8,128)(2,1)} custom-call(bf16[960,2048]{1,0:T(8,128)(2,1)} %get-tuple-element.154.refs_0_.refs_1_.refs_2_, bf16[960,2048]{1,0:T(8,128)(2,1)} %get-tuple-element.154.refs_0_.refs_1_.refs_2_, bf16[960,2048]{1,0:T(8,128)(2,1)} %get-tuple-element.154.refs_0_.refs_1_.refs_2_, bf16[32,1024]{1,0:T(8,128)(2,1)} %bitcast.148, ...), custom_call_target="tpu_custom_call" | custom-call | flops 4194304000 | bytes 1474560 | tf_op jit(solution)/shard_map/attend_back/pallas_call | solution.py:186
  404.5 7.6 %head_grad.3 = (bf16[4,160,480]{2,1,0:T(8,128)(2,1)}, bf16[4,160,480]{2,1,0:T(8,128)(2,1)}) custom-call(s32[1]{0:T(128)} %bitcast.43.x_ref, bf16[2048,1280]{1,0:T(8,128)(2,1)} %get-tuple-element.166.n_ref, bf16[480,2048]{1,0:T(8,128)(2,1)} %bitcast.128), custom_call_target="tpu_custom_call" | custom-call | flops 629145600 | bytes 1802240 | tf_op jit(solution)/shard_map/head_grad/pallas_call | solution.py:771
  419.0 10.1 %project_back.2 = (f32[512,1280]{1,0:T(8,128)}, bf16[512,1280]{1,0:T(8,128)(2,1)}, f32[8,1280]{1,0:T(8,128)}, f32[8,960]{1,0:T(8,128)}) custom-call(bf16[1280,960]{1,0:T(8,128)(2,1)} %bitcast.135, bf16[480,2048]{1,0:T(8,128)(2,1)} %bitcast.132, bf16[480,2048]{1,0:T(8,128)(2,1)} %bitcast.129, bf16[512,1280]{1,0:T(8,128)(2,1)} %collective-permute-done.7.refs_1_.refs_2_, ...), custom_call_target="tpu_custom_call" | custom-call | flops 629145600 | bytes 3235840 | tf_op jit(solution)/shard_map/project_back/pallas_call | solution.py:407
  435.0 3.0 fusion.10
  440.8 9.9 %project_back.3 = (f32[512,1280]{1,0:T(8,128)}, bf16[512,1280]{1,0:T(8,128)(2,1)}, f32[8,1280]{1,0:T(8,128)}, f32[8,960]{1,0:T(8,128)}) custom-call(bf16[1280,960]{1,0:T(8,128)(2,1)} %bitcast.136, bf16[480,2048]{1,0:T(8,128)(2,1)} %bitcast.133, bf16[480,2048]{1,0:T(8,128)(2,1)} %bitcast.130, bf16[512,1280]{1,0:T(8,128)(2,1)} %bitcast.125, ...), custom_call_target="tpu_custom_call" | custom-call | flops 629145600 | bytes 3235840 | tf_op jit(solution)/shard_map/project_back/pallas_call | solution.py:407
  450.8 18.6 %collective-permute-done.63 = bf16[160,1280]{1,0:T(8,128)(2,1)} collective-permute-done((bf16[160,1280]{1,0:T(8,128)(2,1)}, bf16[160,1280]{1,0:T(8,128)(2,1)}, u32[]{:S(2)}, u32[]{:S(2)}) %collective-permute-start.63) | collective-permute-done | bytes 409632 | tf_op jit(solution)/shard_map/ppermute | solution.py:902
  476.9 3.7 multiply_reduce_fusion
  481.1 4.0 collective-permute-done.67
  485.2 2.4 collective-permute-start.68
  488.4 2.9 collective-permute-done.68
  494.2 4.9 collective-permute-done.69
  502.5 2.6 finish_heads.1
  506.9 3.5 finish_feed.1
  (344 shorter events, 107.6 us)
Async XLA Ops:
  7.2 133.9 %all-gather.4.cloned.1.call-start = ((), (), s32[]{:S(2)}) async-start(), calls=%async_computation | async-start | bytes 1843200 | tf_op jit(solution)/shard_map/all_gather | solution.py:950
  16.3 178.1 %all-gather.6.cloned.1.call-start = ((), (), s32[]{:S(2)}) async-start(), calls=%async_computation.1 | async-start | bytes 7372800 | tf_op jit(solution)/shard_map/all_gather | solution.py:950
  19.3 17.5 %collective-permute-start.4 = (bf16[192,960]{1,0:T(8,128)(2,1)S(1)}, bf16[192,960]{1,0:T(8,128)(2,1)S(1)}, u32[]{:S(2)}, u32[]{:S(2)}) collective-permute-start(bf16[192,960]{1,0:T(8,128)(2,1)S(1)} %maximum_select_fusion.2.refs_0_), channel_id=1, source_target_pairs={{0,8},{2,10},{4,12},{6,14},{8,16},{10,18},{12,20},{14,22},{16,24},... | collective-permute-start | bytes 1105928 | tf_op jit(solution)/shard_map/ppermute | solution.py:902
  22.3 35.0 %collective-permute-start.6 = (bf16[192,960]{1,0:T(8,128)(2,1)S(1)}, bf16[192,960]{1,0:T(8,128)(2,1)S(1)}, u32[]{:S(2)}, u32[]{:S(2)}) collective-permute-start(bf16[192,960]{1,0:T(8,128)(2,1)S(1)} %maximum_select_fusion.2.refs_0_), channel_id=1, source_target_pairs={{0,16},{2,18},{4,20},{6,22},{8,24},{10,26},{12,28},{14,30},{16,0},... | collective-permute-start | bytes 1105928 | tf_op jit(solution)/shard_map/ppermute | solution.py:902
  24.8 32.4 %collective-permute-start.9 = (bf16[192,960]{1,0:T(8,128)(2,1)S(1)}, bf16[192,960]{1,0:T(8,128)(2,1)S(1)}, u32[]{:S(2)}, u32[]{:S(2)}) collective-permute-start(bf16[192,960]{1,0:T(8,128)(2,1)S(1)} %maximum_select_fusion.2.refs_0_), channel_id=1, source_target_pairs={{0,24},{2,26},{4,28},{6,30},{8,0},{10,2},{12,4},{14,6},{16,8},{18,... | collective-permute-start | bytes 1105928 | tf_op jit(solution)/shard_map/ppermute | solution.py:902
  57.3 30.8 %collective-permute-start.7 = (bf16[512,1280]{1,0:T(8,128)(2,1)S(1)}, bf16[512,1280]{1,0:T(8,128)(2,1)}, u32[]{:S(2)}, u32[]{:S(2)}) collective-permute-start(bf16[512,1280]{1,0:T(8,128)(2,1)S(1)} %bitcast.126), channel_id=1, source_target_pairs={{0,1},{1,0},{2,3},{3,2},{4,5},{5,4},{6,7},{7,6},{8,9},{9,8},{10,11... | collective-permute-start | bytes 3932168 | tf_op jit(solution)/shard_map/ppermute | solution.py:905
  58.9 32.7 %collective-permute-start.3 = (bf16[192,960]{1,0:T(8,128)(2,1)S(1)}, bf16[192,960]{1,0:T(8,128)(2,1)S(1)}, u32[]{:S(2)}, u32[]{:S(2)}) collective-permute-start(bf16[192,960]{1,0:T(8,128)(2,1)S(1)} %maximum_select_fusion.2.refs_0_), channel_id=1, source_target_pairs={{0,4},{2,6},{4,0},{6,2},{8,12},{10,14},{12,8},{14,10},{16,20},{18,... | collective-permute-start | bytes 1105928 | tf_op jit(solution)/shard_map/ppermute | solution.py:899
  60.4 31.2 %collective-permute-start.5 = (bf16[192,960]{1,0:T(8,128)(2,1)S(1)}, bf16[192,960]{1,0:T(8,128)(2,1)S(1)}, u32[]{:S(2)}, u32[]{:S(2)}) collective-permute-start(bf16[192,960]{1,0:T(8,128)(2,1)S(1)} %collective-permute-done.4.refs_2_), channel_id=1, source_target_pairs={{0,4},{2,6},{4,0},{6,2},{8,12},{10,14},{12,8},{14,10},{16,20},{18,... | collective-permute-start | bytes 1105928 | tf_op jit(solution)/shard_map/ppermute | solution.py:899
  60.9 35.6 %collective-permute-start.10 = (bf16[192,960]{1,0:T(8,128)(2,1)S(1)}, bf16[192,960]{1,0:T(8,128)(2,1)S(1)}, u32[]{:S(2)}, u32[]{:S(2)}) collective-permute-start(bf16[192,960]{1,0:T(8,128)(2,1)S(1)} %collective-permute-done.9.refs_6_), channel_id=1, source_target_pairs={{0,4},{2,6},{4,0},{6,2},{8,12},{10,14},{12,8},{14,10},{16,20},{18,... | collective-permute-start | bytes 1105928 | tf_op jit(solution)/shard_map/ppermute | solution.py:899
  88.1 18.0 %collective-permute-start.8 = (bf16[192,960]{1,0:T(8,128)(2,1)S(1)}, bf16[192,960]{1,0:T(8,128)(2,1)S(1)}, u32[]{:S(2)}, u32[]{:S(2)}) collective-permute-start(bf16[192,960]{1,0:T(8,128)(2,1)S(1)} %collective-permute-done.6.refs_4_), channel_id=1, source_target_pairs={{0,4},{2,6},{4,0},{6,2},{8,12},{10,14},{12,8},{14,10},{16,20},{18,... | collective-permute-start | bytes 1105928 | tf_op jit(solution)/shard_map/ppermute | solution.py:899
  108.4 31.4 %collective-permute-start.15 = (bf16[512,1280]{1,0:T(8,128)(2,1)S(1)}, bf16[512,1280]{1,0:T(8,128)(2,1)}, u32[]{:S(2)}, u32[]{:S(2)}) collective-permute-start(bf16[512,1280]{1,0:T(8,128)(2,1)S(1)} %bitcast_select_fusion.refs_4_.refs_5_.live_ref.refs_3_), channel_id=1, source_target_pairs={{0,1},{1,0},{2,3},{3,2},{4,5},{5,4},{6,7},{7,6},{8,9},{9,8},{10,11... | collective-permute-start | bytes 3932168 | tf_op jit(solution)/shard_map/ppermute | solution.py:905
  127.3 25.2 %collective-permute-start.14 = (bf16[512,1280]{1,0:T(8,128)(2,1)S(1)}, bf16[512,1280]{1,0:T(8,128)(2,1)S(1)}, u32[]{:S(2)}, u32[]{:S(2)}) collective-permute-start(bf16[512,1280]{1,0:T(8,128)(2,1)S(1)} %bitcast_select_fusion.refs_4_.refs_5_.live_ref.refs_3_), channel_id=1, source_target_pairs={{0,2},{2,0},{4,6},{6,4},{8,10},{10,8},{12,14},{14,12},{16,18},{18,... | collective-permute-start | bytes 3932168 | tf_op jit(solution)/shard_map/ppermute | solution.py:896
  139.8 12.8 %collective-permute-start.16 = (bf16[512,1280]{1,0:T(8,128)(2,1)}, bf16[512,1280]{1,0:T(8,128)(2,1)}, u32[]{:S(2)}, u32[]{:S(2)}) collective-permute-start(bf16[512,1280]{1,0:T(8,128)(2,1)} %collective-permute-done.15.refs_2_.refs_7_.refs_9_), channel_id=1, source_target_pairs={{0,2},{2,0},{4,6},{6,4},{8,10},{10,8},{12,14},{14,12},{16,18},{18,... | collective-permute-start | bytes 3932168 | tf_op jit(solution)/shard_map/ppermute | solution.py:896
  141.1 32.1 %collective-permute-start.1 = (bf16[1280,640]{1,0:T(8,128)(2,1)}, bf16[1280,640]{1,0:T(8,128)(2,1)S(1)}, u32[]{:S(2)}, u32[]{:S(2)}) collective-permute-start(bf16[1280,640]{1,0:T(8,128)(2,1)} %bitcast.139), channel_id=1, source_target_pairs={{0,2},{2,0},{4,6},{6,4},{8,10},{10,8},{12,14},{14,12},{16,18},{18,... | collective-permute-start | bytes 4915208 | tf_op jit(solution)/shard_map/ppermute | solution.py:896
  150.6 13.3 %collective-permute-start.17 = (bf16[2,160,512]{2,1,0:T(8,128)(2,1)}, bf16[2,160,512]{2,1,0:T(8,128)(2,1)S(1)}, u32[]{:S(2)}, u32[]{:S(2)}) collective-permute-start(bf16[2,160,512]{2,1,0:T(8,128)(2,1)} %bitcast.160), channel_id=1, source_target_pairs={{0,1},{1,0},{2,3},{3,2},{4,5},{5,4},{6,7},{7,6},{8,9},{9,8},{10,11... | collective-permute-start | bytes 983048 | tf_op jit(solution)/shard_map/ppermute | solution.py:905
  152.6 23.2 %collective-permute-start.19 = (bf16[1,160,512]{2,1,0:T(8,128)(2,1)S(1)}, bf16[1,160,512]{2,1,0:T(8,128)(2,1)S(1)}, u32[]{:S(2)}, u32[]{:S(2)}) collective-permute-start(bf16[1,160,512]{2,1,0:T(8,128)(2,1)S(1)} %get-tuple-element.281), channel_id=1, source_target_pairs={{0,2},{2,0},{4,6},{6,4},{8,10},{10,8},{12,14},{14,12},{16,18},{18,... | collective-permute-start | bytes 491528 | tf_op jit(solution)/shard_map/ppermute | solution.py:896
  164.6 11.2 %collective-permute-start.21 = (bf16[1,160,512]{2,1,0:T(8,128)(2,1)S(1)}, bf16[1,160,512]{2,1,0:T(8,128)(2,1)S(1)}, u32[]{:S(2)}, u32[]{:S(2)}) collective-permute-start(bf16[1,160,512]{2,1,0:T(8,128)(2,1)S(1)} %get-tuple-element.277), channel_id=1, source_target_pairs={{0,2},{2,0},{4,6},{6,4},{8,10},{10,8},{12,14},{14,12},{16,18},{18,... | collective-permute-start | bytes 491528 | tf_op jit(solution)/shard_map/ppermute | solution.py:896
  184.0 32.3 %collective-permute-start.28 = (bf16[256,1280]{1,0:T(8,128)(2,1)}, bf16[256,1280]{1,0:T(8,128)(2,1)S(1)}, u32[]{:S(2)}, u32[]{:S(2)}) collective-permute-start(bf16[256,1280]{1,0:T(8,128)(2,1)} %get-tuple-element.179.refs_0_), channel_id=1, source_target_pairs={{0,1},{1,0},{2,3},{3,2},{4,5},{5,4},{6,7},{7,6},{8,9},{9,8},{10,11... | collective-permute-start | bytes 1966088 | tf_op jit(solution)/shard_map/ppermute | solution.py:905
  187.3 29.1 %collective-permute-start.27 = (bf16[256,1280]{1,0:T(8,128)(2,1)}, bf16[256,1280]{1,0:T(8,128)(2,1)}, u32[]{:S(2)}, u32[]{:S(2)}) collective-permute-start(bf16[256,1280]{1,0:T(8,128)(2,1)} %get-tuple-element.160.refs_1_), channel_id=1, source_target_pairs={{0,1},{1,0},{2,3},{3,2},{4,5},{5,4},{6,7},{7,6},{8,9},{9,8},{10,11... | collective-permute-start | bytes 1966088 | tf_op jit(solution)/shard_map/ppermute | solution.py:905
  232.4 22.5 %collective-permute-start.26 = (bf16[512,1280]{1,0:T(8,128)(2,1)}, bf16[512,1280]{1,0:T(8,128)(2,1)}, u32[]{:S(2)}, u32[]{:S(2)}) collective-permute-start(bf16[512,1280]{1,0:T(8,128)(2,1)} %get-tuple-element.169), channel_id=1, source_target_pairs={{0,2},{2,0},{4,6},{6,4},{8,10},{10,8},{12,14},{14,12},{16,18},{18,... | collective-permute-start | bytes 3932168 | tf_op jit(solution)/shard_map/ppermute | solution.py:896
  250.1 23.1 %collective-permute-start.33 = (bf16[256,1280]{1,0:T(8,128)(2,1)S(1)}, bf16[256,1280]{1,0:T(8,128)(2,1)S(1)}, u32[]{:S(2)}, u32[]{:S(2)}) collective-permute-start(bf16[256,1280]{1,0:T(8,128)(2,1)S(1)} %add_convert_fusion.5), channel_id=1, source_target_pairs={{0,1},{1,0},{2,3},{3,2},{4,5},{5,4},{6,7},{7,6},{8,9},{9,8},{10,11... | collective-permute-start | bytes 1966088 | tf_op jit(solution)/shard_map/ppermute | solution.py:905
  253.3 27.9 %collective-permute-start.34 = (bf16[256,1280]{1,0:T(8,128)(2,1)S(1)}, bf16[256,1280]{1,0:T(8,128)(2,1)S(1)}, u32[]{:S(2)}, u32[]{:S(2)}) collective-permute-start(bf16[256,1280]{1,0:T(8,128)(2,1)S(1)} %add_convert_fusion.4), channel_id=1, source_target_pairs={{0,1},{1,0},{2,3},{3,2},{4,5},{5,4},{6,7},{7,6},{8,9},{9,8},{10,11... | collective-permute-start | bytes 1966088 | tf_op jit(solution)/shard_map/ppermute | solution.py:905
  272.0 46.5 %collective-permute-start.35 = (bf16[4,160,1280]{2,1,0:T(8,128)(2,1)}, bf16[4,160,1280]{2,1,0:T(8,128)(2,1)}, u32[]{:S(2)}, u32[]{:S(2)}) collective-permute-start(bf16[4,160,1280]{2,1,0:T(8,128)(2,1)} %get-tuple-element.183), channel_id=1, source_target_pairs={{0,4},{2,6},{4,0},{6,2},{8,12},{10,14},{12,8},{14,10},{16,20},{18,... | collective-permute-start | bytes 4915208 | tf_op jit(solution)/shard_map/ppermute | solution.py:899
  292.9 16.3 %collective-permute-start.36 = (bf16[2,160,512]{2,1,0:T(8,128)(2,1)}, bf16[2,160,512]{2,1,0:T(8,128)(2,1)}, u32[]{:S(2)}, u32[]{:S(2)}) collective-permute-start(bf16[2,160,512]{2,1,0:T(8,128)(2,1)} %get-tuple-element.195), channel_id=1, source_target_pairs={{0,1},{1,0},{2,3},{3,2},{4,5},{5,4},{6,7},{7,6},{8,9},{9,8},{10,11... | collective-permute-start | bytes 983048 | tf_op jit(solution)/shard_map/ppermute | solution.py:905
  294.3 15.1 %collective-permute-start.37 = (bf16[2,160,512]{2,1,0:T(8,128)(2,1)}, bf16[2,160,512]{2,1,0:T(8,128)(2,1)}, u32[]{:S(2)}, u32[]{:S(2)}) collective-permute-start(bf16[2,160,512]{2,1,0:T(8,128)(2,1)} %get-tuple-element.196), channel_id=1, source_target_pairs={{0,1},{1,0},{2,3},{3,2},{4,5},{5,4},{6,7},{7,6},{8,9},{9,8},{10,11... | collective-permute-start | bytes 983048 | tf_op jit(solution)/shard_map/ppermute | solution.py:905
  317.3 58.3 %collective-permute-start.47 = (bf16[4,160,1280]{2,1,0:T(8,128)(2,1)}, bf16[4,160,1280]{2,1,0:T(8,128)(2,1)}, u32[]{:S(2)}, u32[]{:S(2)}) collective-permute-start(bf16[4,160,1280]{2,1,0:T(8,128)(2,1)} %get-tuple-element.192), channel_id=1, source_target_pairs={{0,4},{2,6},{4,0},{6,2},{8,12},{10,14},{12,8},{14,10},{16,20},{18,... | collective-permute-start | bytes 4915208 | tf_op jit(solution)/shard_map/ppermute | solution.py:899
  317.9 21.5 %collective-permute-start.41 = (bf16[320,512]{1,0:T(8,128)(2,1)}, bf16[320,512]{1,0:T(8,128)(2,1)}, u32[]{:S(2)}, u32[]{:S(2)}) collective-permute-start(bf16[320,512]{1,0:T(8,128)(2,1)} %get-tuple-element.202), channel_id=1, source_target_pairs={{0,2},{2,0},{4,6},{6,4},{8,10},{10,8},{12,14},{14,12},{16,18},{18,... | collective-permute-start | bytes 983048 | tf_op jit(solution)/shard_map/ppermute | solution.py:896
  318.1 12.7 %collective-permute-start.39 = (bf16[2,160,512]{2,1,0:T(8,128)(2,1)}, bf16[2,160,512]{2,1,0:T(8,128)(2,1)}, u32[]{:S(2)}, u32[]{:S(2)}) collective-permute-start(bf16[2,160,512]{2,1,0:T(8,128)(2,1)} %collective-permute-done.36.refs_6_), channel_id=1, source_target_pairs={{0,2},{2,0},{4,6},{6,4},{8,10},{10,8},{12,14},{14,12},{16,18},{18,... | collective-permute-start | bytes 983048 | tf_op jit(solution)/shard_map/ppermute | solution.py:896
  318.5 20.9 %collective-permute-start.40 = (bf16[2,160,512]{2,1,0:T(8,128)(2,1)}, bf16[2,160,512]{2,1,0:T(8,128)(2,1)}, u32[]{:S(2)}, u32[]{:S(2)}) collective-permute-start(bf16[2,160,512]{2,1,0:T(8,128)(2,1)} %collective-permute-done.37.refs_6_), channel_id=1, source_target_pairs={{0,2},{2,0},{4,6},{6,4},{8,10},{10,8},{12,14},{14,12},{16,18},{18,... | collective-permute-start | bytes 983048 | tf_op jit(solution)/shard_map/ppermute | solution.py:896
  327.3 30.6 %collective-permute-start.42 = (bf16[1280,320]{0,1:T(8,128)(2,1)}, bf16[1280,320]{0,1:T(8,128)(2,1)}, u32[]{:S(2)}, u32[]{:S(2)}) collective-permute-start(bf16[1280,320]{0,1:T(8,128)(2,1)} %copy.44), channel_id=1, source_target_pairs={{0,1},{1,0},{2,3},{3,2},{4,5},{5,4},{6,7},{7,6},{8,9},{9,8},{10,11... | collective-permute-start | bytes 2457608 | tf_op jit(solution)/shard_map/ppermute | solution.py:905
  330.9 39.8 %collective-permute-start.46 = (bf16[160,1280]{1,0:T(8,128)(2,1)}, bf16[160,1280]{1,0:T(8,128)(2,1)S(1)}, u32[]{:S(2)}, u32[]{:S(2)}) collective-permute-start(bf16[160,1280]{1,0:T(8,128)(2,1)} %get-tuple-element.268), channel_id=1, source_target_pairs={{0,24},{2,26},{4,28},{6,30},{8,0},{10,2},{12,4},{14,6},{16,8},{18,... | collective-permute-start | bytes 1228808 | tf_op jit(solution)/shard_map/ppermute | solution.py:902
  339.4 35.4 %collective-permute-start.45 = (bf16[160,1280]{1,0:T(8,128)(2,1)}, bf16[160,1280]{1,0:T(8,128)(2,1)S(1)}, u32[]{:S(2)}, u32[]{:S(2)}) collective-permute-start(bf16[160,1280]{1,0:T(8,128)(2,1)} %get-tuple-element.269), channel_id=1, source_target_pairs={{0,16},{2,18},{4,20},{6,22},{8,24},{10,26},{12,28},{14,30},{16,0},... | collective-permute-start | bytes 1228808 | tf_op jit(solution)/shard_map/ppermute | solution.py:902
  339.4 35.4 %collective-permute-start.44 = (bf16[160,1280]{1,0:T(8,128)(2,1)}, bf16[160,1280]{1,0:T(8,128)(2,1)S(1)}, u32[]{:S(2)}, u32[]{:S(2)}) collective-permute-start(bf16[160,1280]{1,0:T(8,128)(2,1)} %get-tuple-element.270), channel_id=1, source_target_pairs={{0,8},{2,10},{4,12},{6,14},{8,16},{10,18},{12,20},{14,22},{16,24},... | collective-permute-start | bytes 1228808 | tf_op jit(solution)/shard_map/ppermute | solution.py:902
  369.1 43.1 %collective-permute-start.54 = (bf16[4,160,800]{2,1,0:T(8,128)(2,1)}, bf16[4,160,800]{2,1,0:T(8,128)(2,1)}, u32[]{:S(2)}, u32[]{:S(2)}) collective-permute-start(bf16[4,160,800]{2,1,0:T(8,128)(2,1)} %get-tuple-element.204), channel_id=1, source_target_pairs={{0,4},{2,6},{4,0},{6,2},{8,12},{10,14},{12,8},{14,10},{16,20},{18,... | collective-permute-start | bytes 3072008 | tf_op jit(solution)/shard_map/ppermute | solution.py:899
  370.6 14.5 %collective-permute-start.43 = (bf16[512,1280]{1,0:T(8,128)(2,1)}, bf16[512,1280]{1,0:T(8,128)(2,1)S(1)}, u32[]{:S(2)}, u32[]{:S(2)}) collective-permute-start(bf16[512,1280]{1,0:T(8,128)(2,1)} %get-tuple-element.205), channel_id=1, source_target_pairs={{0,2},{2,0},{4,6},{6,4},{8,10},{10,8},{12,14},{14,12},{16,18},{18,... | collective-permute-start | bytes 3932168 | tf_op jit(solution)/shard_map/ppermute | solution.py:896
  378.6 36.6 %collective-permute-start.53 = (bf16[160,1280]{1,0:T(8,128)(2,1)}, bf16[160,1280]{1,0:T(8,128)(2,1)}, u32[]{:S(2)}, u32[]{:S(2)}) collective-permute-start(bf16[160,1280]{1,0:T(8,128)(2,1)} %get-tuple-element.265), channel_id=1, source_target_pairs={{0,24},{2,26},{4,28},{6,30},{8,0},{10,2},{12,4},{14,6},{16,8},{18,... | collective-permute-start | bytes 1228808 | tf_op jit(solution)/shard_map/ppermute | solution.py:902
  378.9 38.7 %collective-permute-start.52 = (bf16[160,1280]{1,0:T(8,128)(2,1)}, bf16[160,1280]{1,0:T(8,128)(2,1)}, u32[]{:S(2)}, u32[]{:S(2)}) collective-permute-start(bf16[160,1280]{1,0:T(8,128)(2,1)} %get-tuple-element.266), channel_id=1, source_target_pairs={{0,16},{2,18},{4,20},{6,22},{8,24},{10,26},{12,28},{14,30},{16,0},... | collective-permute-start | bytes 1228808 | tf_op jit(solution)/shard_map/ppermute | solution.py:902
  381.6 36.0 %collective-permute-start.51 = (bf16[160,1280]{1,0:T(8,128)(2,1)S(1)}, bf16[160,1280]{1,0:T(8,128)(2,1)}, u32[]{:S(2)}, u32[]{:S(2)}) collective-permute-start(bf16[160,1280]{1,0:T(8,128)(2,1)S(1)} %get-tuple-element.267), channel_id=1, source_target_pairs={{0,8},{2,10},{4,12},{6,14},{8,16},{10,18},{12,20},{14,22},{16,24},... | collective-permute-start | bytes 1228808 | tf_op jit(solution)/shard_map/ppermute | solution.py:902
  385.1 33.9 %collective-permute-start.50 = (bf16[512,1280]{1,0:T(8,128)(2,1)}, bf16[512,1280]{1,0:T(8,128)(2,1)}, u32[]{:S(2)}, u32[]{:S(2)}) collective-permute-start(bf16[512,1280]{1,0:T(8,128)(2,1)} %pad_maximum_fusion), channel_id=1, source_target_pairs={{0,1},{1,0},{2,3},{3,2},{4,5},{5,4},{6,7},{7,6},{8,9},{9,8},{10,11... | collective-permute-start | bytes 3932168 | tf_op jit(solution)/shard_map/ppermute | solution.py:905
  412.2 17.0 %collective-permute-start.56 = (bf16[4,160,480]{2,1,0:T(8,128)(2,1)}, bf16[4,160,480]{2,1,0:T(8,128)(2,1)}, u32[]{:S(2)}, u32[]{:S(2)}) collective-permute-start(bf16[4,160,480]{2,1,0:T(8,128)(2,1)} %get-tuple-element.217), channel_id=1, source_target_pairs={{0,4},{2,6},{4,0},{6,2},{8,12},{10,14},{12,8},{14,10},{16,20},{18,... | collective-permute-start | bytes 1843208 | tf_op jit(solution)/shard_map/ppermute | solution.py:899
  415.2 25.6 %collective-permute-start.58 = (bf16[2,80,1280]{2,1,0:T(8,128)(2,1)S(1)}, bf16[2,80,1280]{2,1,0:T(8,128)(2,1)}, u32[]{:S(2)}, u32[]{:S(2)}) collective-permute-start(bf16[2,80,1280]{2,1,0:T(8,128)(2,1)S(1)} %pad_maximum_fusion.2.refs_0_), channel_id=1, source_target_pairs={{0,1},{1,0},{2,3},{3,2},{4,5},{5,4},{6,7},{7,6},{8,9},{9,8},{10,11... | collective-permute-start | bytes 1228808 | tf_op jit(solution)/shard_map/ppermute | solution.py:905
  431.8 18.9 %collective-permute-start.64 = (bf16[160,1280]{1,0:T(8,128)(2,1)}, bf16[160,1280]{1,0:T(8,128)(2,1)S(1)}, u32[]{:S(2)}, u32[]{:S(2)}) collective-permute-start(bf16[160,1280]{1,0:T(8,128)(2,1)} %get-tuple-element.262), channel_id=1, source_target_pairs={{0,24},{2,26},{4,28},{6,30},{8,0},{10,2},{12,4},{14,6},{16,8},{18,... | collective-permute-start | bytes 1228808 | tf_op jit(solution)/shard_map/ppermute | solution.py:902
  432.7 36.6 %collective-permute-start.63 = (bf16[160,1280]{1,0:T(8,128)(2,1)}, bf16[160,1280]{1,0:T(8,128)(2,1)}, u32[]{:S(2)}, u32[]{:S(2)}) collective-permute-start(bf16[160,1280]{1,0:T(8,128)(2,1)} %get-tuple-element.264), channel_id=1, source_target_pairs={{0,16},{2,18},{4,20},{6,22},{8,24},{10,26},{12,28},{14,30},{16,0},... | collective-permute-start | bytes 1228808 | tf_op jit(solution)/shard_map/ppermute | solution.py:902
  432.7 36.6 %collective-permute-start.62 = (bf16[160,1280]{1,0:T(8,128)(2,1)}, bf16[160,1280]{1,0:T(8,128)(2,1)}, u32[]{:S(2)}, u32[]{:S(2)}) collective-permute-start(bf16[160,1280]{1,0:T(8,128)(2,1)} %get-tuple-element.263), channel_id=1, source_target_pairs={{0,8},{2,10},{4,12},{6,14},{8,16},{10,18},{12,20},{14,22},{16,24},... | collective-permute-start | bytes 1228808 | tf_op jit(solution)/shard_map/ppermute | solution.py:902
  439.3 37.6 %collective-permute-start.60 = (bf16[512,1280]{1,0:T(8,128)(2,1)}, bf16[512,1280]{1,0:T(8,128)(2,1)}, u32[]{:S(2)}, u32[]{:S(2)}) collective-permute-start(bf16[512,1280]{1,0:T(8,128)(2,1)} %add_convert_fusion), channel_id=1, source_target_pairs={{0,1},{1,0},{2,3},{3,2},{4,5},{5,4},{6,7},{7,6},{8,9},{9,8},{10,11... | collective-permute-start | bytes 3932168 | tf_op jit(solution)/shard_map/ppermute | solution.py:905
  450.7 22.4 %collective-permute-start.59 = (bf16[512,1280]{1,0:T(8,128)(2,1)}, bf16[512,1280]{1,0:T(8,128)(2,1)}, u32[]{:S(2)}, u32[]{:S(2)}) collective-permute-start(bf16[512,1280]{1,0:T(8,128)(2,1)} %get-tuple-element.231), channel_id=1, source_target_pairs={{0,2},{2,0},{4,6},{6,4},{8,10},{10,8},{12,14},{14,12},{16,18},{18,... | collective-permute-start | bytes 3932168 | tf_op jit(solution)/shard_map/ppermute | solution.py:896
  473.7 28.0 %collective-permute-start.70 = (bf16[2,80,1280]{2,1,0:T(8,128)(2,1)S(1)}, bf16[2,80,1280]{2,1,0:T(8,128)(2,1)S(1)}, u32[]{:S(2)}, u32[]{:S(2)}) collective-permute-start(bf16[2,80,1280]{2,1,0:T(8,128)(2,1)S(1)} %pad_maximum_fusion.3.refs_0_), channel_id=1, source_target_pairs={{0,1},{1,0},{2,3},{3,2},{4,5},{5,4},{6,7},{7,6},{8,9},{9,8},{10,11... | collective-permute-start | bytes 1228808 | tf_op jit(solution)/shard_map/ppermute | solution.py:905
  487.6 18.5 %collective-permute-start.71 = (bf16[160,1280]{1,0:T(8,128)(2,1)S(1)}, bf16[160,1280]{1,0:T(8,128)(2,1)S(1)}, u32[]{:S(2)}, u32[]{:S(2)}) collective-permute-start(bf16[160,1280]{1,0:T(8,128)(2,1)S(1)} %add_convert_fusion.7.refs_2_), channel_id=1, source_target_pairs={{0,1},{1,0},{2,3},{3,2},{4,5},{5,4},{6,7},{7,6},{8,9},{9,8},{10,11... | collective-permute-start | bytes 1228808 | tf_op jit(solution)/shard_map/ppermute | solution.py:905
  (80 other events, 882.4 us)
Sparse Core Ops, SparseCore 0:
  16.4 73.6 all-gather.3
  92.8 101.4 all-gather.5

commit v4 on v3

--- a/solution.py
+++ b/solution.py
@@ -744,7 +744,8 @@
     features = grad_heads.shape[0]
     tile = 512 if tokens % 512 == 0 else tokens
     share = width // (2 * depth)
-    cols = features + (extra[0].shape[1] if extra else 0)
+    slab = extra[0].shape[1] // 2 if extra else 0
+    cols = features + slab
 
     def kernel(x_ref, n_ref, g_ref, *refs):
         kept, sent, total = refs[-3:]
@@ -765,7 +766,9 @@
                 more = refs[0][...].astype(f32)
                 for v in refs[1:-3]:
                     more = more + v[...].astype(f32)
-                value = jnp.concatenate([value, more.astype(bf16)], axis=1)
+                more = more.astype(bf16)
+                more = jnp.concatenate([more[:, :slab], more[:, slab:]], axis=0)
+                value = jnp.concatenate([value, more], axis=1)
             part_ways(x_ref, value, kept, sent)
 
     return pl.pallas_call(
@@ -827,13 +830,14 @@
             def _(at=at):
                 for step in range(groups):
                     low = (at + step) % groups * slab
-                    outs[step][...] = value[:, low : low + slab]
+                    part = value[:, low : low + slab]
+                    outs[step][...] = jnp.concatenate([part[: rows // 2, :], part[rows // 2 :, :]], axis=1)
 
     return pl.pallas_call(
         kernel,
         in_specs=[smem()] + vmem(2),
         out_specs=vmem(groups),
-        out_shape=[sds((rows, slab), bf16)] * groups,
+        out_shape=[sds((rows // 2, 2 * slab), bf16)] * groups,
         compiler_params=params(),
         cost_estimate=cost(flops=0, bytes_accessed=6 * rows * half, transcendentals=0),
         name="out_grad_parts",

time: 527 us -> 521 us (0.989)
  local copies, waits for them, and re-layouts: 26.2 us -> 20.8 us
  transfers between devices with their start and end apart: 74 -> 74, of which waited for: 23 -> 22; matrix products, arithmetic and copies ran while one was open for 12% -> 10% of each run, Pallas kernels for 39% -> 39%
where the time goes in v4:
time: 521 us; the launch traced here: 512 us
  Pallas kernels  219 us (42%)
  waiting for transfers between devices  148 us (28%)
  starting transfers between devices  63.7 us (12%)
  other arithmetic  43.6 us (8%)
  local copies, waits for them, and re-layouts  20.8 us (4%)
  between operations  16.5 us (3%)
    ppermute x12, waiting for transfers between devices, over_z(): lax.ppermute(v, 'fsdp', [(i, (i + 4 * step) % shards) for i in range(shar...  54.2 us
    ppermute x16, waiting for transfers between devices, from_seq(): lax.ppermute(v, 'seq', [(i, (i - step) % groups) for i in range(groups)])  52.9 us
    pallas_call x3, Pallas kernels, feed(): pl.pallas_call(lambda *refs: feed_kernel(count, own, tile, refs), grid=(1...  47.1 us
    pallas_call x2, Pallas kernels, attend_back(): pl.pallas_call(lambda *refs: attend_back_kernel(span, 1.0 / math.sqrt(HEA...  35.3 us
    pallas_call x2, Pallas kernels, weight_grad(): pl.pallas_call(kernel, grid=(cols // tile,), in_specs=[smem()] + whole +...  27.6 us
    ppermute x12, starting transfers between devices, over_z(): lax.ppermute(v, 'fsdp', [(i, (i + 4 * step) % shards) for i in range(shar...  24.3 us
    pallas_call x2, Pallas kernels, project_back(): pl.pallas_call(kernel, grid=(count,), in_specs=[pl.BlockSpec(weight.shape...  20 us
    ppermute x16, starting transfers between devices, from_seq(): lax.ppermute(v, 'seq', [(i, (i - step) % groups) for i in range(groups)])  18.7 us
  transfers between devices with their start and end apart: 74, of which 22 were waited for; matrix products, arithmetic and copies ran while one was open for 10% of the time, Pallas kernels for 39%

profile of v4, /device:TPU:0, one launch (start us, length us, event | category | flops | bytes accessed | tf_op | source)
XLA Modules:
  0.0 511.9 jit_solution(1995289775488119690)
XLA Ops:
  10.1 2.8 pick.1
  19.3 3.0 collective-permute-start.4
  22.3 2.6 collective-permute-start.6
  28.5 8.3 %collective-permute-done.4.refs_2_ = bf16[192,960]{1,0:T(8,128)(2,1)S(1)} collective-permute-done((bf16[192,960]{1,0:T(8,128)(2,1)S(1)}, bf16[192,960]{1,0:T(8,128)(2,1)S(1)}, u32[]{:S(2)}, u32[]{:S(2)}) %collective-permute-start.4) | collective-permute-done | bytes 368672 | tf_op jit(solution)/shard_map/ppermute | solution.py:906
  36.8 20.5 %collective-permute-done.6.refs_4_ = bf16[192,960]{1,0:T(8,128)(2,1)S(1)} collective-permute-done((bf16[192,960]{1,0:T(8,128)(2,1)S(1)}, bf16[192,960]{1,0:T(8,128)(2,1)S(1)}, u32[]{:S(2)}, u32[]{:S(2)}) %collective-permute-start.6) | collective-permute-done | bytes 368672 | tf_op jit(solution)/shard_map/ppermute | solution.py:906
  62.4 25.7 %collective-permute-done.7.refs_1_.refs_2_ = bf16[512,1280]{1,0:T(8,128)(2,1)} collective-permute-done((bf16[512,1280]{1,0:T(8,128)(2,1)S(1)}, bf16[512,1280]{1,0:T(8,128)(2,1)}, u32[]{:S(2)}, u32[]{:S(2)}) %collective-permute-start.7) | collective-permute-done | bytes 1310752 | tf_op jit(solution)/shard_map/ppermute | solution.py:909
  91.7 4.9 collective-permute-done.10.refs_7_
  96.6 9.6 %collective-permute-done.8.refs_5_ = bf16[192,960]{1,0:T(8,128)(2,1)S(1)} collective-permute-done((bf16[192,960]{1,0:T(8,128)(2,1)S(1)}, bf16[192,960]{1,0:T(8,128)(2,1)S(1)}, u32[]{:S(2)}, u32[]{:S(2)}) %collective-permute-start.8) | collective-permute-done | bytes 368672 | tf_op jit(solution)/shard_map/ppermute | solution.py:903
  109.3 3.7 place.1
  113.1 14.2 %project.1 = (bf16[2048,1280]{1,0:T(8,128)(2,1)}, bf16[960,2048]{1,0:T(8,128)(2,1)}, f32[16,1280]{1,0:T(8,128)}) custom-call(s32[1]{0:T(128)} %bitcast.5.rank_ref, bf16[16,16,960]{2,1,0:T(8,128)(2,1)} %get-tuple-element.143.small_ref, bf16[1280,960]{1,0:T(8,128)(2,1)} %bitcast.134, bf16[512,1280]{1,0:T(8,128)(2,1)} %bitcast.123, ...), custom_call_target="tpu_custom_call" | custom-call | flops 5033164800 | bytes 18186240 | tf_op jit(solution)/shard_map/project/pallas_call | solution.py:334
  127.8 12.0 %collective-permute-done.15.refs_2_.refs_7_.refs_9_ = bf16[512,1280]{1,0:T(8,128)(2,1)} collective-permute-done((bf16[512,1280]{1,0:T(8,128)(2,1)S(1)}, bf16[512,1280]{1,0:T(8,128)(2,1)}, u32[]{:S(2)}, u32[]{:S(2)}) %collective-permute-start.15) | collective-permute-done | bytes 1310752 | tf_op jit(solution)/shard_map/ppermute | solution.py:909
  141.6 9.0 %attend.2 = (bf16[2,160,512]{2,1,0:T(8,128)(2,1)}, bf16[1,2,160,512]{3,2,1,0:T(8,128)(2,1)}, f32[4,1,1024]{2,1,0:T(1,128)}, f32[4,1,1024]{2,1,0:T(1,128)}) custom-call(bf16[960,2048]{1,0:T(8,128)(2,1)} %get-tuple-element.154.refs_0_.refs_1_.refs_2_, bf16[960,2048]{1,0:T(8,128)(2,1)} %get-tuple-element.154.refs_0_.refs_1_.refs_2_, ...), custom_call_target="tpu_custom_call" | custom-call | flops 8388608000 | bytes 2949120 | tf_op jit(solution)/shard_map/attend/pallas_call | solution.py:110
  152.6 9.5 %attend.3 = (bf16[2,160,512]{2,1,0:T(8,128)(2,1)}, bf16[1,2,160,512]{3,2,1,0:T(8,128)(2,1)}, f32[4,1,1024]{2,1,0:T(1,128)}, f32[4,1,1024]{2,1,0:T(1,128)}) custom-call(bf16[960,2048]{1,0:T(8,128)(2,1)} %get-tuple-element.154.refs_0_.refs_1_.refs_2_, bf16[960,2048]{1,0:T(8,128)(2,1)} %get-tuple-element.154.refs_0_.refs_1_.refs_2_, ...), custom_call_target="tpu_custom_call" | custom-call | flops 8388608000 | bytes 2949120 | tf_op jit(solution)/shard_map/attend/pallas_call | solution.py:110
  166.8 5.7 %collective-permute-done.18 = bf16[2,160,512]{2,1,0:T(8,128)(2,1)S(1)} collective-permute-done((bf16[2,160,512]{2,1,0:T(8,128)(2,1)}, bf16[2,160,512]{2,1,0:T(8,128)(2,1)S(1)}, u32[]{:S(2)}, u32[]{:S(2)}) %collective-permute-start.18) | collective-permute-done | bytes 327712 | tf_op jit(solution)/shard_map/ppermute | solution.py:909
  173.2 2.6 maximum_select_fusion.w_ref
  176.6 6.6 %merge.1 = (bf16[1280,512]{1,0:T(8,128)(2,1)}, f32[512,1280]{1,0:T(8,128)}, bf16[256,1280]{1,0:T(8,128)(2,1)}, bf16[256,1280]{1,0:T(8,128)(2,1)}) custom-call(s32[4]{0:T(128)} %pad_add_fusion.1.slots_ref, bf16[512,1280]{1,0:T(8,128)(2,1)} %bitcast.124, bf16[1280,1280]{1,0:T(8,128)(2,1)} %maximum_select_fusion.w_ref, ...), custom_call_target="tpu_custom_call" | custom-call | flops 1677721600 | bytes 11141120 | tf_op jit(solution)/shard_map/merge/pallas_call | solution.py:610
  187.3 7.0 %all-gather.6.cloned.1.call-done = bf16[2560,1280]{1,0:T(8,128)(2,1)} async-done(((bf16[320,1280]{1,0:T(8,128)(2,1)}), bf16[2560,1280]{1,0:T(8,128)(2,1)}) %all-gather.6.cloned.1.call-update) | async-done | bytes 6553616 | tf_op jit(solution)/shard_map/all_gather | solution.py:954
  194.4 21.8 %feed.3 = (bf16[1024,1280]{1,0:T(8,128)(2,1)}, bf16[1024,1280]{1,0:T(8,128)(2,1)}, f32[512,1280]{1,0:T(8,128)}, bf16[512,1280]{1,0:T(8,128)(2,1)}, f32[512,1280]...) custom-call(bf16[256,1280]{1,0:T(8,128)(2,1)} %get-tuple-element.179.refs_0_, ...), custom_call_target="tpu_custom_call" | custom-call | flops 3355443200 | bytes 6881280 | tf_op jit(solution)/shard_map/feed/pallas_call | solution.py:272
  219.2 12.5 %feed.4 = (bf16[512,1280]{1,0:T(8,128)(2,1)}, bf16[512,1280]{1,0:T(8,128)(2,1)}, f32[256,1280]{1,0:T(8,128)}, bf16[256,1280]{1,0:T(8,128)(2,1)}, f32[256,1280]{1...) custom-call(bf16[256,1280]{1,0:T(8,128)(2,1)} %copy-done.12, bf16[256,1280]{1,0:T(8,128)(2,1)} %copy-done.13, ...), custom_call_target="tpu_custom_call" | custom-call | flops 1677721600 | bytes 4259840 | tf_op jit(solution)/shard_map/feed/pallas_call | solution.py:272
  234.0 2.3 add_convert_fusion.5
  237.2 12.8 %feed.5 = (bf16[512,1280]{1,0:T(8,128)(2,1)}, bf16[512,1280]{1,0:T(8,128)(2,1)}, f32[256,1280]{1,0:T(8,128)}, bf16[256,1280]{1,0:T(8,128)(2,1)}, f32[256,1280]{1...) custom-call(bf16[256,1280]{1,0:T(8,128)(2,1)} %collective-permute-done.27.refs_0_.refs_6_, ...), custom_call_target="tpu_custom_call" | custom-call | flops 1677721600 | bytes 4259840 | tf_op jit(solution)/shard_map/feed/pallas_call | solution.py:272
  253.9 3.2 convert_add_fusion.4.near_ref
  257.1 13.9 %weight_grad.2 = (bf16[4,160,1280]{2,1,0:T(8,128)(2,1)}, bf16[4,160,1280]{2,1,0:T(8,128)(2,1)}) custom-call(s32[1]{0:T(128)} %bitcast.43.x_ref, bf16[256,1280]{1,0:T(8,128)(2,1)} %get-tuple-element.179.refs_0_, bf16[256,1280]{1,0:T(8,128)(2,1)} %get-tuple-element.160.refs_1_, bf16[256,1280]{1,0:T(8,128)(2,1)} %copy-done.10, bf16[256,1280]{1,0:T(8,128)(2,1)} %copy-done.11, ...), custom_call_target="tpu_custom_call" | custom-call | flops 1677721600 | bytes 3440640 | tf_op jit(solution)/shard_map/weight_grad/pallas_call | solution.py:727
  272.2 9.5 %collective-permute-done.34.refs_1_ = bf16[256,1280]{1,0:T(8,128)(2,1)S(1)} collective-permute-done((bf16[256,1280]{1,0:T(8,128)(2,1)S(1)}, bf16[256,1280]{1,0:T(8,128)(2,1)S(1)}, u32[]{:S(2)}, u32[]{:S(2)}) %collective-permute-start.34) | collective-permute-done | bytes 655392 | tf_op jit(solution)/shard_map/ppermute | solution.py:909
  282.5 10.8 %turn.1 = (f32[512,1280]{1,0:T(8,128)}, bf16[512,1280]{1,0:T(8,128)(2,1)}, f32[4,1280]{1,0:T(4,128)}, bf16[2,160,512]{2,1,0:T(8,128)(2,1)}, bf16[2,160,512]{2,1,...) custom-call(s32[4]{0:T(128)} %pad_add_fusion.4.slots_ref, f32[512,1280]{1,0:T(8,128)} %get-tuple-element.158.after_ref, ...), custom_call_target="tpu_custom_call" | custom-call | flops 419430400 | bytes 3440640 | tf_op jit(solution)/shard_map/turn/pallas_call | solution.py:670
  295.8 13.7 %weight_grad.3 = (bf16[4,160,1280]{2,1,0:T(8,128)(2,1)}, bf16[4,160,1280]{2,1,0:T(8,128)(2,1)}) custom-call(s32[1]{0:T(128)} %bitcast.43.x_ref, bf16[1024,1280]{1,0:T(8,128)(2,1)} %get-tuple-element.189.refs_0_, bf16[512,1280]{1,0:T(8,128)(2,1)} %get-tuple-element.190.refs_1_, bf16[512,1280]{1,0:T(8,128)(2,1)} %get-tuple-element.191.refs_2_, ...), custom_call_target="tpu_custom_call" | custom-call | flops 1677721600 | bytes 3440640 | tf_op jit(solution)/shard_map/weight_grad/pallas_call | solution.py:727
  309.7 6.0 %out_grad_halves.1 = (bf16[1280,640]{1,0:T(8,128)(2,1)}, bf16[1280,640]{1,0:T(8,128)(2,1)}) custom-call(s32[1]{0:T(128)} %bitcast.7.core_ref, bf16[1280,512]{1,0:T(8,128)(2,1)} %get-tuple-element.194.m_ref, bf16[512,1280]{1,0:T(8,128)(2,1)} %get-tuple-element.197.g_ref), custom_call_target="tpu_custom_call" | custom-call | flops 419430400 | bytes 1638400 | tf_op jit(solution)/shard_map/out_grad_halves/pallas_call | solution.py:808
  319.6 4.0 out_grad_parts.1
  325.4 8.5 %collective-permute-start.46 = (bf16[160,1280]{1,0:T(8,128)(2,1)S(1)}, bf16[160,1280]{1,0:T(8,128)(2,1)S(1)}, u32[]{:S(2)}, u32[]{:S(2)}) collective-permute-start(bf16[160,1280]{1,0:T(8,128)(2,1)S(1)} %get-tuple-element.268), channel_id=1, source_target_pairs={{0,24},{2,26},{4,28},{6,30},{8,0},{10,2},{12,4},{14,6},{16,8},{18,... | collective-permute-start | bytes 1228808 | tf_op jit(solution)/shard_map/ppermute | solution.py:906
  334.7 17.6 %attend_back.2 = bf16[3,160,2048]{2,1,0:T(8,128)(2,1)} custom-call(bf16[960,2048]{1,0:T(8,128)(2,1)} %get-tuple-element.154.refs_0_.refs_1_.refs_2_, bf16[960,2048]{1,0:T(8,128)(2,1)} %get-tuple-element.154.refs_0_.refs_1_.refs_2_, bf16[960,2048]{1,0:T(8,128)(2,1)} %get-tuple-element.154.refs_0_.refs_1_.refs_2_, bf16[32,1024]{1,0:T(8,128)(2,1)} %bitcast.147, ...), custom_call_target="tpu_custom_call" | custom-call | flops 4194304000 | bytes 1474560 | tf_op jit(solution)/shard_map/attend_back/pallas_call | solution.py:186
  353.3 9.0 %head_grad.2 = (bf16[4,160,800]{2,1,0:T(8,128)(2,1)}, bf16[4,160,800]{2,1,0:T(8,128)(2,1)}) custom-call(s32[1]{0:T(128)} %bitcast.43.x_ref, bf16[2048,1280]{1,0:T(8,128)(2,1)} %get-tuple-element.166.n_ref, bf16[480,2048]{1,0:T(8,128)(2,1)} %bitcast.131, bf16[640,640]{1,0:T(8,128)(2,1)} %get-tuple-element.203.refs_0_, bf16[640,640]{1,0:T(8,128)(2,1)} %copy-done.28), custom_call_target="tpu_custom_call" | custom-call | flops 629145600 | bytes 1802240 | tf_op jit(solution)/shard_map/head_grad/pallas_call | solution.py:774
  363.8 5.4 %collective-permute-done.45 = bf16[160,1280]{1,0:T(8,128)(2,1)S(1)} collective-permute-done((bf16[160,1280]{1,0:T(8,128)(2,1)S(1)}, bf16[160,1280]{1,0:T(8,128)(2,1)S(1)}, u32[]{:S(2)}, u32[]{:S(2)}) %collective-permute-start.45) | collective-permute-done | bytes 409632 | tf_op jit(solution)/shard_map/ppermute | solution.py:906
  373.1 2.7 collective-permute-start.52
  375.9 2.3 collective-permute-start.51
  381.0 17.7 %attend_back.3 = bf16[3,160,2048]{2,1,0:T(8,128)(2,1)} custom-call(bf16[960,2048]{1,0:T(8,128)(2,1)} %get-tuple-element.154.refs_0_.refs_1_.refs_2_, bf16[960,2048]{1,0:T(8,128)(2,1)} %get-tuple-element.154.refs_0_.refs_1_.refs_2_, bf16[960,2048]{1,0:T(8,128)(2,1)} %get-tuple-element.154.refs_0_.refs_1_.refs_2_, bf16[32,1024]{1,0:T(8,128)(2,1)} %bitcast.148, ...), custom_call_target="tpu_custom_call" | custom-call | flops 4194304000 | bytes 1474560 | tf_op jit(solution)/shard_map/attend_back/pallas_call | solution.py:186
  398.7 7.6 %head_grad.3 = (bf16[4,160,480]{2,1,0:T(8,128)(2,1)}, bf16[4,160,480]{2,1,0:T(8,128)(2,1)}) custom-call(s32[1]{0:T(128)} %bitcast.43.x_ref, bf16[2048,1280]{1,0:T(8,128)(2,1)} %get-tuple-element.166.n_ref, bf16[480,2048]{1,0:T(8,128)(2,1)} %bitcast.128), custom_call_target="tpu_custom_call" | custom-call | flops 629145600 | bytes 1802240 | tf_op jit(solution)/shard_map/head_grad/pallas_call | solution.py:774
  413.3 10.1 %project_back.2 = (f32[512,1280]{1,0:T(8,128)}, bf16[512,1280]{1,0:T(8,128)(2,1)}, f32[8,1280]{1,0:T(8,128)}, f32[8,960]{1,0:T(8,128)}) custom-call(bf16[1280,960]{1,0:T(8,128)(2,1)} %bitcast.135, bf16[480,2048]{1,0:T(8,128)(2,1)} %bitcast.132, bf16[480,2048]{1,0:T(8,128)(2,1)} %bitcast.129, bf16[512,1280]{1,0:T(8,128)(2,1)} %collective-permute-done.7.refs_1_.refs_2_, ...), custom_call_target="tpu_custom_call" | custom-call | flops 629145600 | bytes 3235840 | tf_op jit(solution)/shard_map/project_back/pallas_call | solution.py:407
  426.9 2.3 collective-permute-start.62
  429.4 3.0 fusion.10
  435.0 9.9 %project_back.3 = (f32[512,1280]{1,0:T(8,128)}, bf16[512,1280]{1,0:T(8,128)(2,1)}, f32[8,1280]{1,0:T(8,128)}, f32[8,960]{1,0:T(8,128)}) custom-call(bf16[1280,960]{1,0:T(8,128)(2,1)} %bitcast.136, bf16[480,2048]{1,0:T(8,128)(2,1)} %bitcast.133, bf16[480,2048]{1,0:T(8,128)(2,1)} %bitcast.130, bf16[512,1280]{1,0:T(8,128)(2,1)} %bitcast.125, ...), custom_call_target="tpu_custom_call" | custom-call | flops 629145600 | bytes 3235840 | tf_op jit(solution)/shard_map/project_back/pallas_call | solution.py:407
  445.0 18.7 %collective-permute-done.63 = bf16[160,1280]{1,0:T(8,128)(2,1)} collective-permute-done((bf16[160,1280]{1,0:T(8,128)(2,1)}, bf16[160,1280]{1,0:T(8,128)(2,1)}, u32[]{:S(2)}, u32[]{:S(2)}) %collective-permute-start.63) | collective-permute-done | bytes 409632 | tf_op jit(solution)/shard_map/ppermute | solution.py:906
  471.1 3.7 multiply_reduce_fusion
  475.4 4.0 collective-permute-done.67
  479.5 2.4 collective-permute-start.68
  482.7 2.9 collective-permute-done.68
  488.5 4.9 collective-permute-done.69
  496.8 2.6 finish_heads.1
  501.1 3.5 finish_feed.1
  (350 shorter events, 98.9 us)
Async XLA Ops:
  7.2 133.9 %all-gather.4.cloned.1.call-start = ((), (), s32[]{:S(2)}) async-start(), calls=%async_computation | async-start | bytes 1843200 | tf_op jit(solution)/shard_map/all_gather | solution.py:954
  16.3 178.1 %all-gather.6.cloned.1.call-start = ((), (), s32[]{:S(2)}) async-start(), calls=%async_computation.1 | async-start | bytes 7372800 | tf_op jit(solution)/shard_map/all_gather | solution.py:954
  19.3 17.5 %collective-permute-start.4 = (bf16[192,960]{1,0:T(8,128)(2,1)S(1)}, bf16[192,960]{1,0:T(8,128)(2,1)S(1)}, u32[]{:S(2)}, u32[]{:S(2)}) collective-permute-start(bf16[192,960]{1,0:T(8,128)(2,1)S(1)} %maximum_select_fusion.2.refs_0_), channel_id=1, source_target_pairs={{0,8},{2,10},{4,12},{6,14},{8,16},{10,18},{12,20},{14,22},{16,24},... | collective-permute-start | bytes 1105928 | tf_op jit(solution)/shard_map/ppermute | solution.py:906
  22.3 35.0 %collective-permute-start.6 = (bf16[192,960]{1,0:T(8,128)(2,1)S(1)}, bf16[192,960]{1,0:T(8,128)(2,1)S(1)}, u32[]{:S(2)}, u32[]{:S(2)}) collective-permute-start(bf16[192,960]{1,0:T(8,128)(2,1)S(1)} %maximum_select_fusion.2.refs_0_), channel_id=1, source_target_pairs={{0,16},{2,18},{4,20},{6,22},{8,24},{10,26},{12,28},{14,30},{16,0},... | collective-permute-start | bytes 1105928 | tf_op jit(solution)/shard_map/ppermute | solution.py:906
  24.9 32.4 %collective-permute-start.9 = (bf16[192,960]{1,0:T(8,128)(2,1)S(1)}, bf16[192,960]{1,0:T(8,128)(2,1)S(1)}, u32[]{:S(2)}, u32[]{:S(2)}) collective-permute-start(bf16[192,960]{1,0:T(8,128)(2,1)S(1)} %maximum_select_fusion.2.refs_0_), channel_id=1, source_target_pairs={{0,24},{2,26},{4,28},{6,30},{8,0},{10,2},{12,4},{14,6},{16,8},{18,... | collective-permute-start | bytes 1105928 | tf_op jit(solution)/shard_map/ppermute | solution.py:906
  57.3 30.8 %collective-permute-start.7 = (bf16[512,1280]{1,0:T(8,128)(2,1)S(1)}, bf16[512,1280]{1,0:T(8,128)(2,1)}, u32[]{:S(2)}, u32[]{:S(2)}) collective-permute-start(bf16[512,1280]{1,0:T(8,128)(2,1)S(1)} %bitcast.126), channel_id=1, source_target_pairs={{0,1},{1,0},{2,3},{3,2},{4,5},{5,4},{6,7},{7,6},{8,9},{9,8},{10,11... | collective-permute-start | bytes 3932168 | tf_op jit(solution)/shard_map/ppermute | solution.py:909
  58.9 32.7 %collective-permute-start.3 = (bf16[192,960]{1,0:T(8,128)(2,1)S(1)}, bf16[192,960]{1,0:T(8,128)(2,1)S(1)}, u32[]{:S(2)}, u32[]{:S(2)}) collective-permute-start(bf16[192,960]{1,0:T(8,128)(2,1)S(1)} %maximum_select_fusion.2.refs_0_), channel_id=1, source_target_pairs={{0,4},{2,6},{4,0},{6,2},{8,12},{10,14},{12,8},{14,10},{16,20},{18,... | collective-permute-start | bytes 1105928 | tf_op jit(solution)/shard_map/ppermute | solution.py:903
  60.4 31.2 %collective-permute-start.5 = (bf16[192,960]{1,0:T(8,128)(2,1)S(1)}, bf16[192,960]{1,0:T(8,128)(2,1)S(1)}, u32[]{:S(2)}, u32[]{:S(2)}) collective-permute-start(bf16[192,960]{1,0:T(8,128)(2,1)S(1)} %collective-permute-done.4.refs_2_), channel_id=1, source_target_pairs={{0,4},{2,6},{4,0},{6,2},{8,12},{10,14},{12,8},{14,10},{16,20},{18,... | collective-permute-start | bytes 1105928 | tf_op jit(solution)/shard_map/ppermute | solution.py:903
  61.0 35.6 %collective-permute-start.10 = (bf16[192,960]{1,0:T(8,128)(2,1)S(1)}, bf16[192,960]{1,0:T(8,128)(2,1)S(1)}, u32[]{:S(2)}, u32[]{:S(2)}) collective-permute-start(bf16[192,960]{1,0:T(8,128)(2,1)S(1)} %collective-permute-done.9.refs_6_), channel_id=1, source_target_pairs={{0,4},{2,6},{4,0},{6,2},{8,12},{10,14},{12,8},{14,10},{16,20},{18,... | collective-permute-start | bytes 1105928 | tf_op jit(solution)/shard_map/ppermute | solution.py:903
  88.1 18.0 %collective-permute-start.8 = (bf16[192,960]{1,0:T(8,128)(2,1)S(1)}, bf16[192,960]{1,0:T(8,128)(2,1)S(1)}, u32[]{:S(2)}, u32[]{:S(2)}) collective-permute-start(bf16[192,960]{1,0:T(8,128)(2,1)S(1)} %collective-permute-done.6.refs_4_), channel_id=1, source_target_pairs={{0,4},{2,6},{4,0},{6,2},{8,12},{10,14},{12,8},{14,10},{16,20},{18,... | collective-permute-start | bytes 1105928 | tf_op jit(solution)/shard_map/ppermute | solution.py:903
  108.4 31.4 %collective-permute-start.15 = (bf16[512,1280]{1,0:T(8,128)(2,1)S(1)}, bf16[512,1280]{1,0:T(8,128)(2,1)}, u32[]{:S(2)}, u32[]{:S(2)}) collective-permute-start(bf16[512,1280]{1,0:T(8,128)(2,1)S(1)} %bitcast_select_fusion.refs_4_.refs_5_.live_ref.refs_3_), channel_id=1, source_target_pairs={{0,1},{1,0},{2,3},{3,2},{4,5},{5,4},{6,7},{7,6},{8,9},{9,8},{10,11... | collective-permute-start | bytes 3932168 | tf_op jit(solution)/shard_map/ppermute | solution.py:909
  127.3 25.3 %collective-permute-start.14 = (bf16[512,1280]{1,0:T(8,128)(2,1)S(1)}, bf16[512,1280]{1,0:T(8,128)(2,1)S(1)}, u32[]{:S(2)}, u32[]{:S(2)}) collective-permute-start(bf16[512,1280]{1,0:T(8,128)(2,1)S(1)} %bitcast_select_fusion.refs_4_.refs_5_.live_ref.refs_3_), channel_id=1, source_target_pairs={{0,2},{2,0},{4,6},{6,4},{8,10},{10,8},{12,14},{14,12},{16,18},{18,... | collective-permute-start | bytes 3932168 | tf_op jit(solution)/shard_map/ppermute | solution.py:900
  139.8 12.8 %collective-permute-start.16 = (bf16[512,1280]{1,0:T(8,128)(2,1)}, bf16[512,1280]{1,0:T(8,128)(2,1)}, u32[]{:S(2)}, u32[]{:S(2)}) collective-permute-start(bf16[512,1280]{1,0:T(8,128)(2,1)} %collective-permute-done.15.refs_2_.refs_7_.refs_9_), channel_id=1, source_target_pairs={{0,2},{2,0},{4,6},{6,4},{8,10},{10,8},{12,14},{14,12},{16,18},{18,... | collective-permute-start | bytes 3932168 | tf_op jit(solution)/shard_map/ppermute | solution.py:900
  141.1 32.1 %collective-permute-start.1 = (bf16[1280,640]{1,0:T(8,128)(2,1)}, bf16[1280,640]{1,0:T(8,128)(2,1)S(1)}, u32[]{:S(2)}, u32[]{:S(2)}) collective-permute-start(bf16[1280,640]{1,0:T(8,128)(2,1)} %bitcast.139), channel_id=1, source_target_pairs={{0,2},{2,0},{4,6},{6,4},{8,10},{10,8},{12,14},{14,12},{16,18},{18,... | collective-permute-start | bytes 4915208 | tf_op jit(solution)/shard_map/ppermute | solution.py:900
  150.6 13.3 %collective-permute-start.17 = (bf16[2,160,512]{2,1,0:T(8,128)(2,1)}, bf16[2,160,512]{2,1,0:T(8,128)(2,1)S(1)}, u32[]{:S(2)}, u32[]{:S(2)}) collective-permute-start(bf16[2,160,512]{2,1,0:T(8,128)(2,1)} %bitcast.160), channel_id=1, source_target_pairs={{0,1},{1,0},{2,3},{3,2},{4,5},{5,4},{6,7},{7,6},{8,9},{9,8},{10,11... | collective-permute-start | bytes 983048 | tf_op jit(solution)/shard_map/ppermute | solution.py:909
  152.6 23.2 %collective-permute-start.19 = (bf16[1,160,512]{2,1,0:T(8,128)(2,1)S(1)}, bf16[1,160,512]{2,1,0:T(8,128)(2,1)S(1)}, u32[]{:S(2)}, u32[]{:S(2)}) collective-permute-start(bf16[1,160,512]{2,1,0:T(8,128)(2,1)S(1)} %get-tuple-element.281), channel_id=1, source_target_pairs={{0,2},{2,0},{4,6},{6,4},{8,10},{10,8},{12,14},{14,12},{16,18},{18,... | collective-permute-start | bytes 491528 | tf_op jit(solution)/shard_map/ppermute | solution.py:900
  162.1 10.4 %collective-permute-start.18 = (bf16[2,160,512]{2,1,0:T(8,128)(2,1)}, bf16[2,160,512]{2,1,0:T(8,128)(2,1)S(1)}, u32[]{:S(2)}, u32[]{:S(2)}) collective-permute-start(bf16[2,160,512]{2,1,0:T(8,128)(2,1)} %bitcast.161), channel_id=1, source_target_pairs={{0,1},{1,0},{2,3},{3,2},{4,5},{5,4},{6,7},{7,6},{8,9},{9,8},{10,11... | collective-permute-start | bytes 983048 | tf_op jit(solution)/shard_map/ppermute | solution.py:909
  164.6 11.2 %collective-permute-start.21 = (bf16[1,160,512]{2,1,0:T(8,128)(2,1)S(1)}, bf16[1,160,512]{2,1,0:T(8,128)(2,1)S(1)}, u32[]{:S(2)}, u32[]{:S(2)}) collective-permute-start(bf16[1,160,512]{2,1,0:T(8,128)(2,1)S(1)} %get-tuple-element.277), channel_id=1, source_target_pairs={{0,2},{2,0},{4,6},{6,4},{8,10},{10,8},{12,14},{14,12},{16,18},{18,... | collective-permute-start | bytes 491528 | tf_op jit(solution)/shard_map/ppermute | solution.py:900
  183.7 32.4 %collective-permute-start.28 = (bf16[256,1280]{1,0:T(8,128)(2,1)}, bf16[256,1280]{1,0:T(8,128)(2,1)S(1)}, u32[]{:S(2)}, u32[]{:S(2)}) collective-permute-start(bf16[256,1280]{1,0:T(8,128)(2,1)} %get-tuple-element.179.refs_0_), channel_id=1, source_target_pairs={{0,1},{1,0},{2,3},{3,2},{4,5},{5,4},{6,7},{7,6},{8,9},{9,8},{10,11... | collective-permute-start | bytes 1966088 | tf_op jit(solution)/shard_map/ppermute | solution.py:909
  187.0 29.2 %collective-permute-start.27 = (bf16[256,1280]{1,0:T(8,128)(2,1)}, bf16[256,1280]{1,0:T(8,128)(2,1)}, u32[]{:S(2)}, u32[]{:S(2)}) collective-permute-start(bf16[256,1280]{1,0:T(8,128)(2,1)} %get-tuple-element.160.refs_1_), channel_id=1, source_target_pairs={{0,1},{1,0},{2,3},{3,2},{4,5},{5,4},{6,7},{7,6},{8,9},{9,8},{10,11... | collective-permute-start | bytes 1966088 | tf_op jit(solution)/shard_map/ppermute | solution.py:909
  232.2 21.7 %collective-permute-start.26 = (bf16[512,1280]{1,0:T(8,128)(2,1)}, bf16[512,1280]{1,0:T(8,128)(2,1)}, u32[]{:S(2)}, u32[]{:S(2)}) collective-permute-start(bf16[512,1280]{1,0:T(8,128)(2,1)} %get-tuple-element.169), channel_id=1, source_target_pairs={{0,2},{2,0},{4,6},{6,4},{8,10},{10,8},{12,14},{14,12},{16,18},{18,... | collective-permute-start | bytes 3932168 | tf_op jit(solution)/shard_map/ppermute | solution.py:900
  250.4 21.9 %collective-permute-start.33 = (bf16[256,1280]{1,0:T(8,128)(2,1)}, bf16[256,1280]{1,0:T(8,128)(2,1)S(1)}, u32[]{:S(2)}, u32[]{:S(2)}) collective-permute-start(bf16[256,1280]{1,0:T(8,128)(2,1)} %add_convert_fusion.5), channel_id=1, source_target_pairs={{0,1},{1,0},{2,3},{3,2},{4,5},{5,4},{6,7},{7,6},{8,9},{9,8},{10,11... | collective-permute-start | bytes 1966088 | tf_op jit(solution)/shard_map/ppermute | solution.py:909
  252.4 29.3 %collective-permute-start.34 = (bf16[256,1280]{1,0:T(8,128)(2,1)S(1)}, bf16[256,1280]{1,0:T(8,128)(2,1)S(1)}, u32[]{:S(2)}, u32[]{:S(2)}) collective-permute-start(bf16[256,1280]{1,0:T(8,128)(2,1)S(1)} %add_convert_fusion.4), channel_id=1, source_target_pairs={{0,1},{1,0},{2,3},{3,2},{4,5},{5,4},{6,7},{7,6},{8,9},{9,8},{10,11... | collective-permute-start | bytes 1966088 | tf_op jit(solution)/shard_map/ppermute | solution.py:909
  271.0 48.1 %collective-permute-start.35 = (bf16[4,160,1280]{2,1,0:T(8,128)(2,1)}, bf16[4,160,1280]{2,1,0:T(8,128)(2,1)S(1)}, u32[]{:S(2)}, u32[]{:S(2)}) collective-permute-start(bf16[4,160,1280]{2,1,0:T(8,128)(2,1)} %get-tuple-element.183), channel_id=1, source_target_pairs={{0,4},{2,6},{4,0},{6,2},{8,12},{10,14},{12,8},{14,10},{16,20},{18,... | collective-permute-start | bytes 4915208 | tf_op jit(solution)/shard_map/ppermute | solution.py:903
  293.3 16.3 %collective-permute-start.36 = (bf16[2,160,512]{2,1,0:T(8,128)(2,1)}, bf16[2,160,512]{2,1,0:T(8,128)(2,1)S(1)}, u32[]{:S(2)}, u32[]{:S(2)}) collective-permute-start(bf16[2,160,512]{2,1,0:T(8,128)(2,1)} %get-tuple-element.195), channel_id=1, source_target_pairs={{0,1},{1,0},{2,3},{3,2},{4,5},{5,4},{6,7},{7,6},{8,9},{9,8},{10,11... | collective-permute-start | bytes 983048 | tf_op jit(solution)/shard_map/ppermute | solution.py:909
  294.8 14.9 %collective-permute-start.37 = (bf16[2,160,512]{2,1,0:T(8,128)(2,1)}, bf16[2,160,512]{2,1,0:T(8,128)(2,1)S(1)}, u32[]{:S(2)}, u32[]{:S(2)}) collective-permute-start(bf16[2,160,512]{2,1,0:T(8,128)(2,1)} %get-tuple-element.196), channel_id=1, source_target_pairs={{0,1},{1,0},{2,3},{3,2},{4,5},{5,4},{6,7},{7,6},{8,9},{9,8},{10,11... | collective-permute-start | bytes 983048 | tf_op jit(solution)/shard_map/ppermute | solution.py:909
  317.9 52.0 %collective-permute-start.47 = (bf16[4,160,1280]{2,1,0:T(8,128)(2,1)}, bf16[4,160,1280]{2,1,0:T(8,128)(2,1)}, u32[]{:S(2)}, u32[]{:S(2)}) collective-permute-start(bf16[4,160,1280]{2,1,0:T(8,128)(2,1)} %get-tuple-element.192), channel_id=1, source_target_pairs={{0,4},{2,6},{4,0},{6,2},{8,12},{10,14},{12,8},{14,10},{16,20},{18,... | collective-permute-start | bytes 4915208 | tf_op jit(solution)/shard_map/ppermute | solution.py:903
  318.5 15.4 %collective-permute-start.41 = (bf16[320,512]{1,0:T(8,128)(2,1)}, bf16[320,512]{1,0:T(8,128)(2,1)}, u32[]{:S(2)}, u32[]{:S(2)}) collective-permute-start(bf16[320,512]{1,0:T(8,128)(2,1)} %get-tuple-element.202), channel_id=1, source_target_pairs={{0,2},{2,0},{4,6},{6,4},{8,10},{10,8},{12,14},{14,12},{16,18},{18,... | collective-permute-start | bytes 983048 | tf_op jit(solution)/shard_map/ppermute | solution.py:900
  319.1 14.8 %collective-permute-start.40 = (bf16[2,160,512]{2,1,0:T(8,128)(2,1)}, bf16[2,160,512]{2,1,0:T(8,128)(2,1)}, u32[]{:S(2)}, u32[]{:S(2)}) collective-permute-start(bf16[2,160,512]{2,1,0:T(8,128)(2,1)} %copy-done.52), channel_id=1, source_target_pairs={{0,2},{2,0},{4,6},{6,4},{8,10},{10,8},{12,14},{14,12},{16,18},{18,... | collective-permute-start | bytes 983048 | tf_op jit(solution)/shard_map/ppermute | solution.py:900
  323.7 28.7 %collective-permute-start.42 = (bf16[640,640]{1,0:T(8,128)(2,1)}, bf16[640,640]{1,0:T(8,128)(2,1)S(1)}, u32[]{:S(2)}, u32[]{:S(2)}) collective-permute-start(bf16[640,640]{1,0:T(8,128)(2,1)} %get-tuple-element.200), channel_id=1, source_target_pairs={{0,1},{1,0},{2,3},{3,2},{4,5},{5,4},{6,7},{7,6},{8,9},{9,8},{10,11... | collective-permute-start | bytes 2457608 | tf_op jit(solution)/shard_map/ppermute | solution.py:909
  325.4 38.4 %collective-permute-start.46 = (bf16[160,1280]{1,0:T(8,128)(2,1)S(1)}, bf16[160,1280]{1,0:T(8,128)(2,1)S(1)}, u32[]{:S(2)}, u32[]{:S(2)}) collective-permute-start(bf16[160,1280]{1,0:T(8,128)(2,1)S(1)} %get-tuple-element.268), channel_id=1, source_target_pairs={{0,24},{2,26},{4,28},{6,30},{8,0},{10,2},{12,4},{14,6},{16,8},{18,... | collective-permute-start | bytes 1228808 | tf_op jit(solution)/shard_map/ppermute | solution.py:906
  333.9 35.3 %collective-permute-start.45 = (bf16[160,1280]{1,0:T(8,128)(2,1)S(1)}, bf16[160,1280]{1,0:T(8,128)(2,1)S(1)}, u32[]{:S(2)}, u32[]{:S(2)}) collective-permute-start(bf16[160,1280]{1,0:T(8,128)(2,1)S(1)} %get-tuple-element.269), channel_id=1, source_target_pairs={{0,16},{2,18},{4,20},{6,22},{8,24},{10,26},{12,28},{14,30},{16,0},... | collective-permute-start | bytes 1228808 | tf_op jit(solution)/shard_map/ppermute | solution.py:906
  333.9 35.3 %collective-permute-start.44 = (bf16[160,1280]{1,0:T(8,128)(2,1)S(1)}, bf16[160,1280]{1,0:T(8,128)(2,1)S(1)}, u32[]{:S(2)}, u32[]{:S(2)}) collective-permute-start(bf16[160,1280]{1,0:T(8,128)(2,1)S(1)} %get-tuple-element.270), channel_id=1, source_target_pairs={{0,8},{2,10},{4,12},{6,14},{8,16},{10,18},{12,20},{14,22},{16,24},... | collective-permute-start | bytes 1228808 | tf_op jit(solution)/shard_map/ppermute | solution.py:906
  362.2 44.1 %collective-permute-start.54 = (bf16[4,160,800]{2,1,0:T(8,128)(2,1)}, bf16[4,160,800]{2,1,0:T(8,128)(2,1)}, u32[]{:S(2)}, u32[]{:S(2)}) collective-permute-start(bf16[4,160,800]{2,1,0:T(8,128)(2,1)} %get-tuple-element.204), channel_id=1, source_target_pairs={{0,4},{2,6},{4,0},{6,2},{8,12},{10,14},{12,8},{14,10},{16,20},{18,... | collective-permute-start | bytes 3072008 | tf_op jit(solution)/shard_map/ppermute | solution.py:903
  363.8 15.6 %collective-permute-start.43 = (bf16[512,1280]{1,0:T(8,128)(2,1)S(1)}, bf16[512,1280]{1,0:T(8,128)(2,1)S(1)}, u32[]{:S(2)}, u32[]{:S(2)}) collective-permute-start(bf16[512,1280]{1,0:T(8,128)(2,1)S(1)} %copy-done.50), channel_id=1, source_target_pairs={{0,2},{2,0},{4,6},{6,4},{8,10},{10,8},{12,14},{14,12},{16,18},{18,... | collective-permute-start | bytes 3932168 | tf_op jit(solution)/shard_map/ppermute | solution.py:900
  372.9 36.5 %collective-permute-start.53 = (bf16[160,1280]{1,0:T(8,128)(2,1)}, bf16[160,1280]{1,0:T(8,128)(2,1)}, u32[]{:S(2)}, u32[]{:S(2)}) collective-permute-start(bf16[160,1280]{1,0:T(8,128)(2,1)} %get-tuple-element.265), channel_id=1, source_target_pairs={{0,24},{2,26},{4,28},{6,30},{8,0},{10,2},{12,4},{14,6},{16,8},{18,... | collective-permute-start | bytes 1228808 | tf_op jit(solution)/shard_map/ppermute | solution.py:906
  373.1 38.8 %collective-permute-start.52 = (bf16[160,1280]{1,0:T(8,128)(2,1)}, bf16[160,1280]{1,0:T(8,128)(2,1)}, u32[]{:S(2)}, u32[]{:S(2)}) collective-permute-start(bf16[160,1280]{1,0:T(8,128)(2,1)} %get-tuple-element.266), channel_id=1, source_target_pairs={{0,16},{2,18},{4,20},{6,22},{8,24},{10,26},{12,28},{14,30},{16,0},... | collective-permute-start | bytes 1228808 | tf_op jit(solution)/shard_map/ppermute | solution.py:906
  375.9 36.0 %collective-permute-start.51 = (bf16[160,1280]{1,0:T(8,128)(2,1)S(1)}, bf16[160,1280]{1,0:T(8,128)(2,1)}, u32[]{:S(2)}, u32[]{:S(2)}) collective-permute-start(bf16[160,1280]{1,0:T(8,128)(2,1)S(1)} %get-tuple-element.267), channel_id=1, source_target_pairs={{0,8},{2,10},{4,12},{6,14},{8,16},{10,18},{12,20},{14,22},{16,24},... | collective-permute-start | bytes 1228808 | tf_op jit(solution)/shard_map/ppermute | solution.py:906
  379.4 33.9 %collective-permute-start.50 = (bf16[512,1280]{1,0:T(8,128)(2,1)}, bf16[512,1280]{1,0:T(8,128)(2,1)}, u32[]{:S(2)}, u32[]{:S(2)}) collective-permute-start(bf16[512,1280]{1,0:T(8,128)(2,1)} %pad_maximum_fusion), channel_id=1, source_target_pairs={{0,1},{1,0},{2,3},{3,2},{4,5},{5,4},{6,7},{7,6},{8,9},{9,8},{10,11... | collective-permute-start | bytes 3932168 | tf_op jit(solution)/shard_map/ppermute | solution.py:909
  406.4 17.2 %collective-permute-start.56 = (bf16[4,160,480]{2,1,0:T(8,128)(2,1)}, bf16[4,160,480]{2,1,0:T(8,128)(2,1)}, u32[]{:S(2)}, u32[]{:S(2)}) collective-permute-start(bf16[4,160,480]{2,1,0:T(8,128)(2,1)} %get-tuple-element.217), channel_id=1, source_target_pairs={{0,4},{2,6},{4,0},{6,2},{8,12},{10,14},{12,8},{14,10},{16,20},{18,... | collective-permute-start | bytes 1843208 | tf_op jit(solution)/shard_map/ppermute | solution.py:903
  409.4 25.6 %collective-permute-start.58 = (bf16[2,80,1280]{2,1,0:T(8,128)(2,1)S(1)}, bf16[2,80,1280]{2,1,0:T(8,128)(2,1)}, u32[]{:S(2)}, u32[]{:S(2)}) collective-permute-start(bf16[2,80,1280]{2,1,0:T(8,128)(2,1)S(1)} %pad_maximum_fusion.2.refs_0_), channel_id=1, source_target_pairs={{0,1},{1,0},{2,3},{3,2},{4,5},{5,4},{6,7},{7,6},{8,9},{9,8},{10,11... | collective-permute-start | bytes 1228808 | tf_op jit(solution)/shard_map/ppermute | solution.py:909
  426.1 18.9 %collective-permute-start.64 = (bf16[160,1280]{1,0:T(8,128)(2,1)}, bf16[160,1280]{1,0:T(8,128)(2,1)S(1)}, u32[]{:S(2)}, u32[]{:S(2)}) collective-permute-start(bf16[160,1280]{1,0:T(8,128)(2,1)} %get-tuple-element.262), channel_id=1, source_target_pairs={{0,24},{2,26},{4,28},{6,30},{8,0},{10,2},{12,4},{14,6},{16,8},{18,... | collective-permute-start | bytes 1228808 | tf_op jit(solution)/shard_map/ppermute | solution.py:906
  426.9 36.8 %collective-permute-start.63 = (bf16[160,1280]{1,0:T(8,128)(2,1)}, bf16[160,1280]{1,0:T(8,128)(2,1)}, u32[]{:S(2)}, u32[]{:S(2)}) collective-permute-start(bf16[160,1280]{1,0:T(8,128)(2,1)} %get-tuple-element.264), channel_id=1, source_target_pairs={{0,16},{2,18},{4,20},{6,22},{8,24},{10,26},{12,28},{14,30},{16,0},... | collective-permute-start | bytes 1228808 | tf_op jit(solution)/shard_map/ppermute | solution.py:906
  426.9 36.8 %collective-permute-start.62 = (bf16[160,1280]{1,0:T(8,128)(2,1)}, bf16[160,1280]{1,0:T(8,128)(2,1)}, u32[]{:S(2)}, u32[]{:S(2)}) collective-permute-start(bf16[160,1280]{1,0:T(8,128)(2,1)} %get-tuple-element.263), channel_id=1, source_target_pairs={{0,8},{2,10},{4,12},{6,14},{8,16},{10,18},{12,20},{14,22},{16,24},... | collective-permute-start | bytes 1228808 | tf_op jit(solution)/shard_map/ppermute | solution.py:906
  433.6 37.5 %collective-permute-start.60 = (bf16[512,1280]{1,0:T(8,128)(2,1)}, bf16[512,1280]{1,0:T(8,128)(2,1)}, u32[]{:S(2)}, u32[]{:S(2)}) collective-permute-start(bf16[512,1280]{1,0:T(8,128)(2,1)} %add_convert_fusion), channel_id=1, source_target_pairs={{0,1},{1,0},{2,3},{3,2},{4,5},{5,4},{6,7},{7,6},{8,9},{9,8},{10,11... | collective-permute-start | bytes 3932168 | tf_op jit(solution)/shard_map/ppermute | solution.py:909
  444.9 22.5 %collective-permute-start.59 = (bf16[512,1280]{1,0:T(8,128)(2,1)}, bf16[512,1280]{1,0:T(8,128)(2,1)}, u32[]{:S(2)}, u32[]{:S(2)}) collective-permute-start(bf16[512,1280]{1,0:T(8,128)(2,1)} %get-tuple-element.231), channel_id=1, source_target_pairs={{0,2},{2,0},{4,6},{6,4},{8,10},{10,8},{12,14},{14,12},{16,18},{18,... | collective-permute-start | bytes 3932168 | tf_op jit(solution)/shard_map/ppermute | solution.py:900
  468.0 28.0 %collective-permute-start.70 = (bf16[2,80,1280]{2,1,0:T(8,128)(2,1)S(1)}, bf16[2,80,1280]{2,1,0:T(8,128)(2,1)S(1)}, u32[]{:S(2)}, u32[]{:S(2)}) collective-permute-start(bf16[2,80,1280]{2,1,0:T(8,128)(2,1)S(1)} %pad_maximum_fusion.3.refs_0_), channel_id=1, source_target_pairs={{0,1},{1,0},{2,3},{3,2},{4,5},{5,4},{6,7},{7,6},{8,9},{9,8},{10,11... | collective-permute-start | bytes 1228808 | tf_op jit(solution)/shard_map/ppermute | solution.py:909
  481.9 18.5 %collective-permute-start.71 = (bf16[160,1280]{1,0:T(8,128)(2,1)S(1)}, bf16[160,1280]{1,0:T(8,128)(2,1)S(1)}, u32[]{:S(2)}, u32[]{:S(2)}) collective-permute-start(bf16[160,1280]{1,0:T(8,128)(2,1)S(1)} %add_convert_fusion.7.refs_2_), channel_id=1, source_target_pairs={{0,1},{1,0},{2,3},{3,2},{4,5},{5,4},{6,7},{7,6},{8,9},{9,8},{10,11... | collective-permute-start | bytes 1228808 | tf_op jit(solution)/shard_map/ppermute | solution.py:909
  (84 other events, 897.9 us)
Sparse Core Ops, SparseCore 0:
  16.4 73.6 all-gather.3
  92.8 101.4 all-gather.5
